TPU v7x, 32 devices: a whole 2x2x4 slice. The times are simulated.
32 devices in a mesh: members: 2 (over y), tx: 4 (over z), ty: 4 (over x, core).
Axes of the slice: x: 2, y: 2, z: 4, core: 2. Of those that a mesh axis runs over, the one named last changes fastest.
Arguments:
- tracers: float32 [4, 16, 64, 512], P('members', None, 'tx', 'ty'), parts along dimension 0, may hold values from -6 to 6
- costate: float32 [4, 16, 64, 512], P('members', None, 'tx', 'ty'), parts along dimension 0, may hold values from -6 to 6
- mixing_h: float32 [32, 64, 512], P('members', 'tx', 'ty'), parts along dimension 0, may hold values from 0.01 to 0.24
- mixing_v: float32 [32, 64, 512], P('members', 'tx', 'ty'), parts along dimension 0, may hold values from 0.1 to 5
- levels: int32 [64, 512], P('tx', 'ty'), may hold values from 0 to 16
- seam_code: int32 [4], P('ty'), may hold values from 0 to 1
Outputs:
- tracer_adjoint: float32 [4, 16, 64, 512], P('members', None, 'tx', 'ty'), parts along dimension 0
- grad_mixing_h: float32 [32, 64, 512], P('members', 'tx', 'ty'), parts along dimension 0
- grad_mixing_v: float32 [32, 64, 512], P('members', 'tx', 'ty'), parts along dimension 0
There are 2 independent parts, one for each index of `members`. A program takes and returns all parts, laid end to end along the dimension named above; an argument that names none is the same for every part. Nothing has to cross between parts.
All inputs are finite; a program needn't handle non-finite values.
Results may differ from a plain program's by a relative error of at most 0.0001.
Values sent between devices are 32-bit elements; how exact they have to be, the bound alone decides.
No kernel may reach another device: no remote copies, remote signals or barrier semaphores. Data moves between devices by JAX's collectives and lax.ppermute only.
A program may use at most 64 MiB of HBM per device.

v0:
```python
import jax
import jax.numpy as jnp
from jax import lax
from jax.experimental import pallas as pl
from jax.experimental.pallas import tpu as pltpu
from jax.sharding import PartitionSpec as P

LANES = 128
ROWS = 16
GROUP = 16
PER_TILE = LANES // GROUP


FILLER = 3


def in_vmem(array):
    return pltpu.with_memory_space_constraint(array, pltpu.VMEM)


def in_hbm(array):
    return pltpu.with_memory_space_constraint(array, pltpu.HBM)


def vmem_out(*shape):
    return pltpu.VMEM(shape, jnp.float32)


def iota(rows, dim):
    return lax.broadcasted_iota(jnp.int32, (rows, LANES), dim)


def roll(value, shift, axis):
    return pltpu.roll(value, shift % value.shape[axis], axis)


def fold(value):
    return jnp.where(iota(8, 0) < 4, value[:8], value[8:])


def east(value, halo):
    lane = iota(value.shape[0], 1)
    return roll(jnp.where(lane == 0, halo, value), -1, 1)


def west(value, halo):
    lane = iota(value.shape[0], 1)
    return roll(jnp.where(lane == LANES - 1, halo, value), 1, 1)


def rim(tile, base):
    return roll(tile, LANES - 2 - base, 1)


def north(value, beyond):
    sub = iota(8, 0)
    low, high = roll(value[:8], -1, 0), roll(value[8:], -1, 0)
    return jnp.concatenate([jnp.where(sub == 7, high, low), jnp.where(sub == 7, beyond, high)], axis=0)


def south(value, beyond):
    sub = iota(8, 0)
    low, high = roll(value[:8], 1, 0), roll(value[8:], 1, 0)
    return jnp.concatenate([jnp.where(sub == 0, beyond, low), jnp.where(sub == 0, low, high)], axis=0)


def bond(mix_v, level, k, depth):
    under = jnp.minimum(k + 1, depth - 1)
    return jnp.where(level > k + 1, 0.5 * (mix_v[k] + mix_v[under]), 0.0)


def prepare(
    seam,
    tracers,
    costate,
    mix_h_in,
    mix_v_in,
    levels_in,
    fields,
    factors,
    message,
    mix_h,
    mix_v,
    levels,
    sems,
):
    depth = mix_h.shape[0]
    copies = [
        pltpu.make_async_copy(source, target, sems.at[n])
        for n, (source, target) in enumerate(
            (
                (levels_in, levels),
                (mix_v_in, mix_v),
                (costate.at[0], fields.at[:, 2]),
                (costate.at[1], fields.at[:, 3]),
                (tracers.at[0], fields.at[:, 0]),
                (tracers.at[1], fields.at[:, 1]),
                (mix_h_in, mix_h),
            )
        )
    ]
    for copy in copies:
        copy.start()
    for copy in copies[:4]:
        copy.wait()
    level = levels[...]
    lane = iota(ROWS, 1)
    zero = jnp.zeros((ROWS, LANES), jnp.float32)

    def down(k, carry):
        bond_above, inverse, *values = carry
        bond_here = bond(mix_v, level, k, depth)
        inverse = 1.0 / (1.0 + bond_above + bond_here - bond_above * (bond_above * inverse))
        factor = bond_above * inverse
        factors[0, k] = inverse
        factors[1, k] = factor
        factors[2, k] = bond_here * inverse
        for t in range(2):
            values[t] = fields[k, 2 + t] * inverse + factor * values[t]
            fields[k, 2 + t] = values[t]
        return (bond_here, inverse, *values)

    lax.fori_loop(0, depth, down, (zero, zero, zero, zero))
    for copy in copies[4:]:
        copy.wait()
    level_f = level.astype(jnp.float32)
    code = zero + seam[0].astype(jnp.float32)

    def up(n, carry):
        k = depth - 1 - n
        bond_here, inverse, *values = carry
        for t in range(2):
            values[t] = fields[k, 2 + t] + factors[2, k] * values[t]
            fields[k, 2 + t] = values[t]
        bond_above = jnp.where(k > 0, bond(mix_v, level, jnp.maximum(k - 1, 0), depth), 0.0)
        inverse = 1.0 / (1.0 + bond_above + bond_here - bond_here * (bond_here * inverse))
        factors[3, k] = inverse
        factors[4, k] = bond_here * inverse
        factors[5, k] = bond_above * inverse
        tile, base = k // PER_TILE, GROUP * (k % PER_TILE)
        place = lane // 4 - base // 4
        first = message[tile]
        for q, value in enumerate((fields[k, 0], fields[k, 1], values[0], values[1])):
            first = jnp.where(place == q, pltpu.roll(value, (base + 4 * q + 2) % LANES, 1), first)
        message[tile] = first
        second = message[depth // PER_TILE + tile]
        for q, value in enumerate((mix_h[k], mix_v[k], level_f)):
            second = jnp.where(place == q, pltpu.roll(value, (base + 4 * q + 2) % LANES, 1), second)
        message[depth // PER_TILE + tile] = jnp.where(place == FILLER, code, second)
        return (bond_above, inverse, *values)

    lax.fori_loop(0, depth, up, (zero, zero, zero, zero))


def pack_rows(near, far, fields, mix_h, mix_v, levels, lower, upper, merged):
    depth = mix_h.shape[0]
    tiles = depth // PER_TILE
    place = lax.axis_index("ty")
    last = lax.axis_size("ty") - 1
    even = place % 2 == 0
    column = iota(ROWS, 1) % 4
    from_west = column < 2
    missing = ((place == 0) & from_west) | ((place == last) & jnp.logical_not(from_west))
    base_level = 10 * depth
    corners = []
    for j in range(2 * tiles):
        west_tile = jnp.where(even, far[j], near[j])
        east_tile = jnp.where(even, near[j], far[j])
        tile = jnp.where(from_west, west_tile, east_tile)
        if j >= tiles:
            tile = jnp.where(missing, 0.0, tile)
        merged[j] = tile
        other = jnp.where(
            column == 0, roll(west_tile, -2, 1), jnp.where(column == 3, roll(east_tile, 2, 1), tile)
        )
        corners.append(fold(other))
    sub = iota(8, 0)
    level_all = levels[...].astype(jnp.float32)
    level = fold(level_all)
    for target, row in ((lower, 0), (upper, 7)):
        block = jnp.zeros((8, LANES), jnp.float32)
        for n, value in enumerate([level, *corners]):
            block = jnp.where(sub == n, roll(value, n - row, 0), block)
        target[base_level : base_level + 8] = block

    def inner(value):
        return jnp.where(sub < 4, roll(value, -1, 0), roll(value, 1, 0))

    level_rim = rim(fold(merged[tiles]), 8)
    shallow = [
        jnp.minimum(level, near_level)
        for near_level in (east(level, level_rim), west(level, level_rim), inner(level))
    ]

    def row(k, _):
        tile, base = k // PER_TILE, GROUP * (k % PER_TILE)
        coefs = fold(merged[tiles + tile])
        mix = fold(mix_h[k])
        mix_rim = rim(coefs, base)
        mixes = (east(mix, mix_rim), west(mix, mix_rim), inner(mix))
        weights = [
            jnp.where(open_to > k.astype(jnp.float32), 0.5 * (mix + near_mix), 0.0)
            for open_to, near_mix in zip(shallow, mixes)
        ]
        packed = fold(merged[tile])
        low = jnp.zeros((8, LANES), jnp.float32)
        high = low
        for q in range(4):
            value = fold(fields[k, q])
            halo = rim(packed, base + 4 * q)
            part = value
            for near_value, weight in zip(
                (east(value, halo), west(value, halo), inner(value)), weights
            ):
                part = part + weight * (near_value - value)
            for n, thing in ((q, value), (4 + q, part)):
                low = jnp.where(sub == n, roll(thing, n, 0), low)
                high = jnp.where(sub == n, roll(thing, n - 7, 0), high)
        at = pl.ds(pl.multiple_of(8 * k, 8), 8)
        lower[at] = low
        upper[at] = high
        for n, array in enumerate((mix_h, mix_v)):
            at = pl.ds((8 + n) * depth + k, 1)
            lower[at] = array[k, :1]
            upper[at] = array[k, ROWS - 1 :]
        return 0

    lax.fori_loop(0, depth, row, 0)


def finish(
    seam,
    from_below,
    from_above,
    lower,
    upper,
    merged,
    own,
    fields,
    factors,
    mix_h,
    levels,
    adjoint_out,
    grad_h_out,
    grad_v_out,
    below,
    above,
    rows,
    columns,
    packed,
    weights,
    inside,
    later,
    adjoint,
    grad_h,
    grad_v,
    sems,
):
    depth = mix_h.shape[0]
    tiles = depth // PER_TILE
    sub = iota(8, 0)
    lane = iota(ROWS, 1)
    place = lax.axis_index("tx")
    last = lax.axis_size("tx") - 1
    base_mix, base_v, base_level, base_corner = 8 * depth, 9 * depth, 10 * depth, 10 * depth + 1
    zero = jnp.zeros((ROWS, LANES), jnp.float32)
    zero_rows = jnp.zeros((8, LANES), jnp.float32)

    for source, target, edge in ((from_below, below, 0), (from_above, above, last)):
        turn = (seam[0] == 1) & (place == edge)

        @pl.when(turn)
        def _():
            back = LANES - 1 - iota(8, 1)
            for r in range(0, base_level, 8):
                target[r : r + 8] = jnp.take_along_axis(source[r : r + 8], back, axis=1)
            block = source[base_level : base_level + 8]
            target[base_level : base_level + 8] = jnp.where(
                sub < 1, jnp.take_along_axis(block, back, axis=1), block
            )

        @pl.when(jnp.logical_not(turn))
        def _():
            for r in range(0, base_level + 8, 8):
                target[r : r + 8] = source[r : r + 8]

    def both(a, b):
        return jnp.where(sub < 4, a, b)

    column = lane % 4

    def coefficient(value, n):
        kept = iota(value.shape[0], 1) % GROUP // 4 == n
        value = roll(jnp.where(kept, value, 0.0), -4 * n, 1)
        value = value + roll(value, 4, 1)
        return value + roll(value, 8, 1)

    def around(value, mine, below_row, above_row):
        return (
            jnp.where(column == 1, roll(mine, -1, 1), roll(mine, 1, 1)),
            jnp.where(column == 1, roll(value, 1, 1), roll(value, -1, 1)),
            north(value, above_row),
            south(value, below_row),
        )

    turned = coefficient(merged[tiles, :8], FILLER)
    spot = iota(8, 1) % 4
    corner_rows = []
    for target, edge in ((below, 0), (above, last)):
        block = target[base_level : base_level + 8]
        swap = (place == edge) & (turned > 0.5)
        swapped = jnp.where(spot == 1, roll(block, 1, 1), roll(block, -1, 1))
        corner_rows.append(jnp.where(swap, swapped, block))
    for j in range(tiles):
        corner = [block[1 + j : 2 + j] for block in corner_rows]
        corner_coef = [block[1 + tiles + j : 2 + tiles + j] for block in corner_rows]
        level_k = (lane // GROUP + j * PER_TILE).astype(jnp.float32)
        (mix, mixes), (level, level_near) = [
            (
                coefficient(merged[tiles + j], n),
                around(
                    coefficient(merged[tiles + j], n),
                    coefficient(own[tiles + j], n),
                    *(coefficient(c, n) for c in corner_coef),
                ),
            )
            for n in (0, 2)
        ]
        value = merged[j]
        mixed = value
        for near_value, near_mix, near_level in zip(
            around(value, own[j], *corner), mixes, level_near
        ):
            weight = jnp.where(
                jnp.minimum(level, near_level) > level_k, 0.5 * (mix + near_mix), 0.0
            )
            mixed = mixed + weight * (near_value - value)
        packed[0, j] = mixed
        packed[1, j] = coefficient(merged[tiles + j], 1)
        if j == 0:
            level_columns = level

    def unpacked(n, k):
        return roll(packed[n, k // PER_TILE], LANES - GROUP * (k % PER_TILE), 1)

    level_out = both(below[base_level : base_level + 1], above[base_level : base_level + 1])
    level_in = both(lower[base_level : base_level + 1], upper[base_level : base_level + 1])
    level_face = jnp.minimum(level_out, level_in)
    level = levels[...].astype(jnp.float32)

    def near_all(value, halo, below_row, above_row):
        return (
            north(value, above_row),
            south(value, below_row),
            east(value, halo),
            west(value, halo),
        )

    shallow = [
        jnp.minimum(level, near_level)
        for near_level in near_all(
            level,
            rim(merged[tiles], 8),
            below[base_level : base_level + 1],
            above[base_level : base_level + 1],
        )
    ]

    def pivot_step(bond_above, bond_here, inverse):
        return 1.0 / (1.0 + bond_above + bond_here - bond_above * (bond_above * inverse))

    def row_at(ref, start, k):
        return ref[pl.ds(start + k, 1)]

    def mix_v_rows(k):
        return both(row_at(below, base_v, k), row_at(above, base_v, k))

    def steps_of(k, q, below_block, above_block):
        value = fields[k, q]
        halo = rim(merged[k // PER_TILE], GROUP * (k % PER_TILE) + 4 * q)
        nears = near_all(value, halo, below_block[q : q + 1], above_block[q : q + 1])
        return value, [n - value for n in nears]

    def first(k, carry):
        (row_bond, row_inverse, row_value), (col_bond, col_inverse, col_value), values = carry
        kf = k.astype(jnp.float32)
        block = pl.ds(pl.multiple_of(8 * k, 8), 8)
        below_block, above_block = below[block], above[block]
        under = jnp.minimum(k + 1, depth - 1)
        bond_here = jnp.where(
            level_out > kf + 1.0, 0.5 * (mix_v_rows(k) + mix_v_rows(under)), 0.0
        )
        row_inverse = pivot_step(row_bond, bond_here, row_inverse)
        out = both(below_block, roll(above_block, 4, 0))
        part = both(roll(below_block, 4, 0), above_block)
        inn = both(lower[block], roll(upper[block], 4, 0))
        weight = 0.5 * (
            both(row_at(below, base_mix, k), row_at(above, base_mix, k))
            + both(row_at(lower, base_mix, k), row_at(upper, base_mix, k))
        )
        rhs = part + jnp.where(level_face > kf, weight, 0.0) * (inn - out)
        row_value = rhs * row_inverse + row_bond * row_inverse * row_value
        rows[0, k] = row_value
        rows[1, k] = bond_here * row_inverse
        row_carry = (bond_here, row_inverse, row_value)
        bond_here = jnp.where(
            level_columns > kf + 1.0, 0.5 * (unpacked(1, k) + unpacked(1, under)), 0.0
        )
        col_inverse = pivot_step(col_bond, bond_here, col_inverse)
        col_value = unpacked(0, k) * col_inverse + col_bond * col_inverse * col_value
        columns[0, k] = col_value
        columns[1, k] = bond_here * col_inverse
        col_carry = (bond_here, col_inverse, col_value)
        mix = mix_h[k]
        mix_rim = rim(merged[tiles + k // PER_TILE], GROUP * (k % PER_TILE))
        near_mixes = near_all(mix, mix_rim, row_at(below, base_mix, k), row_at(above, base_mix, k))
        weight = [
            jnp.where(open_to > kf, 0.5 * (mix + near_mix), 0.0)
            for open_to, near_mix in zip(shallow, near_mixes)
        ]
        for n in range(4):
            weights[k, n] = weight[n]
        inverse, factor = factors[0, k], factors[1, k]
        values = list(values)
        for q in range(4):
            value, steps = steps_of(k, q, below_block, above_block)
            for n in range(4):
                value = value + weight[n] * steps[n]
            values[q] = value * inverse + factor * values[q]
            inside[k, q] = values[q]
        return (row_carry, col_carry, tuple(values))

    lax.fori_loop(
        0, depth, first, ((zero_rows,) * 3, (zero,) * 3, (zero,) * 4)
    )

    def second(n, carry):
        row_value, col_value, values, later_values = carry
        k = depth - 1 - n
        kf = k.astype(jnp.float32)
        block = pl.ds(pl.multiple_of(8 * k, 8), 8)
        below_block, above_block = below[block], above[block]
        row_value = rows[0, k] + rows[1, k] * row_value
        col_value = columns[0, k] + columns[1, k] * col_value
        values, later_values = list(values), list(later_values)
        factor = factors[2, k]
        first_steps, later_steps = [], []
        weight = [weights[k, n] for n in range(4)]
        for q in range(4):
            value = inside[k, q] + factor * values[q]
            inside[k, q] = value
            values[q] = value
            nears = near_all(
                value, rim(col_value, 4 * q), row_value[q : q + 1], row_value[4 + q : 5 + q]
            )
            steps = [near_value - value for near_value in nears]
            later_steps.append(steps)
            first_steps.append(steps_of(k, q, below_block, above_block)[1])
            for n in range(4):
                value = value + weight[n] * steps[n]
            if q < 2:
                later_values[q] = value * factors[3, k] + factors[4, k] * later_values[q]
                later[k, q] = later_values[q]
            else:
                adjoint[q - 2, k] = value
        total = zero
        for n in range(4):
            face = zero
            for t in range(2):
                face = face + first_steps[t][n] * later_steps[2 + t][n]
                face = face + later_steps[t][n] * first_steps[2 + t][n]
            total = total + jnp.where(shallow[n] > kf, face, 0.0)
        grad_h[k] = -0.5 * total
        return (row_value, col_value, tuple(values), tuple(later_values))

    lax.fori_loop(0, depth, second, (zero_rows, zero, (zero,) * 4, (zero,) * 2))
    copies = [
        pltpu.make_async_copy(source, target, sems.at[n])
        for n, (source, target) in enumerate(
            ((adjoint, adjoint_out), (grad_h, grad_h_out), (grad_v, grad_v_out))
        )
    ]
    copies[0].start()
    copies[1].start()

    def third(k, carry):
        face_above, later_above, inside_above, fields_above = carry
        inside_here = [inside[k, q] for q in range(4)]
        fields_here = [fields[k, 2 + t] for t in range(2)]
        later_here = [later[k, t] + factors[5, k] * later_above[t] for t in range(2)]
        total = zero
        for t in range(2):
            total = total + (inside_above[2 + t] - inside_here[2 + t]) * (
                inside_above[t] - inside_here[t]
            )
            total = total + (fields_above[t] - fields_here[t]) * (later_above[t] - later_here[t])
        face = jnp.where((k > 0) & (level > k.astype(jnp.float32)), total, 0.0)
        grad_v[jnp.maximum(k - 1, 0)] = -0.5 * (face + face_above)
        return face, tuple(later_here), tuple(inside_here), tuple(fields_here)

    face = lax.fori_loop(0, depth, third, (zero, (zero,) * 2, (zero,) * 4, (zero,) * 2))[0]
    grad_v[depth - 1] = -0.5 * face
    copies[2].start()
    for copy in copies:
        copy.wait()


def per_device(tracers, costate, mixing_h, mixing_v, levels, seam_code):
    depth = tracers.shape[1]
    tiles = depth // PER_TILE
    height = 10 * depth + 8
    params = pltpu.CompilerParams(vmem_limit_bytes=48 * 2**20)
    smem = pl.BlockSpec(memory_space=pltpu.SMEM)
    vmem = pl.BlockSpec(memory_space=pltpu.VMEM)
    hbm = pl.BlockSpec(memory_space=pltpu.HBM)
    tile = (ROWS, LANES)
    fields, factors, own, mix_h, mix_v, levels_here = pl.pallas_call(
        prepare,
        out_shape=(
            vmem_out(depth, 4, *tile),
            vmem_out(6, depth, *tile),
            vmem_out(2 * tiles, *tile),
            vmem_out(depth, *tile),
            vmem_out(depth, *tile),
            pltpu.VMEM(tile, jnp.int32),
        ),
        in_specs=[smem] + [hbm] * 5,
        scratch_shapes=[pltpu.SemaphoreType.DMA((7,))],
        compiler_params=params,
        name="prepare",
    )(seam_code, *(in_hbm(a) for a in (tracers, costate, mixing_h, mixing_v, levels)))

    count = lax.axis_size("ty")
    near_pairs = [(i, i ^ 1) for i in range(count)]
    far_pairs = [(i, (i + 1 if i % 2 else i - 1) % count) for i in range(count)]
    far = lax.ppermute(own, "ty", far_pairs)
    near = lax.ppermute(own, "ty", near_pairs)
    lower, upper, merged = pl.pallas_call(
        pack_rows,
        out_shape=(
            vmem_out(height, LANES),
            vmem_out(height, LANES),
            vmem_out(2 * tiles, *tile),
        ),
        compiler_params=params,
        name="pack_rows",
    )(*(in_vmem(a) for a in (near, far, fields, mix_h, mix_v, levels_here)))

    count = lax.axis_size("tx")
    from_below = lax.ppermute(upper, "tx", [(i, (i + 1) % count) for i in range(count)])
    from_above = lax.ppermute(lower, "tx", [(i, (i - 1) % count) for i in range(count)])
    block = jax.ShapeDtypeStruct(mixing_h.shape, jnp.float32)
    return pl.pallas_call(
        finish,
        out_shape=(jax.ShapeDtypeStruct(tracers.shape, jnp.float32), block, block),
        in_specs=[smem] + [vmem] * 10,
        out_specs=(hbm, hbm, hbm),
        scratch_shapes=[
            vmem_out(height, LANES),
            vmem_out(height, LANES),
            vmem_out(2, depth, 8, LANES),
            vmem_out(2, depth, *tile),
            vmem_out(2, tiles, *tile),
            vmem_out(depth, 4, *tile),
            vmem_out(depth, 4, *tile),
            vmem_out(depth, 2, *tile),
            vmem_out(2, depth, *tile),
            vmem_out(depth, *tile),
            vmem_out(depth, *tile),
            pltpu.SemaphoreType.DMA((3,)),
        ],
        compiler_params=params,
        name="finish",
    )(
        seam_code,
        *(
            in_vmem(a)
            for a in (
                from_below,
                from_above,
                lower,
                upper,
                merged,
                own,
                fields,
                factors,
                mix_h,
                levels_here,
            )
        ),
    )


def solution(mesh):
    placed = (
        P("members", None, "tx", "ty"),
        P("members", None, "tx", "ty"),
        P("members", "tx", "ty"),
        P("members", "tx", "ty"),
        P("tx", "ty"),
        P("ty"),
    )
    return jax.shard_map(
        per_device,
        mesh=mesh,
        in_specs=placed,
        out_specs=(
            P("members", None, "tx", "ty"),
            P("members", "tx", "ty"),
            P("members", "tx", "ty"),
        ),
        check_vma=False,
    )
```

profile of v0, /device:TPU:0, one launch (start us, length us, event | category | flops | bytes accessed | tf_op | source)
XLA Modules:
  0.0 26.8 jit_solution(9270124902396808418)
XLA Ops:
  1.3 2.9 %prepare.1 = (f32[16,4,16,128]{3,2,1,0:T(8,128)S(1)}, f32[6,16,16,128]{3,2,1,0:T(8,128)S(1)}, f32[4,16,128]{2,1,0:T(8,128)S(1)}, f32[16,16,128]{2,1,0:T(8,128)S(...) custom-call(s32[1]{0:T(128)S(6)} %copy.9.seam, f32[2,16,16,128]{3,2,1,0:T(8,128)} %tracers.1, ...), custom_call_target="tpu_custom_call" | custom-call | tf_op jit(solution)/shard_map/prepare/pallas_call | solution.py:517
  4.2 2.4 %collective-permute-start.1 = (f32[4,16,128]{2,1,0:T(8,128)S(1)}, f32[4,16,128]{2,1,0:T(8,128)S(1)}, u32[]{:S(2)}, u32[]{:S(2)}) collective-permute-start(f32[4,16,128]{2,1,0:T(8,128)S(1)} %get-tuple-element.12.own), channel_id=1, source_target_pairs={{0,3},{1,2},{2,1},{3,0},{4,7},{5,6},{6,5},{7,4},{8,11},{9,10},{10,... | collective-permute-start | bytes 98312 | tf_op jit(solution)/shard_map/ppermute | solution.py:536
  6.6 0.7 %collective-permute-start = (f32[4,16,128]{2,1,0:T(8,128)S(1)}, f32[4,16,128]{2,1,0:T(8,128)S(1)}, u32[]{:S(2)}, u32[]{:S(2)}) collective-permute-start(f32[4,16,128]{2,1,0:T(8,128)S(1)} %get-tuple-element.12.own), channel_id=1, source_target_pairs={{0,1},{1,0},{2,3},{3,2},{4,5},{5,4},{6,7},{7,6},{8,9},{9,8},{10,11... | collective-permute-start | bytes 98312 | tf_op jit(solution)/shard_map/ppermute | solution.py:537
  7.3 1.1 %collective-permute-done.1.far = f32[4,16,128]{2,1,0:T(8,128)S(1)} collective-permute-done((f32[4,16,128]{2,1,0:T(8,128)S(1)}, f32[4,16,128]{2,1,0:T(8,128)S(1)}, u32[]{:S(2)}, u32[]{:S(2)}) %collective-permute-start.1) | collective-permute-done | bytes 32800 | tf_op jit(solution)/shard_map/ppermute | solution.py:536
  8.4 0.0 collective-permute-done.near
  8.4 2.7 %pack_rows.1 = (f32[168,128]{1,0:T(8,128)S(1)}, f32[168,128]{1,0:T(8,128)S(1)}, f32[4,16,128]{2,1,0:T(8,128)S(1)}) custom-call(f32[4,16,128]{2,1,0:T(8,128)S(1)} %collective-permute-done.near, f32[4,16,128]{2,1,0:T(8,128)S(1)} %collective-permute-done.1.far, f32[16,4,16,128]{3,2,1,0:T(8,128)S(1)} %get-tuple-element.13.fields, ...), custom_call_target="tpu_custom_call" | custom-call | tf_op jit(solution)/shard_map/pack_rows/pallas_call | solution.py:538
  11.1 2.6 %collective-permute-start.2 = (f32[168,128]{1,0:T(8,128)S(1)}, f32[168,128]{1,0:T(8,128)S(1)}, u32[]{:S(2)}, u32[]{:S(2)}) collective-permute-start(f32[168,128]{1,0:T(8,128)S(1)} %get-tuple-element.17.upper), channel_id=1, source_target_pairs={{0,4},{4,8},{8,12},{12,0},{1,5},{5,9},{9,13},{13,1},{2,6},{6,10},{... | collective-permute-start | bytes 258056 | tf_op jit(solution)/shard_map/ppermute | solution.py:550
  13.7 2.1 %collective-permute-start.3 = (f32[168,128]{1,0:T(8,128)S(1)}, f32[168,128]{1,0:T(8,128)S(1)}, u32[]{:S(2)}, u32[]{:S(2)}) collective-permute-start(f32[168,128]{1,0:T(8,128)S(1)} %get-tuple-element.18.lower), channel_id=1, source_target_pairs={{0,12},{4,0},{8,4},{12,8},{1,13},{5,1},{9,5},{13,9},{2,14},{6,2},{... | collective-permute-start | bytes 258056 | tf_op jit(solution)/shard_map/ppermute | solution.py:551
  15.7 3.1 %collective-permute-done.2.from_below = f32[168,128]{1,0:T(8,128)S(1)} collective-permute-done((f32[168,128]{1,0:T(8,128)S(1)}, f32[168,128]{1,0:T(8,128)S(1)}, u32[]{:S(2)}, u32[]{:S(2)}) %collective-permute-start.2) | collective-permute-done | bytes 86048 | tf_op jit(solution)/shard_map/ppermute | solution.py:550
  18.9 0.9 %collective-permute-done.3.from_above = f32[168,128]{1,0:T(8,128)S(1)} collective-permute-done((f32[168,128]{1,0:T(8,128)S(1)}, f32[168,128]{1,0:T(8,128)S(1)}, u32[]{:S(2)}, u32[]{:S(2)}) %collective-permute-start.3) | collective-permute-done | bytes 86048 | tf_op jit(solution)/shard_map/ppermute | solution.py:551
  19.8 7.0 %finish.1 = (f32[2,16,16,128]{3,2,1,0:T(8,128)}, f32[16,16,128]{2,1,0:T(8,128)}, f32[16,16,128]{2,1,0:T(8,128)}) custom-call(s32[1]{0:T(128)S(6)} %copy.9.seam, f32[168,128]{1,0:T(8,128)S(1)} %collective-permute-done.2.from_below, f32[168,128]{1,0:T(8,128)S(1)} %collective-permute-done.3.from_above, f32[168,128]{1,0:T(8,128)S(1)} %get-tuple-element.18.lower, ...), custom_call_target="tpu_custom_call" | custom-call | tf_op jit(solution)/shard_map/finish/pallas_call | solution.py:553
Async XLA Ops:
  4.2 4.2 %collective-permute-start.1 = (f32[4,16,128]{2,1,0:T(8,128)S(1)}, f32[4,16,128]{2,1,0:T(8,128)S(1)}, u32[]{:S(2)}, u32[]{:S(2)}) collective-permute-start(f32[4,16,128]{2,1,0:T(8,128)S(1)} %get-tuple-element.12.own), channel_id=1, source_target_pairs={{0,3},{1,2},{2,1},{3,0},{4,7},{5,6},{6,5},{7,4},{8,11},{9,10},{10,... | collective-permute-start | bytes 98312 | tf_op jit(solution)/shard_map/ppermute | solution.py:536
  6.6 1.8 %collective-permute-start = (f32[4,16,128]{2,1,0:T(8,128)S(1)}, f32[4,16,128]{2,1,0:T(8,128)S(1)}, u32[]{:S(2)}, u32[]{:S(2)}) collective-permute-start(f32[4,16,128]{2,1,0:T(8,128)S(1)} %get-tuple-element.12.own), channel_id=1, source_target_pairs={{0,1},{1,0},{2,3},{3,2},{4,5},{5,4},{6,7},{7,6},{8,9},{9,8},{10,11... | collective-permute-start | bytes 98312 | tf_op jit(solution)/shard_map/ppermute | solution.py:537
  11.1 7.8 %collective-permute-start.2 = (f32[168,128]{1,0:T(8,128)S(1)}, f32[168,128]{1,0:T(8,128)S(1)}, u32[]{:S(2)}, u32[]{:S(2)}) collective-permute-start(f32[168,128]{1,0:T(8,128)S(1)} %get-tuple-element.17.upper), channel_id=1, source_target_pairs={{0,4},{4,8},{8,12},{12,0},{1,5},{5,9},{9,13},{13,1},{2,6},{6,10},{... | collective-permute-start | bytes 258056 | tf_op jit(solution)/shard_map/ppermute | solution.py:550
  13.7 6.1 %collective-permute-start.3 = (f32[168,128]{1,0:T(8,128)S(1)}, f32[168,128]{1,0:T(8,128)S(1)}, u32[]{:S(2)}, u32[]{:S(2)}) collective-permute-start(f32[168,128]{1,0:T(8,128)S(1)} %get-tuple-element.18.lower), channel_id=1, source_target_pairs={{0,12},{4,0},{8,4},{12,8},{1,13},{5,1},{9,5},{13,9},{2,14},{6,2},{... | collective-permute-start | bytes 258056 | tf_op jit(solution)/shard_map/ppermute | solution.py:551
where the time goes:
time: 27 us; the launch traced here: 26.8 us
  Pallas kernels  12.6 us (47%)
  starting transfers between devices  7.77 us (29%)
  waiting for transfers between devices  5.13 us (19%)
  between operations  1.3 us (5%)
    pallas_call x1, Pallas kernels, per_device(): pl.pallas_call(finish, out_shape=(jax.ShapeDtypeStruct(tracers.shape, jnp...  7 us
    ppermute x1, waiting for transfers between devices, per_device(): lax.ppermute(upper, 'tx', [(i, (i + 1) % count) for i in range(count)])  3.14 us
    pallas_call x1, Pallas kernels, per_device(): pl.pallas_call(prepare, out_shape=(vmem_out(depth, 4, *tile), vmem_out(6,...  2.89 us
    pallas_call x1, Pallas kernels, per_device(): pl.pallas_call(pack_rows, out_shape=(vmem_out(height, LANES), vmem_out(he...  2.69 us
    ppermute x1, starting transfers between devices, per_device(): lax.ppermute(upper, 'tx', [(i, (i + 1) % count) for i in range(count)])  2.56 us
    ppermute x1, starting transfers between devices, per_device(): far = lax.ppermute(own, 'ty', far_pairs)  2.44 us
    ppermute x1, starting transfers between devices, per_device(): lax.ppermute(lower, 'tx', [(i, (i - 1) % count) for i in range(count)])  2.09 us
    ppermute x1, waiting for transfers between devices, per_device(): far = lax.ppermute(own, 'ty', far_pairs)  1.1 us
  transfers between devices with their start and end apart: 4, of which 3 were waited for; matrix products, arithmetic and copies ran while one was open for 0% of the time, Pallas kernels for 0%

commit v1 on v0

--- a/solution.py
+++ b/solution.py
@@ -39,17 +39,31 @@
 
 
 def east(value, halo):
-    lane = iota(value.shape[0], 1)
-    return roll(jnp.where(lane == 0, halo, value), -1, 1)
+    return jnp.where(iota(value.shape[0], 1) == LANES - 1, halo, roll(value, -1, 1))
 
 
 def west(value, halo):
-    lane = iota(value.shape[0], 1)
-    return roll(jnp.where(lane == LANES - 1, halo, value), 1, 1)
+    return jnp.where(iota(value.shape[0], 1) == 0, halo, roll(value, 1, 1))
 
 
 def rim(tile, base):
     return roll(tile, LANES - 2 - base, 1)
+
+
+def crossed(tile):
+    column = iota(tile.shape[0], 1) % 4
+    return jnp.where(
+        column == 1, roll(tile, -1, 1), jnp.where(column == 2, roll(tile, 1, 1), tile)
+    )
+
+
+def loop(count, body, carry, together=1):
+    def several(n, carry):
+        for m in range(together):
+            carry = body(n * together + m, carry)
+        return carry
+
+    return lax.fori_loop(0, count // together, several, carry)
 
 
 def north(value, beyond):
@@ -120,7 +134,7 @@
             fields[k, 2 + t] = values[t]
         return (bond_here, inverse, *values)
 
-    lax.fori_loop(0, depth, down, (zero, zero, zero, zero))
+    loop(depth, down, (zero, zero, zero, zero), 4)
     for copy in copies[4:]:
         copy.wait()
     level_f = level.astype(jnp.float32)
@@ -149,7 +163,7 @@
         message[depth // PER_TILE + tile] = jnp.where(place == FILLER, code, second)
         return (bond_above, inverse, *values)
 
-    lax.fori_loop(0, depth, up, (zero, zero, zero, zero))
+    loop(depth, up, (zero, zero, zero, zero), 4)
 
 
 def pack_rows(near, far, fields, mix_h, mix_v, levels, lower, upper, merged):
@@ -169,11 +183,11 @@
         tile = jnp.where(from_west, west_tile, east_tile)
         if j >= tiles:
             tile = jnp.where(missing, 0.0, tile)
-        merged[j] = tile
+        merged[j] = crossed(tile)
         other = jnp.where(
             column == 0, roll(west_tile, -2, 1), jnp.where(column == 3, roll(east_tile, 2, 1), tile)
         )
-        corners.append(fold(other))
+        corners.append(crossed(fold(other)))
     sub = iota(8, 0)
     level_all = levels[...].astype(jnp.float32)
     level = fold(level_all)
@@ -225,7 +239,7 @@
             upper[at] = array[k, ROWS - 1 :]
         return 0
 
-    lax.fori_loop(0, depth, row, 0)
+    loop(depth, row, 0, 4)
 
 
 def finish(
@@ -297,8 +311,8 @@
 
     def around(value, mine, below_row, above_row):
         return (
-            jnp.where(column == 1, roll(mine, -1, 1), roll(mine, 1, 1)),
-            jnp.where(column == 1, roll(value, 1, 1), roll(value, -1, 1)),
+            mine,
+            jnp.where(column == 1, roll(value, -2, 1), roll(value, 2, 1)),
             north(value, above_row),
             south(value, below_row),
         )
@@ -309,7 +323,7 @@
     for target, edge in ((below, 0), (above, last)):
         block = target[base_level : base_level + 8]
         swap = (place == edge) & (turned > 0.5)
-        swapped = jnp.where(spot == 1, roll(block, 1, 1), roll(block, -1, 1))
+        swapped = jnp.where(spot == 1, roll(block, -2, 1), roll(block, 2, 1))
         corner_rows.append(jnp.where(swap, swapped, block))
     for j in range(tiles):
         corner = [block[1 + j : 2 + j] for block in corner_rows]
@@ -430,9 +444,7 @@
             inside[k, q] = values[q]
         return (row_carry, col_carry, tuple(values))
 
-    lax.fori_loop(
-        0, depth, first, ((zero_rows,) * 3, (zero,) * 3, (zero,) * 4)
-    )
+    loop(depth, first, ((zero_rows,) * 3, (zero,) * 3, (zero,) * 4), 4)
 
     def second(n, carry):
         row_value, col_value, values, later_values = carry
@@ -473,7 +485,7 @@
         grad_h[k] = -0.5 * total
         return (row_value, col_value, tuple(values), tuple(later_values))
 
-    lax.fori_loop(0, depth, second, (zero_rows, zero, (zero,) * 4, (zero,) * 2))
+    loop(depth, second, (zero_rows, zero, (zero,) * 4, (zero,) * 2), 4)
     copies = [
         pltpu.make_async_copy(source, target, sems.at[n])
         for n, (source, target) in enumerate(
@@ -498,7 +510,7 @@
         grad_v[jnp.maximum(k - 1, 0)] = -0.5 * (face + face_above)
         return face, tuple(later_here), tuple(inside_here), tuple(fields_here)
 
-    face = lax.fori_loop(0, depth, third, (zero, (zero,) * 2, (zero,) * 4, (zero,) * 2))[0]
+    face = loop(depth, third, (zero, (zero,) * 2, (zero,) * 4, (zero,) * 2), 4)[0]
     grad_v[depth - 1] = -0.5 * face
     copies[2].start()
     for copy in copies:

time: 27 us -> 20.7 us (0.77)
  Pallas kernels: 12.6 us -> 6.28 us
    pallas_call x1, Pallas kernels: 7 us -> 3.53 us  [per_device(): pl.pallas_call(finish, out_shape=(jax.ShapeDtypeStruct(tracers.shape, jnp...]
    pallas_call x1, Pallas kernels: 2.69 us -> 0.83 us  [per_device(): pl.pallas_call(pack_rows, out_shape=(vmem_out(height, LANES), vmem_out(he...]
    pallas_call x1, Pallas kernels: 2.89 us -> 1.91 us  [per_device(): pl.pallas_call(prepare, out_shape=(vmem_out(depth, 4, *tile), vmem_out(6,...]
where the time goes in v1:
time: 20.7 us; the launch traced here: 20.5 us
  starting transfers between devices  7.77 us (38%)
  Pallas kernels  6.28 us (30%)
  waiting for transfers between devices  5.13 us (25%)
  between operations  1.3 us (6%)
    pallas_call x1, Pallas kernels, per_device(): pl.pallas_call(finish, out_shape=(jax.ShapeDtypeStruct(tracers.shape, jnp...  3.53 us
    ppermute x1, waiting for transfers between devices, per_device(): lax.ppermute(upper, 'tx', [(i, (i + 1) % count) for i in range(count)])  3.14 us
    ppermute x1, starting transfers between devices, per_device(): lax.ppermute(upper, 'tx', [(i, (i + 1) % count) for i in range(count)])  2.56 us
    ppermute x1, starting transfers between devices, per_device(): far = lax.ppermute(own, 'ty', far_pairs)  2.44 us
    ppermute x1, starting transfers between devices, per_device(): lax.ppermute(lower, 'tx', [(i, (i - 1) % count) for i in range(count)])  2.09 us
    pallas_call x1, Pallas kernels, per_device(): pl.pallas_call(prepare, out_shape=(vmem_out(depth, 4, *tile), vmem_out(6,...  1.91 us
    ppermute x1, waiting for transfers between devices, per_device(): far = lax.ppermute(own, 'ty', far_pairs)  1.1 us
    ppermute x1, waiting for transfers between devices, per_device(): lax.ppermute(lower, 'tx', [(i, (i - 1) % count) for i in range(count)])  0.88 us
  transfers between devices with their start and end apart: 4, of which 3 were waited for; matrix products, arithmetic and copies ran while one was open for 0% of the time, Pallas kernels for 0%

profile of v1, /device:TPU:0, one launch (start us, length us, event | category | flops | bytes accessed | tf_op | source)
XLA Modules:
  0.0 20.5 jit_solution(12688538436537379072)
XLA Ops:
  1.3 1.9 %prepare.1 = (f32[16,4,16,128]{3,2,1,0:T(8,128)S(1)}, f32[6,16,16,128]{3,2,1,0:T(8,128)S(1)}, f32[4,16,128]{2,1,0:T(8,128)S(1)}, f32[16,16,128]{2,1,0:T(8,128)S(...) custom-call(s32[1]{0:T(128)S(6)} %copy.9.seam, f32[2,16,16,128]{3,2,1,0:T(8,128)} %tracers.1, ...), custom_call_target="tpu_custom_call" | custom-call | tf_op jit(solution)/shard_map/prepare/pallas_call | solution.py:529
  3.2 2.4 %collective-permute-start.1 = (f32[4,16,128]{2,1,0:T(8,128)S(1)}, f32[4,16,128]{2,1,0:T(8,128)S(1)}, u32[]{:S(2)}, u32[]{:S(2)}) collective-permute-start(f32[4,16,128]{2,1,0:T(8,128)S(1)} %get-tuple-element.12.own), channel_id=1, source_target_pairs={{0,3},{1,2},{2,1},{3,0},{4,7},{5,6},{6,5},{7,4},{8,11},{9,10},{10,... | collective-permute-start | bytes 98312 | tf_op jit(solution)/shard_map/ppermute | solution.py:548
  5.6 0.7 %collective-permute-start = (f32[4,16,128]{2,1,0:T(8,128)S(1)}, f32[4,16,128]{2,1,0:T(8,128)S(1)}, u32[]{:S(2)}, u32[]{:S(2)}) collective-permute-start(f32[4,16,128]{2,1,0:T(8,128)S(1)} %get-tuple-element.12.own), channel_id=1, source_target_pairs={{0,1},{1,0},{2,3},{3,2},{4,5},{5,4},{6,7},{7,6},{8,9},{9,8},{10,11... | collective-permute-start | bytes 98312 | tf_op jit(solution)/shard_map/ppermute | solution.py:549
  6.3 1.1 %collective-permute-done.1.far = f32[4,16,128]{2,1,0:T(8,128)S(1)} collective-permute-done((f32[4,16,128]{2,1,0:T(8,128)S(1)}, f32[4,16,128]{2,1,0:T(8,128)S(1)}, u32[]{:S(2)}, u32[]{:S(2)}) %collective-permute-start.1) | collective-permute-done | bytes 32800 | tf_op jit(solution)/shard_map/ppermute | solution.py:548
  7.4 0.0 collective-permute-done.near
  7.4 0.8 %pack_rows.1 = (f32[168,128]{1,0:T(8,128)S(1)}, f32[168,128]{1,0:T(8,128)S(1)}, f32[4,16,128]{2,1,0:T(8,128)S(1)}) custom-call(f32[4,16,128]{2,1,0:T(8,128)S(1)} %collective-permute-done.near, f32[4,16,128]{2,1,0:T(8,128)S(1)} %collective-permute-done.1.far, f32[16,4,16,128]{3,2,1,0:T(8,128)S(1)} %get-tuple-element.13.fields, ...), custom_call_target="tpu_custom_call" | custom-call | tf_op jit(solution)/shard_map/pack_rows/pallas_call | solution.py:550
  8.3 2.6 %collective-permute-start.2 = (f32[168,128]{1,0:T(8,128)S(1)}, f32[168,128]{1,0:T(8,128)S(1)}, u32[]{:S(2)}, u32[]{:S(2)}) collective-permute-start(f32[168,128]{1,0:T(8,128)S(1)} %get-tuple-element.17.upper), channel_id=1, source_target_pairs={{0,4},{4,8},{8,12},{12,0},{1,5},{5,9},{9,13},{13,1},{2,6},{6,10},{... | collective-permute-start | bytes 258056 | tf_op jit(solution)/shard_map/ppermute | solution.py:562
  10.8 2.1 %collective-permute-start.3 = (f32[168,128]{1,0:T(8,128)S(1)}, f32[168,128]{1,0:T(8,128)S(1)}, u32[]{:S(2)}, u32[]{:S(2)}) collective-permute-start(f32[168,128]{1,0:T(8,128)S(1)} %get-tuple-element.18.lower), channel_id=1, source_target_pairs={{0,12},{4,0},{8,4},{12,8},{1,13},{5,1},{9,5},{13,9},{2,14},{6,2},{... | collective-permute-start | bytes 258056 | tf_op jit(solution)/shard_map/ppermute | solution.py:563
  12.9 3.1 %collective-permute-done.2.from_below = f32[168,128]{1,0:T(8,128)S(1)} collective-permute-done((f32[168,128]{1,0:T(8,128)S(1)}, f32[168,128]{1,0:T(8,128)S(1)}, u32[]{:S(2)}, u32[]{:S(2)}) %collective-permute-start.2) | collective-permute-done | bytes 86048 | tf_op jit(solution)/shard_map/ppermute | solution.py:562
  16.1 0.9 %collective-permute-done.3.from_above = f32[168,128]{1,0:T(8,128)S(1)} collective-permute-done((f32[168,128]{1,0:T(8,128)S(1)}, f32[168,128]{1,0:T(8,128)S(1)}, u32[]{:S(2)}, u32[]{:S(2)}) %collective-permute-start.3) | collective-permute-done | bytes 86048 | tf_op jit(solution)/shard_map/ppermute | solution.py:563
  16.9 3.5 %finish.1 = (f32[2,16,16,128]{3,2,1,0:T(8,128)}, f32[16,16,128]{2,1,0:T(8,128)}, f32[16,16,128]{2,1,0:T(8,128)}) custom-call(s32[1]{0:T(128)S(6)} %copy.9.seam, f32[168,128]{1,0:T(8,128)S(1)} %collective-permute-done.2.from_below, f32[168,128]{1,0:T(8,128)S(1)} %collective-permute-done.3.from_above, f32[168,128]{1,0:T(8,128)S(1)} %get-tuple-element.18.lower, ...), custom_call_target="tpu_custom_call" | custom-call | tf_op jit(solution)/shard_map/finish/pallas_call | solution.py:565
Async XLA Ops:
  3.2 4.2 %collective-permute-start.1 = (f32[4,16,128]{2,1,0:T(8,128)S(1)}, f32[4,16,128]{2,1,0:T(8,128)S(1)}, u32[]{:S(2)}, u32[]{:S(2)}) collective-permute-start(f32[4,16,128]{2,1,0:T(8,128)S(1)} %get-tuple-element.12.own), channel_id=1, source_target_pairs={{0,3},{1,2},{2,1},{3,0},{4,7},{5,6},{6,5},{7,4},{8,11},{9,10},{10,... | collective-permute-start | bytes 98312 | tf_op jit(solution)/shard_map/ppermute | solution.py:548
  5.6 1.8 %collective-permute-start = (f32[4,16,128]{2,1,0:T(8,128)S(1)}, f32[4,16,128]{2,1,0:T(8,128)S(1)}, u32[]{:S(2)}, u32[]{:S(2)}) collective-permute-start(f32[4,16,128]{2,1,0:T(8,128)S(1)} %get-tuple-element.12.own), channel_id=1, source_target_pairs={{0,1},{1,0},{2,3},{3,2},{4,5},{5,4},{6,7},{7,6},{8,9},{9,8},{10,11... | collective-permute-start | bytes 98312 | tf_op jit(solution)/shard_map/ppermute | solution.py:549
  8.3 7.8 %collective-permute-start.2 = (f32[168,128]{1,0:T(8,128)S(1)}, f32[168,128]{1,0:T(8,128)S(1)}, u32[]{:S(2)}, u32[]{:S(2)}) collective-permute-start(f32[168,128]{1,0:T(8,128)S(1)} %get-tuple-element.17.upper), channel_id=1, source_target_pairs={{0,4},{4,8},{8,12},{12,0},{1,5},{5,9},{9,13},{13,1},{2,6},{6,10},{... | collective-permute-start | bytes 258056 | tf_op jit(solution)/shard_map/ppermute | solution.py:562
  10.8 6.1 %collective-permute-start.3 = (f32[168,128]{1,0:T(8,128)S(1)}, f32[168,128]{1,0:T(8,128)S(1)}, u32[]{:S(2)}, u32[]{:S(2)}) collective-permute-start(f32[168,128]{1,0:T(8,128)S(1)} %get-tuple-element.18.lower), channel_id=1, source_target_pairs={{0,12},{4,0},{8,4},{12,8},{1,13},{5,1},{9,5},{13,9},{2,14},{6,2},{... | collective-permute-start | bytes 258056 | tf_op jit(solution)/shard_map/ppermute | solution.py:563

commit v2 on v1

v2 whole, which is shorter than its diff:
```python
import jax
import jax.numpy as jnp
from jax import lax
from jax.experimental import pallas as pl
from jax.experimental.pallas import tpu as pltpu
from jax.sharding import PartitionSpec as P

LANES = 128
ROWS = 16
GROUP = 16
PER_TILE = LANES // GROUP


FILLER = 3


def in_vmem(array):
    return pltpu.with_memory_space_constraint(array, pltpu.VMEM)


def in_hbm(array):
    return pltpu.with_memory_space_constraint(array, pltpu.HBM)


def vmem_out(*shape):
    return pltpu.VMEM(shape, jnp.float32)


def iota(rows, dim):
    return lax.broadcasted_iota(jnp.int32, (rows, LANES), dim)


def roll(value, shift, axis):
    return pltpu.roll(value, shift % value.shape[axis], axis)


def fold(value):
    return jnp.where(iota(8, 0) < 4, value[:8], value[8:])


def east(value, halo):
    return jnp.where(iota(value.shape[0], 1) == LANES - 1, halo, roll(value, -1, 1))


def west(value, halo):
    return jnp.where(iota(value.shape[0], 1) == 0, halo, roll(value, 1, 1))


def rim(tile, base):
    return roll(tile, LANES - 2 - base, 1)


def crossed(tile):
    column = iota(tile.shape[0], 1) % 4
    return jnp.where(
        column == 1, roll(tile, -1, 1), jnp.where(column == 2, roll(tile, 1, 1), tile)
    )


def loop(count, body, carry):
    for n in range(count):
        carry = body(n, carry)
    return carry


def north(value, beyond):
    sub = iota(8, 0)
    low, high = roll(value[:8], -1, 0), roll(value[8:], -1, 0)
    return jnp.concatenate([jnp.where(sub == 7, high, low), jnp.where(sub == 7, beyond, high)], axis=0)


def south(value, beyond):
    sub = iota(8, 0)
    low, high = roll(value[:8], 1, 0), roll(value[8:], 1, 0)
    return jnp.concatenate([jnp.where(sub == 0, beyond, low), jnp.where(sub == 0, low, high)], axis=0)


def bond(mix_v, level, k, depth):
    if k in (-1, depth - 1):
        return jnp.zeros(level.shape, jnp.float32)
    return jnp.where(level > k + 1, 0.5 * (mix_v[k] + mix_v[k + 1]), 0.0)


def prepare(
    seam,
    tracers,
    costate,
    mix_h_in,
    mix_v_in,
    levels_in,
    fields,
    factors,
    message,
    mix_h,
    mix_v,
    levels,
    sems,
):
    depth = mix_h.shape[0]
    copies = [
        pltpu.make_async_copy(source, target, sems.at[n])
        for n, (source, target) in enumerate(
            (
                (levels_in, levels),
                (mix_v_in, mix_v),
                (costate.at[0], fields.at[:, 2]),
                (costate.at[1], fields.at[:, 3]),
                (tracers.at[0], fields.at[:, 0]),
                (tracers.at[1], fields.at[:, 1]),
                (mix_h_in, mix_h),
            )
        )
    ]
    for copy in copies:
        copy.start()
    for copy in copies[:4]:
        copy.wait()
    level = levels[...]
    lane = iota(ROWS, 1)
    zero = jnp.zeros((ROWS, LANES), jnp.float32)

    def down(k, carry):
        bond_above, inverse, *values = carry
        bond_here = bond(mix_v, level, k, depth)
        inverse = 1.0 / (1.0 + bond_above + bond_here - bond_above * (bond_above * inverse))
        factor = bond_above * inverse
        factors[0, k] = inverse
        factors[1, k] = factor
        factors[2, k] = bond_here * inverse
        for t in range(2):
            values[t] = fields[k, 2 + t] * inverse + factor * values[t]
            fields[k, 2 + t] = values[t]
        return (bond_here, inverse, *values)

    loop(depth, down, (zero, zero, zero, zero))
    for copy in copies[4:]:
        copy.wait()
    level_f = level.astype(jnp.float32)
    code = zero + seam[0].astype(jnp.float32)

    def up(n, carry):
        k = depth - 1 - n
        bond_here, inverse, *values = carry
        for t in range(2):
            values[t] = fields[k, 2 + t] + factors[2, k] * values[t]
            fields[k, 2 + t] = values[t]
        bond_above = bond(mix_v, level, k - 1, depth)
        inverse = 1.0 / (1.0 + bond_above + bond_here - bond_here * (bond_here * inverse))
        factors[3, k] = inverse
        factors[4, k] = bond_here * inverse
        factors[5, k] = bond_above * inverse
        tile, base = k // PER_TILE, GROUP * (k % PER_TILE)
        place = lane // 4 - base // 4
        first = message[tile]
        for q, value in enumerate((fields[k, 0], fields[k, 1], values[0], values[1])):
            first = jnp.where(place == q, roll(value, base + 4 * q + 2, 1), first)
        message[tile] = first
        second = message[depth // PER_TILE + tile]
        for q, value in enumerate((mix_h[k], mix_v[k], level_f)):
            second = jnp.where(place == q, roll(value, base + 4 * q + 2, 1), second)
        message[depth // PER_TILE + tile] = jnp.where(place == FILLER, code, second)
        return (bond_above, inverse, *values)

    loop(depth, up, (zero, zero, zero, zero))


def pack_rows(near, far, fields, mix_h, mix_v, levels, lower, upper, merged):
    depth = mix_h.shape[0]
    tiles = depth // PER_TILE
    place = lax.axis_index("ty")
    last = lax.axis_size("ty") - 1
    even = place % 2 == 0
    column = iota(ROWS, 1) % 4
    from_west = column < 2
    missing = ((place == 0) & from_west) | ((place == last) & jnp.logical_not(from_west))
    base_level = 10 * depth
    corners = []
    for j in range(2 * tiles):
        west_tile = jnp.where(even, far[j], near[j])
        east_tile = jnp.where(even, near[j], far[j])
        tile = jnp.where(from_west, west_tile, east_tile)
        if j >= tiles:
            tile = jnp.where(missing, 0.0, tile)
        merged[j] = crossed(tile)
        other = jnp.where(
            column == 0, roll(west_tile, -2, 1), jnp.where(column == 3, roll(east_tile, 2, 1), tile)
        )
        corners.append(crossed(fold(other)))
    sub = iota(8, 0)
    level_all = levels[...].astype(jnp.float32)
    level = fold(level_all)
    for target, row in ((lower, 0), (upper, 7)):
        block = jnp.zeros((8, LANES), jnp.float32)
        for n, value in enumerate([level, *corners]):
            block = jnp.where(sub == n, roll(value, n - row, 0), block)
        target[base_level : base_level + 8] = block

    def inner(value):
        return jnp.where(sub < 4, roll(value, -1, 0), roll(value, 1, 0))

    level_rim = rim(fold(merged[tiles]), 8)
    shallow = [
        jnp.minimum(level, near_level)
        for near_level in (east(level, level_rim), west(level, level_rim), inner(level))
    ]

    def row(k, _):
        tile, base = k // PER_TILE, GROUP * (k % PER_TILE)
        coefs = fold(merged[tiles + tile])
        mix = fold(mix_h[k])
        mix_rim = rim(coefs, base)
        mixes = (east(mix, mix_rim), west(mix, mix_rim), inner(mix))
        weights = [
            jnp.where(open_to > float(k), 0.5 * (mix + near_mix), 0.0)
            for open_to, near_mix in zip(shallow, mixes)
        ]
        packed = fold(merged[tile])
        low = jnp.zeros((8, LANES), jnp.float32)
        high = low
        for q in range(4):
            value = fold(fields[k, q])
            halo = rim(packed, base + 4 * q)
            part = value
            for near_value, weight in zip(
                (east(value, halo), west(value, halo), inner(value)), weights
            ):
                part = part + weight * (near_value - value)
            for n, thing in ((q, value), (4 + q, part)):
                low = jnp.where(sub == n, roll(thing, n, 0), low)
                high = jnp.where(sub == n, roll(thing, n - 7, 0), high)
        at = slice(8 * k, 8 * k + 8)
        lower[at] = low
        upper[at] = high
        for n, array in enumerate((mix_h, mix_v)):
            at = slice((8 + n) * depth + k, (8 + n) * depth + k + 1)
            lower[at] = array[k, :1]
            upper[at] = array[k, ROWS - 1 :]
        return 0

    loop(depth, row, 0)


def both(low, high):
    return jnp.where(iota(8, 0) < 4, low, high)


def coefficient(value, n):
    kept = iota(value.shape[0], 1) % GROUP // 4 == n
    value = roll(jnp.where(kept, value, 0.0), -4 * n, 1)
    value = value + roll(value, 4, 1)
    return value + roll(value, 8, 1)


def pivot(bond_above, bond_here, inverse):
    return 1.0 / (1.0 + bond_above + bond_here - bond_above * (bond_above * inverse))


def near_all(value, halo, below_row=0.0, above_row=0.0):
    return (
        north(value, above_row),
        south(value, below_row),
        east(value, halo),
        west(value, halo),
    )


def steps_of(fields, merged, k, q):
    value = fields[k, q]
    halo = rim(merged[k // PER_TILE], GROUP * (k % PER_TILE) + 4 * q)
    return value, [near - value for near in near_all(value, halo)]


def interior(
    merged,
    own,
    fields,
    factors,
    mix_h,
    levels,
    inside,
    columns,
    column_factors,
    weights,
    adjoint,
    grad_h,
    grad_v,
    packed,
    later,
):
    depth = mix_h.shape[0]
    tiles = depth // PER_TILE
    lane = iota(ROWS, 1)
    zero = jnp.zeros((ROWS, LANES), jnp.float32)

    column = lane % 4

    def around(value, mine):
        return (
            mine,
            jnp.where(column == 1, roll(value, -2, 1), roll(value, 2, 1)),
            north(value, 0.0),
            south(value, 0.0),
        )

    for j in range(tiles):
        level_k = (lane // GROUP + j * PER_TILE).astype(jnp.float32)
        here = [coefficient(merged[tiles + j], n) for n in range(3)]
        (mix, mixes), (level, level_near) = [
            (here[n], around(here[n], coefficient(own[tiles + j], n))) for n in (0, 2)
        ]
        value = merged[j]
        mixed = value
        for near, near_mix, near_level in zip(around(value, own[j]), mixes, level_near):
            weight = jnp.where(
                jnp.minimum(level, near_level) > level_k, 0.5 * (mix + near_mix), 0.0
            )
            mixed = mixed + weight * (near - value)
        packed[0, j] = mixed
        packed[1, j] = here[1]
        if j == 0:
            level_columns = level

    def unpacked(n, k):
        return roll(packed[n, k // PER_TILE], -GROUP * (k % PER_TILE), 1)

    level = levels[...].astype(jnp.float32)
    shallow = [jnp.minimum(level, near) for near in near_all(level, rim(merged[tiles], 8))]

    def first(k, carry):
        (col_bond, col_inverse, col_value), values = carry
        under = min(k + 1, depth - 1)
        bond_here = jnp.where(
            level_columns > k + 1.0, 0.5 * (unpacked(1, k) + unpacked(1, under)), 0.0
        )
        col_inverse = pivot(col_bond, bond_here, col_inverse)
        col_factor = col_bond * col_inverse
        col_value = unpacked(0, k) * col_inverse + col_factor * col_value
        columns[k] = col_value
        column_factors[0, k] = col_inverse
        column_factors[1, k] = col_factor
        column_factors[2, k] = bond_here * col_inverse
        mix = mix_h[k]
        mix_rim = rim(merged[tiles + k // PER_TILE], GROUP * (k % PER_TILE))
        weight = [
            jnp.where(open_to > float(k), 0.5 * (mix + near), 0.0)
            for open_to, near in zip(shallow, near_all(mix, mix_rim))
        ]
        for n in range(4):
            weights[k, n] = weight[n]
        inverse, factor = factors[0, k], factors[1, k]
        values = list(values)
        for q in range(4):
            value, steps = steps_of(fields, merged, k, q)
            for n in range(4):
                value = value + weight[n] * steps[n]
            values[q] = value * inverse + factor * values[q]
            inside[k, q] = values[q]
        return (bond_here, col_inverse, col_value), tuple(values)

    loop(depth, first, ((zero,) * 3, (zero,) * 4))

    def second(n, carry):
        col_value, values, later_values = carry
        k = depth - 1 - n
        col_value = columns[k] + column_factors[2, k] * col_value
        columns[k] = col_value
        values, later_values = list(values), list(later_values)
        first_steps, later_steps = [], []
        for q in range(4):
            value = inside[k, q] + factors[2, k] * values[q]
            inside[k, q] = value
            values[q] = value
            steps = [near - value for near in near_all(value, rim(col_value, 4 * q))]
            later_steps.append(steps)
            first_steps.append(steps_of(fields, merged, k, q)[1])
            for n in range(4):
                value = value + weights[k, n] * steps[n]
            if q < 2:
                later_values[q] = value * factors[3, k] + factors[4, k] * later_values[q]
                later[k, q] = later_values[q]
            else:
                adjoint[q - 2, k] = value
        total = zero
        for n in range(4):
            face = zero
            for t in range(2):
                face = face + first_steps[t][n] * later_steps[2 + t][n]
                face = face + later_steps[t][n] * first_steps[2 + t][n]
            total = total + jnp.where(shallow[n] > float(k), face, 0.0)
        grad_h[k] = -0.5 * total
        return col_value, tuple(values), tuple(later_values)

    loop(depth, second, (zero, (zero,) * 4, (zero,) * 2))
    vertical_gradient(
        depth,
        level,
        lambda i: factors[5, i],
        lambda k, q: inside[k, q],
        lambda k, t: fields[k, 2 + t],
        lambda k, t: later[k, t],
        grad_v,
    )


def vertical_gradient(depth, level, factor, inside, ahead, later, put):
    zero = jnp.zeros(level.shape, jnp.float32)
    face_above = zero
    later_above = inside_above = ahead_above = None
    for k in range(depth):
        inside_here = [inside(k, q) for q in range(4)]
        ahead_here = [ahead(k, t) for t in range(2)]
        later_here = [later(k, t) for t in range(2)]
        if k > 0:
            later_here = [later_here[t] + factor(k) * later_above[t] for t in range(2)]
            total = zero
            for t in range(2):
                total = total + (inside_above[2 + t] - inside_here[2 + t]) * (
                    inside_above[t] - inside_here[t]
                )
                total = total + (ahead_above[t] - ahead_here[t]) * (
                    later_above[t] - later_here[t]
                )
            face = jnp.where(level > float(k), total, 0.0)
            put[k - 1] = -0.5 * (face + face_above)
            face_above = face
        later_above, inside_above, ahead_above = later_here, inside_here, ahead_here
    put[depth - 1] = -0.5 * face_above


def finish(
    seam,
    from_below,
    from_above,
    lower,
    upper,
    merged,
    fields,
    factors,
    levels,
    inside,
    columns,
    column_factors,
    weights,
    adjoint_in,
    grad_h_in,
    grad_v_in,
    adjoint_out,
    grad_h_out,
    grad_v_out,
    below,
    above,
    out_rows,
    in_rows,
    corners,
    faces,
    later,
    edge_v,
    adjoint,
    grad_h,
    grad_v,
    sems,
):
    depth = fields.shape[0]
    tiles = depth // PER_TILE
    sub = iota(8, 0)
    lane = iota(8, 1)
    place = lax.axis_index("tx")
    last = lax.axis_size("tx") - 1
    base_mix, base_v, base_level = 8 * depth, 9 * depth, 10 * depth
    zero = jnp.zeros((8, LANES), jnp.float32)

    for source, target, edge in ((from_below, below, 0), (from_above, above, last)):
        turn = (seam[0] == 1) & (place == edge)

        @pl.when(turn)
        def _():
            back = LANES - 1 - lane
            for r in range(0, base_level, 8):
                target[r : r + 8] = jnp.take_along_axis(source[r : r + 8], back, axis=1)
            block = source[base_level : base_level + 8]
            target[base_level : base_level + 8] = jnp.where(
                sub < 1, jnp.take_along_axis(block, back, axis=1), block
            )

        @pl.when(jnp.logical_not(turn))
        def _():
            for r in range(0, base_level + 8, 8):
                target[r : r + 8] = source[r : r + 8]

    def ends(low, high, between=0.0):
        return jnp.where(sub == 0, low, jnp.where(sub == 7, high, between))

    folded = [fold(merged[j]) for j in range(2 * tiles)]
    turned = coefficient(folded[tiles], FILLER)
    corner_rows = []
    for target, edge in ((below, 0), (above, last)):
        block = target[base_level : base_level + 8]
        swap = (place == edge) & (turned[:1] > 0.5)
        swapped = jnp.where(lane % 4 == 1, roll(block, -2, 1), roll(block, 2, 1))
        corner_rows.append(jnp.where(swap, swapped, block))
    corner_flow = []
    for j in range(tiles):
        value, coefs = [
            ends(corner_rows[0][r : r + 1], corner_rows[1][r : r + 1])
            for r in (1 + j, 1 + tiles + j)
        ]
        level_k = (lane // GROUP + j * PER_TILE).astype(jnp.float32)
        mix, level = [
            (coefficient(coefs, n), coefficient(folded[tiles + j], n)) for n in (0, 2)
        ]
        weight = jnp.where(jnp.minimum(*level) > level_k, 0.5 * (mix[0] + mix[1]), 0.0)
        corner_flow.append(ends(1.0, 1.0) * weight * (value - folded[j]))

    def level_row(ref):
        return ref[base_level : base_level + 1]

    level_out = both(level_row(below), level_row(above))
    level_face = jnp.minimum(level_out, both(level_row(lower), level_row(upper)))

    def row_at(ref, start, k):
        return ref[start + k : start + k + 1]

    def mix_v_out(k):
        return both(row_at(below, base_v, k), row_at(above, base_v, k))

    def first(k, carry):
        bond_above, inverse, out_value, in_value, corner_value = carry
        block = slice(8 * k, 8 * k + 8)
        below_block, above_block = below[block], above[block]
        bond_here = jnp.where(
            level_out > k + 1.0, 0.5 * (mix_v_out(k) + mix_v_out(min(k + 1, depth - 1))), 0.0
        )
        inverse = pivot(bond_above, bond_here, inverse)
        out = both(below_block, roll(above_block, 4, 0))
        part = both(roll(below_block, 4, 0), above_block)
        inn = both(lower[block], roll(upper[block], 4, 0))
        mixes = 0.5 * (
            both(row_at(below, base_mix, k), row_at(above, base_mix, k))
            + both(row_at(lower, base_mix, k), row_at(upper, base_mix, k))
        )
        weight = jnp.where(level_face > float(k), mixes, 0.0)
        faces[k] = weight
        flow = weight * (inn - out)
        out_value = (part + flow) * inverse + bond_above * inverse * out_value
        out_rows[0, k] = out_value
        out_rows[1, k] = bond_here * inverse
        own = [both(factors[n, k, :1], factors[n, k, ROWS - 1 :]) for n in range(2)]
        in_value = own[1] * in_value - flow * own[0]
        in_rows[k] = in_value
        added = roll(corner_flow[k // PER_TILE], -GROUP * (k % PER_TILE), 1)
        corner_value = added * fold(column_factors[0, k]) + fold(column_factors[1, k]) * corner_value
        corners[k] = corner_value
        return bond_here, inverse, out_value, in_value, corner_value

    loop(depth, first, (zero,) * 5)

    level = fold(levels[...].astype(jnp.float32))
    level_rim = rim(folded[tiles], 8)

    def near_ends(value, halo, below_row, above_row):
        return (
            jnp.where(sub == 7, above_row, roll(value, -1, 0)),
            jnp.where(sub == 0, below_row, roll(value, 1, 0)),
            east(value, halo),
            west(value, halo),
        )

    shallow = [
        jnp.minimum(level, near)
        for near in near_ends(level, level_rim, level_row(below), level_row(above))
    ]

    def second(n, carry):
        out_value, in_value, corner_value, later_values = carry
        k = depth - 1 - n
        block = slice(8 * k, 8 * k + 8)
        below_block, above_block = below[block], above[block]
        out_value = out_rows[0, k] + out_rows[1, k] * out_value
        in_value = in_rows[k] + both(factors[2, k, :1], factors[2, k, ROWS - 1 :]) * in_value
        corner_value = corners[k] + fold(column_factors[2, k]) * corner_value
        column = fold(columns[k]) + corner_value
        face = faces[k]
        weight = [fold(weights[k, n]) for n in range(4)]
        weight[0] = jnp.where(sub == 7, face[4:5], weight[0])
        weight[1] = jnp.where(sub == 0, face[:1], weight[1])
        later_values = list(later_values)
        first_steps, later_steps = [], []
        for q in range(4):
            value = fold(fields[k, q])
            halo = rim(folded[k // PER_TILE], GROUP * (k % PER_TILE) + 4 * q)
            nears = near_ends(value, halo, below_block[q : q + 1], above_block[q : q + 1])
            first_steps.append([near - value for near in nears])
            value = fold(inside[k, q]) + ends(in_value[q : q + 1], in_value[4 + q : 5 + q])
            edge_v[k, q] = value
            nears = near_ends(
                value, rim(column, 4 * q), out_value[q : q + 1], out_value[4 + q : 5 + q]
            )
            steps = [near - value for near in nears]
            later_steps.append(steps)
            for n in range(4):
                value = value + weight[n] * steps[n]
            if q < 2:
                later_values[q] = (
                    value * fold(factors[3, k]) + fold(factors[4, k]) * later_values[q]
                )
                later[k, q] = later_values[q]
            else:
                merge_ends(adjoint, adjoint_in, (q - 2, k), value)
        total = zero
        for n in range(4):
            product = zero
            for t in range(2):
                product = product + first_steps[t][n] * later_steps[2 + t][n]
                product = product + later_steps[t][n] * first_steps[2 + t][n]
            total = total + jnp.where(shallow[n] > float(k), product, 0.0)
        merge_ends(grad_h, grad_h_in, (k,), -0.5 * total)
        return out_value, in_value, corner_value, tuple(later_values)

    def merge_ends(target, source, at, value):
        target[(*at, slice(0, 8))] = jnp.where(sub < 2, value, source[(*at, slice(0, 8))])
        target[(*at, slice(8, 16))] = jnp.where(sub < 6, source[(*at, slice(8, 16))], value)

    loop(depth, second, (zero, zero, zero, (zero, zero)))
    copies = [
        pltpu.make_async_copy(source, target, sems.at[n])
        for n, (source, target) in enumerate(
            ((adjoint, adjoint_out), (grad_h, grad_h_out), (grad_v, grad_v_out))
        )
    ]
    copies[0].start()
    copies[1].start()

    class Merged:
        def __setitem__(self, k, value):
            merge_ends(grad_v, grad_v_in, (k,), value)

    vertical_gradient(
        depth,
        level,
        lambda i: fold(factors[5, i]),
        lambda k, q: edge_v[k, q],
        lambda k, t: fold(fields[k, 2 + t]),
        lambda k, t: later[k, t],
        Merged(),
    )
    copies[2].start()
    for copy in copies:
        copy.wait()


def per_device(tracers, costate, mixing_h, mixing_v, levels, seam_code):
    depth = tracers.shape[1]
    tiles = depth // PER_TILE
    height = 10 * depth + 8
    params = pltpu.CompilerParams(vmem_limit_bytes=48 * 2**20)
    smem = pl.BlockSpec(memory_space=pltpu.SMEM)
    vmem = pl.BlockSpec(memory_space=pltpu.VMEM)
    hbm = pl.BlockSpec(memory_space=pltpu.HBM)
    tile = (ROWS, LANES)
    fields, factors, own, mix_h, mix_v, levels_here = pl.pallas_call(
        prepare,
        out_shape=(
            vmem_out(depth, 4, *tile),
            vmem_out(6, depth, *tile),
            vmem_out(2 * tiles, *tile),
            vmem_out(depth, *tile),
            vmem_out(depth, *tile),
            pltpu.VMEM(tile, jnp.int32),
        ),
        in_specs=[smem] + [hbm] * 5,
        scratch_shapes=[pltpu.SemaphoreType.DMA((7,))],
        compiler_params=params,
        name="prepare",
    )(seam_code, *(in_hbm(a) for a in (tracers, costate, mixing_h, mixing_v, levels)))

    count = lax.axis_size("ty")
    near_pairs = [(i, i ^ 1) for i in range(count)]
    far_pairs = [(i, (i + 1 if i % 2 else i - 1) % count) for i in range(count)]
    far = lax.ppermute(own, "ty", far_pairs)
    near = lax.ppermute(own, "ty", near_pairs)
    lower, upper, merged = pl.pallas_call(
        pack_rows,
        out_shape=(
            vmem_out(height, LANES),
            vmem_out(height, LANES),
            vmem_out(2 * tiles, *tile),
        ),
        compiler_params=params,
        name="pack_rows",
    )(*(in_vmem(a) for a in (near, far, fields, mix_h, mix_v, levels_here)))

    count = lax.axis_size("tx")
    from_below = lax.ppermute(upper, "tx", [(i, (i + 1) % count) for i in range(count)])
    from_above = lax.ppermute(lower, "tx", [(i, (i - 1) % count) for i in range(count)])
    inside = pl.pallas_call(
        interior,
        out_shape=(
            vmem_out(depth, 4, *tile),
            vmem_out(depth, *tile),
            vmem_out(3, depth, *tile),
            vmem_out(depth, 4, *tile),
            vmem_out(2, depth, *tile),
            vmem_out(depth, *tile),
            vmem_out(depth, *tile),
        ),
        scratch_shapes=[vmem_out(2, tiles, *tile), vmem_out(depth, 2, *tile)],
        compiler_params=params,
        cost_estimate=pl.CostEstimate(flops=20_000_000, bytes_accessed=8_000_000, transcendentals=0),
        name="interior",
    )(*(in_vmem(a) for a in (merged, own, fields, factors, mix_h, levels_here)))
    block = jax.ShapeDtypeStruct(mixing_h.shape, jnp.float32)
    row_block = (depth, 8, LANES)
    return pl.pallas_call(
        finish,
        out_shape=(jax.ShapeDtypeStruct(tracers.shape, jnp.float32), block, block),
        in_specs=[smem] + [vmem] * 15,
        out_specs=(hbm, hbm, hbm),
        scratch_shapes=[
            vmem_out(height, LANES),
            vmem_out(height, LANES),
            vmem_out(2, *row_block),
            vmem_out(*row_block),
            vmem_out(*row_block),
            vmem_out(*row_block),
            vmem_out(depth, 2, 8, LANES),
            vmem_out(depth, 4, 8, LANES),
            vmem_out(2, depth, *tile),
            vmem_out(depth, *tile),
            vmem_out(depth, *tile),
            pltpu.SemaphoreType.DMA((3,)),
        ],
        compiler_params=params,
        name="finish",
    )(
        seam_code,
        *(
            in_vmem(a)
            for a in (
                from_below,
                from_above,
                lower,
                upper,
                merged,
                fields,
                factors,
                levels_here,
                *inside,
            )
        ),
    )


def solution(mesh):
    placed = (
        P("members", None, "tx", "ty"),
        P("members", None, "tx", "ty"),
        P("members", "tx", "ty"),
        P("members", "tx", "ty"),
        P("tx", "ty"),
        P("ty"),
    )
    return jax.shard_map(
        per_device,
        mesh=mesh,
        in_specs=placed,
        out_specs=(
            P("members", None, "tx", "ty"),
            P("members", "tx", "ty"),
            P("members", "tx", "ty"),
        ),
        check_vma=False,
    )
```

time: 20.7 us -> 18.3 us (0.88)
  waiting for transfers between devices: 5.13 us -> 3.3 us
  Pallas kernels: 6.28 us -> 5.69 us
    ppermute x1, waiting for transfers between devices: 3.14 us -> 1.31 us  [per_device(): lax.ppermute(upper, 'tx', [(i, (i + 1) % count) for i in range(count)])]
    pallas_call x0 -> x1, Pallas kernels: none -> 1.82 us  [per_device(): pl.pallas_call(interior, out_shape=(vmem_out(depth, 4, *tile), vmem_out(d...]
    pallas_call x1, Pallas kernels: 3.53 us -> 1.87 us  [per_device(): pl.pallas_call(finish, out_shape=(jax.ShapeDtypeStruct(tracers.shape, jnp...]
    pallas_call x1, Pallas kernels: 0.83 us -> 0.41 us  [per_device(): pl.pallas_call(pack_rows, out_shape=(vmem_out(height, LANES), vmem_out(he...]
    pallas_call x1, Pallas kernels: 1.91 us -> 1.58 us  [per_device(): pl.pallas_call(prepare, out_shape=(vmem_out(depth, 4, *tile), vmem_out(6,...]
  transfers between devices with their start and end apart: 4 -> 4, of which waited for: 3 -> 3; matrix products, arithmetic and copies ran while one was open for 0% -> 0% of each run, Pallas kernels for 0% -> 10%
where the time goes in v2:
time: 18.3 us; the launch traced here: 18.1 us
  starting transfers between devices  7.77 us (42%)
  Pallas kernels  5.69 us (31%)
  waiting for transfers between devices  3.3 us (18%)
  between operations  1.31 us (7%)
    ppermute x1, starting transfers between devices, per_device(): lax.ppermute(upper, 'tx', [(i, (i + 1) % count) for i in range(count)])  2.56 us
    ppermute x1, starting transfers between devices, per_device(): far = lax.ppermute(own, 'ty', far_pairs)  2.44 us
    ppermute x1, starting transfers between devices, per_device(): lax.ppermute(lower, 'tx', [(i, (i - 1) % count) for i in range(count)])  2.09 us
    pallas_call x1, Pallas kernels, per_device(): pl.pallas_call(finish, out_shape=(jax.ShapeDtypeStruct(tracers.shape, jnp...  1.87 us
    pallas_call x1, Pallas kernels, per_device(): pl.pallas_call(interior, out_shape=(vmem_out(depth, 4, *tile), vmem_out(d...  1.82 us
    pallas_call x1, Pallas kernels, per_device(): pl.pallas_call(prepare, out_shape=(vmem_out(depth, 4, *tile), vmem_out(6,...  1.58 us
    ppermute x1, waiting for transfers between devices, per_device(): lax.ppermute(upper, 'tx', [(i, (i + 1) % count) for i in range(count)])  1.31 us
    ppermute x1, waiting for transfers between devices, per_device(): far = lax.ppermute(own, 'ty', far_pairs)  1.1 us
  transfers between devices with their start and end apart: 4, of which 3 were waited for; matrix products, arithmetic and copies ran while one was open for 0% of the time, Pallas kernels for 10%

profile of v2, /device:TPU:0, one launch (start us, length us, event | category | flops | bytes accessed | tf_op | source)
XLA Modules:
  0.0 18.1 jit_solution(309475925026331715)
XLA Ops:
  1.3 1.6 %prepare.1 = (f32[16,4,16,128]{3,2,1,0:T(8,128)S(1)}, f32[6,16,16,128]{3,2,1,0:T(8,128)S(1)}, f32[4,16,128]{2,1,0:T(8,128)S(1)}, f32[16,16,128]{2,1,0:T(8,128)S(...) custom-call(s32[1]{0:T(128)S(6)} %copy.9.seam, f32[2,16,16,128]{3,2,1,0:T(8,128)} %tracers.1, ...), custom_call_target="tpu_custom_call" | custom-call | tf_op jit(solution)/shard_map/prepare/pallas_call | solution.py:660
  2.9 2.4 %collective-permute-start.1 = (f32[4,16,128]{2,1,0:T(8,128)S(1)}, f32[4,16,128]{2,1,0:T(8,128)S(1)}, u32[]{:S(2)}, u32[]{:S(2)}) collective-permute-start(f32[4,16,128]{2,1,0:T(8,128)S(1)} %get-tuple-element.19.own), channel_id=1, source_target_pairs={{0,3},{1,2},{2,1},{3,0},{4,7},{5,6},{6,5},{7,4},{8,11},{9,10},{10,... | collective-permute-start | bytes 98312 | tf_op jit(solution)/shard_map/ppermute | solution.py:679
  5.3 0.7 %collective-permute-start = (f32[4,16,128]{2,1,0:T(8,128)S(1)}, f32[4,16,128]{2,1,0:T(8,128)S(1)}, u32[]{:S(2)}, u32[]{:S(2)}) collective-permute-start(f32[4,16,128]{2,1,0:T(8,128)S(1)} %get-tuple-element.19.own), channel_id=1, source_target_pairs={{0,1},{1,0},{2,3},{3,2},{4,5},{5,4},{6,7},{7,6},{8,9},{9,8},{10,11... | collective-permute-start | bytes 98312 | tf_op jit(solution)/shard_map/ppermute | solution.py:680
  6.0 1.1 %collective-permute-done.1.far = f32[4,16,128]{2,1,0:T(8,128)S(1)} collective-permute-done((f32[4,16,128]{2,1,0:T(8,128)S(1)}, f32[4,16,128]{2,1,0:T(8,128)S(1)}, u32[]{:S(2)}, u32[]{:S(2)}) %collective-permute-start.1) | collective-permute-done | bytes 32800 | tf_op jit(solution)/shard_map/ppermute | solution.py:679
  7.1 0.0 collective-permute-done.near
  7.1 0.4 %pack_rows.1 = (f32[168,128]{1,0:T(8,128)S(1)}, f32[168,128]{1,0:T(8,128)S(1)}, f32[4,16,128]{2,1,0:T(8,128)S(1)}) custom-call(f32[4,16,128]{2,1,0:T(8,128)S(1)} %collective-permute-done.near, f32[4,16,128]{2,1,0:T(8,128)S(1)} %collective-permute-done.1.far, f32[16,4,16,128]{3,2,1,0:T(8,128)S(1)} %get-tuple-element.20.fields, ...), custom_call_target="tpu_custom_call" | custom-call | tf_op jit(solution)/shard_map/pack_rows/pallas_call | solution.py:681
  7.5 2.6 %collective-permute-start.2 = (f32[168,128]{1,0:T(8,128)S(1)}, f32[168,128]{1,0:T(8,128)S(1)}, u32[]{:S(2)}, u32[]{:S(2)}) collective-permute-start(f32[168,128]{1,0:T(8,128)S(1)} %get-tuple-element.24.upper), channel_id=1, source_target_pairs={{0,4},{4,8},{8,12},{12,0},{1,5},{5,9},{9,13},{13,1},{2,6},{6,10},{... | collective-permute-start | bytes 258056 | tf_op jit(solution)/shard_map/ppermute | solution.py:693
  10.1 2.1 %collective-permute-start.3 = (f32[168,128]{1,0:T(8,128)S(1)}, f32[168,128]{1,0:T(8,128)S(1)}, u32[]{:S(2)}, u32[]{:S(2)}) collective-permute-start(f32[168,128]{1,0:T(8,128)S(1)} %get-tuple-element.25.lower), channel_id=1, source_target_pairs={{0,12},{4,0},{8,4},{12,8},{1,13},{5,1},{9,5},{13,9},{2,14},{6,2},{... | collective-permute-start | bytes 258056 | tf_op jit(solution)/shard_map/ppermute | solution.py:694
  12.2 1.8 %interior.1 = (f32[16,4,16,128]{3,2,1,0:T(8,128)S(1)}, f32[16,16,128]{2,1,0:T(8,128)S(1)}, f32[3,16,16,128]{3,2,1,0:T(8,128)S(1)}, f32[16,4,16,128]{3,2,1,0:T(8,...) custom-call(f32[4,16,128]{2,1,0:T(8,128)S(1)} %get-tuple-element.26.merged, ...), custom_call_target="tpu_custom_call" | custom-call | flops 20000000 | bytes 8000000 | tf_op jit(solution)/shard_map/interior/pallas_call | solution.py:695
  14.0 1.3 %collective-permute-done.2.from_below = f32[168,128]{1,0:T(8,128)S(1)} collective-permute-done((f32[168,128]{1,0:T(8,128)S(1)}, f32[168,128]{1,0:T(8,128)S(1)}, u32[]{:S(2)}, u32[]{:S(2)}) %collective-permute-start.2) | collective-permute-done | bytes 86048 | tf_op jit(solution)/shard_map/ppermute | solution.py:693
  15.3 0.9 %collective-permute-done.3.from_above = f32[168,128]{1,0:T(8,128)S(1)} collective-permute-done((f32[168,128]{1,0:T(8,128)S(1)}, f32[168,128]{1,0:T(8,128)S(1)}, u32[]{:S(2)}, u32[]{:S(2)}) %collective-permute-start.3) | collective-permute-done | bytes 86048 | tf_op jit(solution)/shard_map/ppermute | solution.py:694
  16.2 1.9 %finish.1 = (f32[2,16,16,128]{3,2,1,0:T(8,128)}, f32[16,16,128]{2,1,0:T(8,128)}, f32[16,16,128]{2,1,0:T(8,128)}) custom-call(s32[1]{0:T(128)S(6)} %copy.9.seam, f32[168,128]{1,0:T(8,128)S(1)} %collective-permute-done.2.from_below, f32[168,128]{1,0:T(8,128)S(1)} %collective-permute-done.3.from_above, f32[168,128]{1,0:T(8,128)S(1)} %get-tuple-element.25.lower, ...), custom_call_target="tpu_custom_call" | custom-call | tf_op jit(solution)/shard_map/finish/pallas_call | solution.py:713
Async XLA Ops:
  2.9 4.2 %collective-permute-start.1 = (f32[4,16,128]{2,1,0:T(8,128)S(1)}, f32[4,16,128]{2,1,0:T(8,128)S(1)}, u32[]{:S(2)}, u32[]{:S(2)}) collective-permute-start(f32[4,16,128]{2,1,0:T(8,128)S(1)} %get-tuple-element.19.own), channel_id=1, source_target_pairs={{0,3},{1,2},{2,1},{3,0},{4,7},{5,6},{6,5},{7,4},{8,11},{9,10},{10,... | collective-permute-start | bytes 98312 | tf_op jit(solution)/shard_map/ppermute | solution.py:679
  5.3 1.8 %collective-permute-start = (f32[4,16,128]{2,1,0:T(8,128)S(1)}, f32[4,16,128]{2,1,0:T(8,128)S(1)}, u32[]{:S(2)}, u32[]{:S(2)}) collective-permute-start(f32[4,16,128]{2,1,0:T(8,128)S(1)} %get-tuple-element.19.own), channel_id=1, source_target_pairs={{0,1},{1,0},{2,3},{3,2},{4,5},{5,4},{6,7},{7,6},{8,9},{9,8},{10,11... | collective-permute-start | bytes 98312 | tf_op jit(solution)/shard_map/ppermute | solution.py:680
  7.5 7.8 %collective-permute-start.2 = (f32[168,128]{1,0:T(8,128)S(1)}, f32[168,128]{1,0:T(8,128)S(1)}, u32[]{:S(2)}, u32[]{:S(2)}) collective-permute-start(f32[168,128]{1,0:T(8,128)S(1)} %get-tuple-element.24.upper), channel_id=1, source_target_pairs={{0,4},{4,8},{8,12},{12,0},{1,5},{5,9},{9,13},{13,1},{2,6},{6,10},{... | collective-permute-start | bytes 258056 | tf_op jit(solution)/shard_map/ppermute | solution.py:693
  10.1 6.1 %collective-permute-start.3 = (f32[168,128]{1,0:T(8,128)S(1)}, f32[168,128]{1,0:T(8,128)S(1)}, u32[]{:S(2)}, u32[]{:S(2)}) collective-permute-start(f32[168,128]{1,0:T(8,128)S(1)} %get-tuple-element.25.lower), channel_id=1, source_target_pairs={{0,12},{4,0},{8,4},{12,8},{1,13},{5,1},{9,5},{13,9},{2,14},{6,2},{... | collective-permute-start | bytes 258056 | tf_op jit(solution)/shard_map/ppermute | solution.py:694

commit v3 on v2

v3 whole, which is shorter than its diff:
```python
import jax
import jax.numpy as jnp
from jax import lax
from jax.experimental import pallas as pl
from jax.experimental.pallas import tpu as pltpu
from jax.sharding import PartitionSpec as P

LANES = 128
ROWS = 16
GROUP = 16
PER_TILE = LANES // GROUP


FILLER = 3


def in_vmem(array):
    return pltpu.with_memory_space_constraint(array, pltpu.VMEM)


def in_hbm(array):
    return pltpu.with_memory_space_constraint(array, pltpu.HBM)


def vmem_out(*shape):
    return pltpu.VMEM(shape, jnp.float32)


def iota(rows, dim):
    return lax.broadcasted_iota(jnp.int32, (rows, LANES), dim)


def roll(value, shift, axis):
    return pltpu.roll(value, shift % value.shape[axis], axis)


def fold(value):
    return jnp.where(iota(8, 0) < 4, value[:8], value[8:])


def east(value, halo):
    return jnp.where(iota(value.shape[0], 1) == LANES - 1, halo, roll(value, -1, 1))


def west(value, halo):
    return jnp.where(iota(value.shape[0], 1) == 0, halo, roll(value, 1, 1))


def rim(tile, base):
    return roll(tile, LANES - 2 - base, 1)


def crossed(tile):
    column = iota(tile.shape[0], 1) % 4
    return jnp.where(
        column == 1, roll(tile, -1, 1), jnp.where(column == 2, roll(tile, 1, 1), tile)
    )


def loop(count, body, carry):
    for n in range(count):
        carry = body(n, carry)
    return carry


def north(value, beyond):
    sub = iota(8, 0)
    low, high = roll(value[:8], -1, 0), roll(value[8:], -1, 0)
    return jnp.concatenate([jnp.where(sub == 7, high, low), jnp.where(sub == 7, beyond, high)], axis=0)


def south(value, beyond):
    sub = iota(8, 0)
    low, high = roll(value[:8], 1, 0), roll(value[8:], 1, 0)
    return jnp.concatenate([jnp.where(sub == 0, beyond, low), jnp.where(sub == 0, low, high)], axis=0)


def bond(mix_v, level, k, depth):
    if k in (-1, depth - 1):
        return jnp.zeros(level.shape, jnp.float32)
    return jnp.where(level > k + 1, 0.5 * (mix_v[k] + mix_v[k + 1]), 0.0)


def factorize(depth, level, mix_v, put):
    bond_above = jnp.zeros(level.shape, jnp.float32)
    inverse = bond_above
    for k in range(depth):
        bond_here = bond(mix_v, level, k, depth)
        inverse = pivot(bond_above, bond_here, inverse)
        put(k, inverse, bond_above * inverse, bond_here * inverse)
        bond_above = bond_here


def pivot(bond_above, bond_here, inverse):
    return 1.0 / (1.0 + bond_above + bond_here - bond_above * (bond_above * inverse))


def prepare(
    seam,
    tracers,
    costate,
    mix_h_in,
    mix_v_in,
    levels_in,
    fields,
    factors,
    message,
    mix_h,
    mix_v,
    levels,
    sems,
):
    depth = mix_h.shape[0]
    tiles = depth // PER_TILE
    copies = [
        pltpu.make_async_copy(source, target, sems.at[n])
        for n, (source, target) in enumerate(
            (
                (levels_in, levels),
                (mix_v_in, mix_v),
                (costate, fields.at[2:]),
                (tracers, fields.at[:2]),
                (mix_h_in, mix_h),
            )
        )
    ]
    for copy in copies:
        copy.start()
    for copy in copies[:2]:
        copy.wait()
    level = levels[...]
    place = iota(ROWS, 1) // 4
    zero = jnp.zeros((ROWS, LANES), jnp.float32)

    def put(k, *three):
        for n in range(3):
            factors[n, k] = three[n]

    factorize(depth, level, mix_v, put)
    seconds = [jnp.where(place % 4 == FILLER, seam[0].astype(jnp.float32), zero)] * tiles
    level_f = level.astype(jnp.float32)
    for k in range(depth):
        tile, base = k // PER_TILE, GROUP * (k % PER_TILE)
        for n, value in ((1, mix_v[k]), (2, level_f)):
            seconds[tile] = jnp.where(
                place == base // 4 + n, roll(value, base + 4 * n + 2, 1), seconds[tile]
            )
    for copy in copies[2:]:
        copy.wait()
    values = [zero, zero]
    for k in range(depth):
        for t in range(2):
            values[t] = fields[2 + t, k] * factors[0, k] + factors[1, k] * values[t]
            fields[2 + t, k] = values[t]
    firsts = [zero] * tiles
    values = [zero, zero]
    for k in range(depth - 1, -1, -1):
        tile, base = k // PER_TILE, GROUP * (k % PER_TILE)
        for t in range(2):
            values[t] = fields[2 + t, k] + factors[2, k] * values[t]
            fields[2 + t, k] = values[t]
        for q, value in enumerate((fields[0, k], fields[1, k], *values)):
            firsts[tile] = jnp.where(
                place == base // 4 + q, roll(value, base + 4 * q + 2, 1), firsts[tile]
            )
        seconds[tile] = jnp.where(
            place == base // 4, roll(mix_h[k], base + 2, 1), seconds[tile]
        )
    for tile in range(tiles):
        message[tile] = firsts[tile]
        message[tiles + tile] = seconds[tile]


def pack_rows(near, far, fields, mix_h, mix_v, levels, lower, upper, merged):
    depth = mix_h.shape[0]
    tiles = depth // PER_TILE
    place = lax.axis_index("ty")
    last = lax.axis_size("ty") - 1
    even = place % 2 == 0
    column = iota(ROWS, 1) % 4
    from_west = column < 2
    missing = ((place == 0) & from_west) | ((place == last) & jnp.logical_not(from_west))
    base_level = 10 * depth
    corners = []
    for j in range(2 * tiles):
        west_tile = jnp.where(even, far[j], near[j])
        east_tile = jnp.where(even, near[j], far[j])
        tile = jnp.where(from_west, west_tile, east_tile)
        if j >= tiles:
            tile = jnp.where(missing, 0.0, tile)
        merged[j] = crossed(tile)
        other = jnp.where(
            column == 0, roll(west_tile, -2, 1), jnp.where(column == 3, roll(east_tile, 2, 1), tile)
        )
        corners.append(crossed(fold(other)))
    sub = iota(8, 0)
    level_all = levels[...].astype(jnp.float32)
    level = fold(level_all)
    for target, row in ((lower, 0), (upper, 7)):
        block = jnp.zeros((8, LANES), jnp.float32)
        for n, value in enumerate([level, *corners]):
            block = jnp.where(sub == n, roll(value, n - row, 0), block)
        target[base_level : base_level + 8] = block

    def inner(value):
        return jnp.where(sub < 4, roll(value, -1, 0), roll(value, 1, 0))

    level_rim = rim(fold(merged[tiles]), 8)
    shallow = [
        jnp.minimum(level, near_level)
        for near_level in (east(level, level_rim), west(level, level_rim), inner(level))
    ]

    def row(k, _):
        tile, base = k // PER_TILE, GROUP * (k % PER_TILE)
        coefs = fold(merged[tiles + tile])
        mix = fold(mix_h[k])
        mix_rim = rim(coefs, base)
        mixes = (east(mix, mix_rim), west(mix, mix_rim), inner(mix))
        weights = [
            jnp.where(open_to > float(k), 0.5 * (mix + near_mix), 0.0)
            for open_to, near_mix in zip(shallow, mixes)
        ]
        packed = fold(merged[tile])
        low = jnp.zeros((8, LANES), jnp.float32)
        high = low
        for q in range(4):
            value = fold(fields[q, k])
            halo = rim(packed, base + 4 * q)
            part = value
            for near_value, weight in zip(
                (east(value, halo), west(value, halo), inner(value)), weights
            ):
                part = part + weight * (near_value - value)
            for n, thing in ((q, value), (4 + q, part)):
                low = jnp.where(sub == n, roll(thing, n, 0), low)
                high = jnp.where(sub == n, roll(thing, n - 7, 0), high)
        at = slice(8 * k, 8 * k + 8)
        lower[at] = low
        upper[at] = high
        for n, array in enumerate((mix_h, mix_v)):
            at = slice((8 + n) * depth + k, (8 + n) * depth + k + 1)
            lower[at] = array[k, :1]
            upper[at] = array[k, ROWS - 1 :]
        return 0

    loop(depth, row, 0)


def both(low, high):
    return jnp.where(iota(8, 0) < 4, low, high)


def coefficient(value, n):
    kept = iota(value.shape[0], 1) % GROUP // 4 == n
    value = roll(jnp.where(kept, value, 0.0), -4 * n, 1)
    value = value + roll(value, 4, 1)
    return value + roll(value, 8, 1)


def near_all(value, halo, below_row=0.0, above_row=0.0):
    return (
        north(value, above_row),
        south(value, below_row),
        east(value, halo),
        west(value, halo),
    )


def steps_of(fields, merged, k, q):
    value = fields[q, k]
    halo = rim(merged[k // PER_TILE], GROUP * (k % PER_TILE) + 4 * q)
    return value, [near - value for near in near_all(value, halo)]


EDGES = (
    "field",
    "mix",
    "inv_down",
    "up_down",
    "down_down",
    "inv_up",
    "up_up",
    "down_up",
    "inv_up_1",
    "up_up_1",
    "down_up_1",
    "to_east",
    "to_west",
    "to_inner",
    "cross_east",
    "cross_west",
    "cross_inner",
    "inside",
    "adjoint",
    "adjoint_1",
    "later",
    "ahead",
    "ahead_1",
    "grad_h",
    "grad_h_1",
    "grad_v_1",
    "column",
    "mix_column",
    "inv_column",
    "up_column",
    "down_column",
)
EDGE_LEVELS = ("own", "own_1", "east", "west", "inner", "column")


def exchange(value):
    return jnp.where(iota(8, 0) % 4 < 2, roll(value, -2, 0), roll(value, 2, 0))


def at_edges(rows, shift):
    sub = iota(8, 0) % 4
    out = roll(rows, LANES - 2 - shift, 1)
    for q in range(1, 4):
        out = jnp.where(sub == q, roll(rows, LANES - 2 - shift - 4 * q, 1), out)
    return out


def stacked(*rows):
    sub = iota(8, 0)
    out = jnp.zeros((8, LANES), jnp.float32)
    for n, row in enumerate(rows):
        if row is not None:
            out = jnp.where(sub == n, row, out)
    return out


def interior(
    merged,
    own,
    fields,
    factors,
    mix_h,
    mix_v,
    levels,
    lower,
    upper,
    edges,
    edge_levels,
    adjoint,
    grad_h,
    grad_v,
    inside,
    columns,
    column_factors,
    weights,
    packed,
    later,
    up_factors,
):
    depth = mix_h.shape[0]
    face_below = jnp.zeros((ROWS, LANES), jnp.float32)
    inverse = face_below
    level_int = levels[...]
    for k in range(depth - 1, -1, -1):
        face_above = bond(mix_v, level_int, k - 1, depth)
        inverse = pivot(face_below, face_above, inverse)
        up_factors[0, k] = inverse
        up_factors[1, k] = face_below * inverse
        up_factors[2, k] = face_above * inverse
        face_below = face_above
    tiles = depth // PER_TILE
    lane = iota(ROWS, 1)
    zero = jnp.zeros((ROWS, LANES), jnp.float32)

    column = lane % 4

    def around(value, mine):
        return (
            mine,
            jnp.where(column == 1, roll(value, -2, 1), roll(value, 2, 1)),
            north(value, 0.0),
            south(value, 0.0),
        )

    for j in range(tiles):
        level_k = (lane // GROUP + j * PER_TILE).astype(jnp.float32)
        here = [coefficient(merged[tiles + j], n) for n in range(3)]
        (mix, mixes), (level, level_near) = [
            (here[n], around(here[n], coefficient(own[tiles + j], n))) for n in (0, 2)
        ]
        value = merged[j]
        mixed = value
        for near, near_mix, near_level in zip(around(value, own[j]), mixes, level_near):
            weight = jnp.where(
                jnp.minimum(level, near_level) > level_k, 0.5 * (mix + near_mix), 0.0
            )
            mixed = mixed + weight * (near - value)
        packed[0, j] = mixed
        packed[1, j] = here[1]
        if j == 0:
            level_columns = level

    def unpacked(n, k):
        return roll(packed[n, k // PER_TILE], -GROUP * (k % PER_TILE), 1)

    level = levels[...].astype(jnp.float32)
    shallow = [jnp.minimum(level, near) for near in near_all(level, rim(merged[tiles], 8))]

    def first(k, carry):
        (col_bond, col_inverse, col_value), values = carry
        under = min(k + 1, depth - 1)
        bond_here = jnp.where(
            level_columns > k + 1.0, 0.5 * (unpacked(1, k) + unpacked(1, under)), 0.0
        )
        col_inverse = pivot(col_bond, bond_here, col_inverse)
        col_factor = col_bond * col_inverse
        col_value = unpacked(0, k) * col_inverse + col_factor * col_value
        columns[k] = col_value
        column_factors[0, k] = col_inverse
        column_factors[1, k] = col_factor
        column_factors[2, k] = bond_here * col_inverse
        mix = mix_h[k]
        mix_rim = rim(merged[tiles + k // PER_TILE], GROUP * (k % PER_TILE))
        weight = [
            jnp.where(open_to > float(k), 0.5 * (mix + near), 0.0)
            for open_to, near in zip(shallow, near_all(mix, mix_rim))
        ]
        for n in range(4):
            weights[k, n] = weight[n]
        inverse, factor = factors[0, k], factors[1, k]
        values = list(values)
        for q in range(4):
            value, steps = steps_of(fields, merged, k, q)
            for n in range(4):
                value = value + weight[n] * steps[n]
            values[q] = value * inverse + factor * values[q]
            inside[k, q] = values[q]
        return (bond_here, col_inverse, col_value), tuple(values)

    loop(depth, first, ((zero,) * 3, (zero,) * 4))

    def second(n, carry):
        col_value, values, later_values = carry
        k = depth - 1 - n
        col_value = columns[k] + column_factors[2, k] * col_value
        columns[k] = col_value
        values, later_values = list(values), list(later_values)
        first_steps, later_steps = [], []
        for q in range(4):
            value = inside[k, q] + factors[2, k] * values[q]
            inside[k, q] = value
            values[q] = value
            steps = [near - value for near in near_all(value, rim(col_value, 4 * q))]
            later_steps.append(steps)
            first_steps.append(steps_of(fields, merged, k, q)[1])
            for n in range(4):
                value = value + weights[k, n] * steps[n]
            if q < 2:
                later_values[q] = value * up_factors[0, k] + up_factors[1, k] * later_values[q]
                later[k, q] = later_values[q]
            else:
                adjoint[q - 2, k] = value
        total = zero
        for n in range(4):
            face = zero
            for t in range(2):
                face = face + first_steps[t][n] * later_steps[2 + t][n]
                face = face + later_steps[t][n] * first_steps[2 + t][n]
            total = total + jnp.where(shallow[n] > float(k), face, 0.0)
        grad_h[k] = -0.5 * total
        return col_value, tuple(values), tuple(later_values)

    loop(depth, second, (zero, (zero,) * 4, (zero,) * 2))

    face_above = zero
    for k in range(depth):
        if k > 0:
            total = zero
            for t in range(2):
                later[k, t] = later[k, t] + up_factors[2, k] * later[k - 1, t]
                total = total + (inside[k - 1, 2 + t] - inside[k, 2 + t]) * (
                    inside[k - 1, t] - inside[k, t]
                )
                total = total + (fields[2 + t, k - 1] - fields[2 + t, k]) * (
                    later[k - 1, t] - later[k, t]
                )
            face = jnp.where(level > float(k), total, 0.0)
            grad_v[k - 1] = -0.5 * (face + face_above)
            face_above = face
    grad_v[depth - 1] = -0.5 * face_above

    def ends(value, depth_in=0):
        return both(value[depth_in : depth_in + 1], value[ROWS - 1 - depth_in : ROWS - depth_in])

    coef_rows = ends(merged[tiles])
    for n, value in enumerate(
        (
            ends(level),
            ends(level, 1),
            ends(shallow[2]),
            ends(shallow[3]),
            both(shallow[0][:1], shallow[1][ROWS - 1 :]),
            rim(coef_rows, 8),
        )
    ):
        edge_levels[n] = value
    last_lane, first_lane = iota(8, 1) == LANES - 1, iota(8, 1) == 0

    def four(row, depth_in):
        low, high = depth_in, ROWS - 1 - depth_in
        return stacked(
            *(row(q, slice(low, low + 1)) for q in range(4)),
            *(row(q, slice(high, high + 1)) for q in range(4)),
        )

    for k in range(depth):
        j, i = divmod(k, PER_TILE)
        block = slice(8 * k, 8 * k + 8)
        field = both(lower[block], roll(upper[block], 4, 0))
        field_1 = four(lambda q, r: fields[q, k, r], 1)
        column = at_edges(ends(merged[j]), GROUP * i)
        steps = (
            jnp.where(last_lane, column, roll(field, -1, 1)) - field,
            jnp.where(first_lane, column, roll(field, 1, 1)) - field,
            field_1 - field,
        )

        def tracer(ref):
            return lambda q, r: ref[k, q, r] if q < 2 else None

        def result(q, r):
            return adjoint[q - 2, k, r] if q > 1 else None

        things = dict(
            field=field,
            mix=ends(mix_h[k]),
            to_east=ends(weights[k, 2]),
            to_west=ends(weights[k, 3]),
            to_inner=both(weights[k, 0, :1], weights[k, 1, ROWS - 1 :]),
            cross_east=exchange(steps[0]),
            cross_west=exchange(steps[1]),
            cross_inner=exchange(steps[2]),
            inside=four(lambda q, r: inside[k, q, r], 0),
            adjoint=four(result, 0),
            adjoint_1=four(result, 1),
            later=four(tracer(later), 0),
            ahead=roll(field, -2, 0),
            ahead_1=roll(field_1, -2, 0),
            grad_h=ends(grad_h[k]),
            grad_h_1=ends(grad_h[k], 1),
            grad_v_1=ends(grad_v[k], 1),
            column=column,
            mix_column=rim(ends(merged[tiles + j]), GROUP * i),
        )
        for n, name in enumerate(("inv", "up", "down")):
            things[name + "_down"] = ends(factors[n, k])
            things[name + "_up"] = ends(up_factors[n, k])
            things[name + "_up_1"] = ends(up_factors[n, k], 1)
            things[name + "_column"] = rim(ends(column_factors[n, k]), 0)
        for name, value in things.items():
            edges[EDGES.index(name), k] = value


def finish(
    seam,
    from_below,
    from_above,
    merged,
    edges,
    edge_levels,
    adjoint_in,
    grad_h_in,
    grad_v_in,
    adjoint_out,
    grad_h_out,
    grad_v_out,
    below,
    above,
    rows,
    later,
    adjoint,
    grad_h,
    grad_v,
    sems,
):
    depth, tiles = grad_h.shape[0], grad_h.shape[0] // PER_TILE
    sub = iota(8, 0)
    lane = iota(8, 1)
    place = lax.axis_index("tx")
    last = lax.axis_size("tx") - 1
    base_mix, base_v, base_level = 8 * depth, 9 * depth, 10 * depth
    zero = jnp.zeros((8, LANES), jnp.float32)

    def edge(name, k):
        return edges[EDGES.index(name), k]

    def edge_level(name):
        return edge_levels[EDGE_LEVELS.index(name)]

    for source, target, border in ((from_below, below, 0), (from_above, above, last)):
        turn = (seam[0] == 1) & (place == border)

        @pl.when(turn)
        def _():
            back = LANES - 1 - lane
            for r in range(0, base_level, 8):
                target[r : r + 8] = jnp.take_along_axis(source[r : r + 8], back, axis=1)
            block = source[base_level : base_level + 8]
            target[base_level : base_level + 8] = jnp.where(
                sub < 1, jnp.take_along_axis(block, back, axis=1), block
            )

        @pl.when(jnp.logical_not(turn))
        def _():
            for r in range(0, base_level + 8, 8):
                target[r : r + 8] = source[r : r + 8]

    for k in range(depth):
        for t in range(2):
            adjoint[t, k] = adjoint_in[t, k]
        grad_h[k] = grad_h_in[k]
        grad_v[k] = grad_v_in[k]

    turned = coefficient(merged[tiles, :8], FILLER)[:1]
    corners = []
    for target, border in ((below, 0), (above, last)):
        block = target[base_level : base_level + 8]
        swapped = jnp.where(lane % 4 == 1, roll(block, -2, 1), roll(block, 2, 1))
        corners.append(jnp.where((place == border) & (turned > 0.5), swapped, block))

    def corner(r):
        return both(corners[0][r : r + 1], corners[1][r : r + 1])

    def outer(start, k=0):
        at = slice(start + k, start + k + 1)
        return both(below[at], above[at])

    level_out = outer(base_level)
    level_face = jnp.minimum(level_out, edge_level("own"))
    level_corner = jnp.minimum(rim(corner(1 + tiles), 8), edge_level("column"))

    bond_above = inverse = out_value = added = column_added = zero
    flows = []
    for k in range(depth):
        j, i = divmod(k, PER_TILE)
        block = slice(8 * k, 8 * k + 8)
        below_block, above_block = below[block], above[block]
        bond_here = jnp.where(
            level_out > k + 1.0,
            0.5 * (outer(base_v, k) + outer(base_v, min(k + 1, depth - 1))),
            0.0,
        )
        inverse = pivot(bond_above, bond_here, inverse)
        out = both(below_block, roll(above_block, 4, 0))
        part = both(roll(below_block, 4, 0), above_block)
        step = out - edge("field", k)
        weight = jnp.where(level_face > float(k), 0.5 * (outer(base_mix, k) + edge("mix", k)), 0.0)
        flow = weight * step
        out_value = (part - flow) * inverse + bond_above * inverse * out_value
        added = flow * edge("inv_down", k) + edge("up_down", k) * added
        weight_corner = jnp.where(
            level_corner > float(k),
            0.5 * (rim(corner(1 + tiles + j), GROUP * i) + edge("mix_column", k)),
            0.0,
        )
        step_corner = at_edges(corner(1 + j), GROUP * i) - edge("column", k)
        column_added = (
            weight_corner * step_corner * edge("inv_column", k)
            + edge("up_column", k) * column_added
        )
        rows[0, k] = out_value
        rows[1, k] = bond_here * inverse
        rows[2, k] = added
        rows[3, k] = column_added
        rows[4, k] = weight
        rows[5, k] = exchange(step)
        bond_above = bond_here

    out_value = added = column_added = later_0 = later_1 = zero
    for k in range(depth - 1, -1, -1):
        out_value = rows[0, k] + rows[1, k] * out_value
        added = rows[2, k] + edge("down_down", k) * added
        column_added = rows[3, k] + edge("down_column", k) * column_added
        value = edge("inside", k) + added
        rows[0, k] = value
        east_step = jnp.where(lane == LANES - 1, column_added, roll(added, -1, 1)) - added
        west_step = jnp.where(lane == 0, column_added, roll(added, 1, 1)) - added
        out_step = out_value - value
        inner_flow = edge("to_inner", k) * added
        change = (
            added
            + edge("to_east", k) * east_step
            + edge("to_west", k) * west_step
            - inner_flow
            + rows[4, k] * out_step
        )
        later_0 = change * edge("inv_up", k) + edge("up_up", k) * later_0
        later_1 = inner_flow * edge("inv_up_1", k) + edge("up_up_1", k) * later_1
        later[0, k] = later_0
        later[1, k] = later_1
        result = edge("adjoint", k) + change
        result_1 = edge("adjoint_1", k) + inner_flow
        for t in range(2):
            for at, source, row in (
                (0, result, 2),
                (ROWS - 1, result, 6),
                (1, result_1, 2),
                (ROWS - 2, result_1, 6),
            ):
                adjoint[t, k, at : at + 1] = source[row + t : row + t + 1]
        product_1 = jnp.where(
            edge_level("inner") > float(k), -edge("cross_inner", k) * added, 0.0
        )
        product = (
            product_1
            + jnp.where(edge_level("east") > float(k), edge("cross_east", k) * east_step, 0.0)
            + jnp.where(edge_level("west") > float(k), edge("cross_west", k) * west_step, 0.0)
            + jnp.where(level_face > float(k), rows[5, k] * out_step, 0.0)
        )
        for name, inset, value in (("grad_h", 0, product), ("grad_h_1", 1, product_1)):
            value = value + roll(value, -1, 0)
            value = edge(name, k) - 0.5 * (value + roll(value, -2, 0))
            grad_h[k, inset : inset + 1] = value[:1]
            grad_h[k, ROWS - 1 - inset : ROWS - inset] = value[4:5]

    copies = [
        pltpu.make_async_copy(source, target, sems.at[n])
        for n, (source, target) in enumerate(
            ((adjoint, adjoint_out), (grad_h, grad_h_out), (grad_v, grad_v_out))
        )
    ]
    copies[0].start()
    copies[1].start()

    face_0 = face_1 = later_0 = later_1 = zero
    for k in range(depth + 1):
        if k < depth:
            above_0, above_1 = later_0, later_1
            later_0 = later[0, k] + edge("down_up", k) * later_0
            later_1 = later[1, k] + edge("down_up_1", k) * later_1
        if k == 0:
            continue
        next_0 = next_1 = zero
        if k < depth:
            step = rows[0, k - 1] - rows[0, k]
            next_0 = step * roll(step, -2, 0) + (edge("ahead", k - 1) - edge("ahead", k)) * (
                edge("later", k - 1) + above_0 - edge("later", k) - later_0
            )
            next_1 = (edge("ahead_1", k - 1) - edge("ahead_1", k)) * (above_1 - later_1)
            next_0 = jnp.where(
                edge_level("own") > float(k), next_0 + roll(next_0, -1, 0), 0.0
            )
            next_1 = jnp.where(
                edge_level("own_1") > float(k), next_1 + roll(next_1, -1, 0), 0.0
            )
        value_0 = -0.5 * (face_0 + next_0)
        value_1 = edge("grad_v_1", k - 1) - 0.5 * (face_1 + next_1)
        for inset, value in ((0, value_0), (1, value_1)):
            grad_v[k - 1, inset : inset + 1] = value[:1]
            grad_v[k - 1, ROWS - 1 - inset : ROWS - inset] = value[4:5]
        face_0, face_1 = next_0, next_1
    copies[2].start()
    for copy in copies:
        copy.wait()


def per_device(tracers, costate, mixing_h, mixing_v, levels, seam_code):
    depth = tracers.shape[1]
    tiles = depth // PER_TILE
    height = 10 * depth + 8
    params = pltpu.CompilerParams(vmem_limit_bytes=48 * 2**20)
    smem = pl.BlockSpec(memory_space=pltpu.SMEM)
    vmem = pl.BlockSpec(memory_space=pltpu.VMEM)
    hbm = pl.BlockSpec(memory_space=pltpu.HBM)
    tile = (ROWS, LANES)
    fields, factors, own, mix_h, mix_v, levels_here = pl.pallas_call(
        prepare,
        out_shape=(
            vmem_out(4, depth, *tile),
            vmem_out(3, depth, *tile),
            vmem_out(2 * tiles, *tile),
            vmem_out(depth, *tile),
            vmem_out(depth, *tile),
            pltpu.VMEM(tile, jnp.int32),
        ),
        in_specs=[smem] + [hbm] * 5,
        scratch_shapes=[pltpu.SemaphoreType.DMA((5,))],
        compiler_params=params,
        name="prepare",
    )(seam_code, *(in_hbm(a) for a in (tracers, costate, mixing_h, mixing_v, levels)))

    count = lax.axis_size("ty")
    near_pairs = [(i, i ^ 1) for i in range(count)]
    far_pairs = [(i, (i + 1 if i % 2 else i - 1) % count) for i in range(count)]
    far = lax.ppermute(own, "ty", far_pairs)
    near = lax.ppermute(own, "ty", near_pairs)
    lower, upper, merged = pl.pallas_call(
        pack_rows,
        out_shape=(
            vmem_out(height, LANES),
            vmem_out(height, LANES),
            vmem_out(2 * tiles, *tile),
        ),
        compiler_params=params,
        name="pack_rows",
    )(*(in_vmem(a) for a in (near, far, fields, mix_h, mix_v, levels_here)))

    count = lax.axis_size("tx")
    from_below = lax.ppermute(upper, "tx", [(i, (i + 1) % count) for i in range(count)])
    from_above = lax.ppermute(lower, "tx", [(i, (i - 1) % count) for i in range(count)])
    row_block = (depth, 8, LANES)
    inner = pl.pallas_call(
        interior,
        out_shape=(
            vmem_out(len(EDGES), *row_block),
            vmem_out(len(EDGE_LEVELS), 8, LANES),
            vmem_out(2, depth, *tile),
            vmem_out(depth, *tile),
            vmem_out(depth, *tile),
        ),
        scratch_shapes=[
            vmem_out(depth, 4, *tile),
            vmem_out(depth, *tile),
            vmem_out(3, depth, *tile),
            vmem_out(depth, 4, *tile),
            vmem_out(2, tiles, *tile),
            vmem_out(depth, 2, *tile),
            vmem_out(3, depth, *tile),
        ],
        compiler_params=params,
        cost_estimate=pl.CostEstimate(flops=20_000_000, bytes_accessed=8_000_000, transcendentals=0),
        name="interior",
    )(
        *(
            in_vmem(a)
            for a in (merged, own, fields, factors, mix_h, mix_v, levels_here, lower, upper)
        )
    )
    block = jax.ShapeDtypeStruct(mixing_h.shape, jnp.float32)
    return pl.pallas_call(
        finish,
        out_shape=(jax.ShapeDtypeStruct(tracers.shape, jnp.float32), block, block),
        in_specs=[smem] + [vmem] * 8,
        out_specs=(hbm, hbm, hbm),
        scratch_shapes=[
            vmem_out(height, LANES),
            vmem_out(height, LANES),
            vmem_out(6, *row_block),
            vmem_out(2, *row_block),
            vmem_out(2, depth, *tile),
            vmem_out(depth, *tile),
            vmem_out(depth, *tile),
            pltpu.SemaphoreType.DMA((3,)),
        ],
        compiler_params=params,
        name="finish",
    )(seam_code, *(in_vmem(a) for a in (from_below, from_above, merged, *inner)))


def solution(mesh):
    placed = (
        P("members", None, "tx", "ty"),
        P("members", None, "tx", "ty"),
        P("members", "tx", "ty"),
        P("members", "tx", "ty"),
        P("tx", "ty"),
        P("ty"),
    )
    return jax.shard_map(
        per_device,
        mesh=mesh,
        in_specs=placed,
        out_specs=(
            P("members", None, "tx", "ty"),
            P("members", "tx", "ty"),
            P("members", "tx", "ty"),
        ),
        check_vma=False,
    )
```

time: 18.3 us -> 17.8 us (0.973)
  starting transfers between devices: 7.77 us -> 7.01 us
  waiting for transfers between devices: 3.3 us -> 3.82 us
  Pallas kernels: 5.69 us -> 5.39 us
    ppermute x1, starting transfers between devices: 2.56 us -> 1.76 us  [per_device(): lax.ppermute(upper, 'tx', [(i, (i + 1) % count) for i in range(count)])]
    ppermute x1, waiting for transfers between devices: 1.1 us -> 1.67 us  [per_device(): far = lax.ppermute(own, 'ty', far_pairs)]
    pallas_call x1, Pallas kernels: 1.87 us -> 1.34 us  [per_device(): pl.pallas_call(finish, out_shape=(jax.ShapeDtypeStruct(tracers.shape, jnp...]
    pallas_call x2, Pallas kernels: 3.4 us -> 3.64 us  [the longest x1 2.17 us: per_device(): pl.pallas_call(interior, out_shape=(vmem_out(len(EDGES), *row_block), vme...]
  transfers between devices with their start and end apart: 4 -> 4, of which waited for: 3 -> 3; matrix products, arithmetic and copies ran while one was open for 0% -> 0% of each run, Pallas kernels for 10% -> 12%
where the time goes in v3:
time: 17.8 us; the launch traced here: 17.5 us
  starting transfers between devices  7.01 us (39%)
  Pallas kernels  5.39 us (30%)
  waiting for transfers between devices  3.82 us (21%)
  between operations  1.3 us (7%)
    ppermute x1, starting transfers between devices, per_device(): far = lax.ppermute(own, 'ty', far_pairs)  2.61 us
    pallas_call x1, Pallas kernels, per_device(): pl.pallas_call(interior, out_shape=(vmem_out(len(EDGES), *row_block), vme...  2.17 us
    ppermute x1, starting transfers between devices, per_device(): lax.ppermute(lower, 'tx', [(i, (i - 1) % count) for i in range(count)])  2.12 us
    ppermute x1, starting transfers between devices, per_device(): lax.ppermute(upper, 'tx', [(i, (i + 1) % count) for i in range(count)])  1.76 us
    ppermute x1, waiting for transfers between devices, per_device(): far = lax.ppermute(own, 'ty', far_pairs)  1.67 us
    pallas_call x1, Pallas kernels, per_device(): pl.pallas_call(prepare, out_shape=(vmem_out(4, depth, *tile), vmem_out(3,...  1.46 us
    pallas_call x1, Pallas kernels, per_device(): pl.pallas_call(finish, out_shape=(jax.ShapeDtypeStruct(tracers.shape, jnp...  1.34 us
    ppermute x1, waiting for transfers between devices, per_device(): lax.ppermute(upper, 'tx', [(i, (i + 1) % count) for i in range(count)])  1.2 us
  transfers between devices with their start and end apart: 4, of which 3 were waited for; matrix products, arithmetic and copies ran while one was open for 0% of the time, Pallas kernels for 12%

profile of v3, /device:TPU:0, one launch (start us, length us, event | category | flops | bytes accessed | tf_op | source)
XLA Modules:
  0.0 17.5 jit_solution(269770756139038069)
XLA Ops:
  1.3 1.5 %prepare.1 = (f32[4,16,16,128]{3,2,1,0:T(8,128)S(1)}, f32[3,16,16,128]{3,2,1,0:T(8,128)S(1)}, f32[4,16,128]{2,1,0:T(8,128)S(1)}, f32[16,16,128]{2,1,0:T(8,128)S(...) custom-call(s32[1]{0:T(128)S(6)} %copy.9.seam, f32[2,16,16,128]{3,2,1,0:T(8,128)} %tracers.1, ...), custom_call_target="tpu_custom_call" | custom-call | tf_op jit(solution)/shard_map/prepare/pallas_call | solution.py:772
  2.8 0.5 %collective-permute-start = (f32[4,16,128]{2,1,0:T(8,128)S(1)}, f32[4,16,128]{2,1,0:T(8,128)S(1)}, u32[]{:S(2)}, u32[]{:S(2)}) collective-permute-start(f32[4,16,128]{2,1,0:T(8,128)S(1)} %get-tuple-element.17.own), channel_id=1, source_target_pairs={{0,1},{1,0},{2,3},{3,2},{4,5},{5,4},{6,7},{7,6},{8,9},{9,8},{10,11... | collective-permute-start | bytes 98312 | tf_op jit(solution)/shard_map/ppermute | solution.py:792
  3.3 2.6 %collective-permute-start.1 = (f32[4,16,128]{2,1,0:T(8,128)S(1)}, f32[4,16,128]{2,1,0:T(8,128)S(1)}, u32[]{:S(2)}, u32[]{:S(2)}) collective-permute-start(f32[4,16,128]{2,1,0:T(8,128)S(1)} %get-tuple-element.17.own), channel_id=1, source_target_pairs={{0,3},{1,2},{2,1},{3,0},{4,7},{5,6},{6,5},{7,4},{8,11},{9,10},{10,... | collective-permute-start | bytes 98312 | tf_op jit(solution)/shard_map/ppermute | solution.py:791
  5.9 0.0 collective-permute-done.near
  5.9 1.7 %collective-permute-done.1.far = f32[4,16,128]{2,1,0:T(8,128)S(1)} collective-permute-done((f32[4,16,128]{2,1,0:T(8,128)S(1)}, f32[4,16,128]{2,1,0:T(8,128)S(1)}, u32[]{:S(2)}, u32[]{:S(2)}) %collective-permute-start.1) | collective-permute-done | bytes 32800 | tf_op jit(solution)/shard_map/ppermute | solution.py:791
  7.6 0.4 %pack_rows.1 = (f32[168,128]{1,0:T(8,128)S(1)}, f32[168,128]{1,0:T(8,128)S(1)}, f32[4,16,128]{2,1,0:T(8,128)S(1)}) custom-call(f32[4,16,128]{2,1,0:T(8,128)S(1)} %collective-permute-done.near, f32[4,16,128]{2,1,0:T(8,128)S(1)} %collective-permute-done.1.far, f32[4,16,16,128]{3,2,1,0:T(8,128)S(1)} %get-tuple-element.18.fields, ...), custom_call_target="tpu_custom_call" | custom-call | tf_op jit(solution)/shard_map/pack_rows/pallas_call | solution.py:793
  8.0 1.8 %collective-permute-start.2 = (f32[168,128]{1,0:T(8,128)S(1)}, f32[168,128]{1,0:T(8,128)S(1)}, u32[]{:S(2)}, u32[]{:S(2)}) collective-permute-start(f32[168,128]{1,0:T(8,128)S(1)} %get-tuple-element.22.upper), channel_id=1, source_target_pairs={{0,4},{4,8},{8,12},{12,0},{1,5},{5,9},{9,13},{13,1},{2,6},{6,10},{... | collective-permute-start | bytes 258056 | tf_op jit(solution)/shard_map/ppermute | solution.py:805
  9.7 2.1 %collective-permute-start.3 = (f32[168,128]{1,0:T(8,128)S(1)}, f32[168,128]{1,0:T(8,128)S(1)}, u32[]{:S(2)}, u32[]{:S(2)}) collective-permute-start(f32[168,128]{1,0:T(8,128)S(1)} %get-tuple-element.23.lower), channel_id=1, source_target_pairs={{0,12},{4,0},{8,4},{12,8},{1,13},{5,1},{9,5},{13,9},{2,14},{6,2},{... | collective-permute-start | bytes 258056 | tf_op jit(solution)/shard_map/ppermute | solution.py:806
  11.9 2.2 %interior.1 = (f32[31,16,8,128]{3,2,1,0:T(8,128)S(1)}, f32[6,8,128]{2,1,0:T(8,128)S(1)}, f32[2,16,16,128]{3,2,1,0:T(8,128)S(1)}, f32[16,16,128]{2,1,0:T(8,128)S(1)}, f32[16,16,128]{2,1,0:T(8,128)S(1)}) custom-call(f32[4,16,128]{2,1,0:T(8,128)S(1)} %get-tuple-element.24.merged, f32[4,16,128]{2,1,0:T(8,128)S(1)} %get-tuple-element.17.own, ...), custom_call_target="tpu_custom_call" | custom-call | flops 20000000 | bytes 8000000 | tf_op jit(solution)/shard_map/interior/pallas_call | solution.py:808
  14.0 1.2 %collective-permute-done.2.from_below = f32[168,128]{1,0:T(8,128)S(1)} collective-permute-done((f32[168,128]{1,0:T(8,128)S(1)}, f32[168,128]{1,0:T(8,128)S(1)}, u32[]{:S(2)}, u32[]{:S(2)}) %collective-permute-start.2) | collective-permute-done | bytes 86048 | tf_op jit(solution)/shard_map/ppermute | solution.py:805
  15.2 0.9 %collective-permute-done.3.from_above = f32[168,128]{1,0:T(8,128)S(1)} collective-permute-done((f32[168,128]{1,0:T(8,128)S(1)}, f32[168,128]{1,0:T(8,128)S(1)}, u32[]{:S(2)}, u32[]{:S(2)}) %collective-permute-start.3) | collective-permute-done | bytes 86048 | tf_op jit(solution)/shard_map/ppermute | solution.py:806
  16.2 1.3 %finish.1 = (f32[2,16,16,128]{3,2,1,0:T(8,128)}, f32[16,16,128]{2,1,0:T(8,128)}, f32[16,16,128]{2,1,0:T(8,128)}) custom-call(s32[1]{0:T(128)S(6)} %copy.9.seam, f32[168,128]{1,0:T(8,128)S(1)} %collective-permute-done.2.from_below, f32[168,128]{1,0:T(8,128)S(1)} %collective-permute-done.3.from_above, f32[4,16,128]{2,1,0:T(8,128)S(1)} %get-tuple-element.24.merged, ...), custom_call_target="tpu_custom_call" | custom-call | tf_op jit(solution)/shard_map/finish/pallas_call | solution.py:836
Async XLA Ops:
  2.8 3.1 %collective-permute-start = (f32[4,16,128]{2,1,0:T(8,128)S(1)}, f32[4,16,128]{2,1,0:T(8,128)S(1)}, u32[]{:S(2)}, u32[]{:S(2)}) collective-permute-start(f32[4,16,128]{2,1,0:T(8,128)S(1)} %get-tuple-element.17.own), channel_id=1, source_target_pairs={{0,1},{1,0},{2,3},{3,2},{4,5},{5,4},{6,7},{7,6},{8,9},{9,8},{10,11... | collective-permute-start | bytes 98312 | tf_op jit(solution)/shard_map/ppermute | solution.py:792
  3.3 4.3 %collective-permute-start.1 = (f32[4,16,128]{2,1,0:T(8,128)S(1)}, f32[4,16,128]{2,1,0:T(8,128)S(1)}, u32[]{:S(2)}, u32[]{:S(2)}) collective-permute-start(f32[4,16,128]{2,1,0:T(8,128)S(1)} %get-tuple-element.17.own), channel_id=1, source_target_pairs={{0,3},{1,2},{2,1},{3,0},{4,7},{5,6},{6,5},{7,4},{8,11},{9,10},{10,... | collective-permute-start | bytes 98312 | tf_op jit(solution)/shard_map/ppermute | solution.py:791
  8.0 7.3 %collective-permute-start.2 = (f32[168,128]{1,0:T(8,128)S(1)}, f32[168,128]{1,0:T(8,128)S(1)}, u32[]{:S(2)}, u32[]{:S(2)}) collective-permute-start(f32[168,128]{1,0:T(8,128)S(1)} %get-tuple-element.22.upper), channel_id=1, source_target_pairs={{0,4},{4,8},{8,12},{12,0},{1,5},{5,9},{9,13},{13,1},{2,6},{6,10},{... | collective-permute-start | bytes 258056 | tf_op jit(solution)/shard_map/ppermute | solution.py:805
  9.7 6.4 %collective-permute-start.3 = (f32[168,128]{1,0:T(8,128)S(1)}, f32[168,128]{1,0:T(8,128)S(1)}, u32[]{:S(2)}, u32[]{:S(2)}) collective-permute-start(f32[168,128]{1,0:T(8,128)S(1)} %get-tuple-element.23.lower), channel_id=1, source_target_pairs={{0,12},{4,0},{8,4},{12,8},{1,13},{5,1},{9,5},{13,9},{2,14},{6,2},{... | collective-permute-start | bytes 258056 | tf_op jit(solution)/shard_map/ppermute | solution.py:806

commit v4 on v3

--- a/solution.py
+++ b/solution.py
@@ -171,16 +171,56 @@
         message[tiles + tile] = seconds[tile]
 
 
-def pack_rows(near, far, fields, mix_h, mix_v, levels, lower, upper, merged):
+def row_blocks(depth, row, half, weights_of, halo_of, inner_shift, fields, mix_h, mix_v, target):
+    sub = iota(8, 0)
+    at = row % 8
+    for k in range(depth):
+        weights = weights_of(k)
+        block = jnp.zeros((8, LANES), jnp.float32)
+        for q in range(4):
+            value = fields[q, k, half]
+            halo = halo_of(k, q)
+            part = value
+            for near, weight in zip(
+                (east(value, halo), west(value, halo), roll(value, inner_shift, 0)), weights
+            ):
+                part = part + weight * (near - value)
+            for n, thing in ((q, value), (4 + q, part)):
+                block = jnp.where(sub == n, roll(thing, n - at, 0), block)
+        target[8 * k : 8 * k + 8] = block
+        for n, array in enumerate((mix_h, mix_v)):
+            start = (8 + n) * depth + k
+            target[start : start + 1] = array[k, row : row + 1]
+
+
+def pack_up(fields, mix_h, mix_v, levels, upper):
     depth = mix_h.shape[0]
-    tiles = depth // PER_TILE
+    half = slice(8, 16)
+    level = levels[half].astype(jnp.float32)
+    shallow = [
+        jnp.minimum(level, near)
+        for near in (east(level, 0.0), west(level, 0.0), roll(level, 1, 0))
+    ]
+
+    def weights_of(k):
+        mix = mix_h[k, half]
+        return [
+            jnp.where(open_to > float(k), 0.5 * (mix + near), 0.0)
+            for open_to, near in zip(shallow, (east(mix, 0.0), west(mix, 0.0), roll(mix, 1, 0)))
+        ]
+
+    row_blocks(depth, 15, half, weights_of, lambda k, q: 0.0, 1, fields, mix_h, mix_v, upper)
+    upper[10 * depth : 10 * depth + 8] = stacked(level[7:])
+
+
+def pack_sides(near, far, own, merged, corner, rest):
+    tiles = near.shape[0] // 2
     place = lax.axis_index("ty")
     last = lax.axis_size("ty") - 1
     even = place % 2 == 0
     column = iota(ROWS, 1) % 4
     from_west = column < 2
     missing = ((place == 0) & from_west) | ((place == last) & jnp.logical_not(from_west))
-    base_level = 10 * depth
     corners = []
     for j in range(2 * tiles):
         west_tile = jnp.where(even, far[j], near[j])
@@ -189,62 +229,56 @@
         if j >= tiles:
             tile = jnp.where(missing, 0.0, tile)
         merged[j] = crossed(tile)
-        other = jnp.where(
-            column == 0, roll(west_tile, -2, 1), jnp.where(column == 3, roll(east_tile, 2, 1), tile)
-        )
-        corners.append(crossed(fold(other)))
-    sub = iota(8, 0)
-    level_all = levels[...].astype(jnp.float32)
-    level = fold(level_all)
-    for target, row in ((lower, 0), (upper, 7)):
-        block = jnp.zeros((8, LANES), jnp.float32)
-        for n, value in enumerate([level, *corners]):
-            block = jnp.where(sub == n, roll(value, n - row, 0), block)
-        target[base_level : base_level + 8] = block
-
-    def inner(value):
-        return jnp.where(sub < 4, roll(value, -1, 0), roll(value, 1, 0))
-
-    level_rim = rim(fold(merged[tiles]), 8)
+        corners.append(
+            crossed(
+                fold(
+                    jnp.where(
+                        column == 0,
+                        roll(west_tile, -2, 1),
+                        jnp.where(column == 3, roll(east_tile, 2, 1), tile),
+                    )
+                )
+            )
+        )
+    flows = []
+    lane = iota(1, 1)
+    for j in range(tiles):
+        level_k = (lane // GROUP + j * PER_TILE).astype(jnp.float32)
+        mix, level = [
+            [coefficient(ref[tiles + j, ROWS - 1 :], n) for ref in (merged, own)] for n in (0, 2)
+        ]
+        weight = jnp.where(jnp.minimum(*level) > level_k, 0.5 * (mix[0] + mix[1]), 0.0)
+        flows.append(weight * (merged[j, ROWS - 1 :] - own[j, ROWS - 1 :]))
+    corner[...] = stacked(*(value[7:] for value in corners), *flows)
+    rest[...] = stacked(*(value[:1] for value in corners))
+
+
+def pack_down(merged, rest, fields, mix_h, mix_v, levels, lower):
+    depth = mix_h.shape[0]
+    tiles = depth // PER_TILE
+    half = slice(0, 8)
+    level = levels[half].astype(jnp.float32)
+    halo = rim(merged[tiles, half], 8)
     shallow = [
-        jnp.minimum(level, near_level)
-        for near_level in (east(level, level_rim), west(level, level_rim), inner(level))
+        jnp.minimum(level, near)
+        for near in (east(level, halo), west(level, halo), roll(level, -1, 0))
     ]
 
-    def row(k, _):
-        tile, base = k // PER_TILE, GROUP * (k % PER_TILE)
-        coefs = fold(merged[tiles + tile])
-        mix = fold(mix_h[k])
-        mix_rim = rim(coefs, base)
-        mixes = (east(mix, mix_rim), west(mix, mix_rim), inner(mix))
-        weights = [
-            jnp.where(open_to > float(k), 0.5 * (mix + near_mix), 0.0)
-            for open_to, near_mix in zip(shallow, mixes)
+    def weights_of(k):
+        mix = mix_h[k, half]
+        halo = rim(merged[tiles + k // PER_TILE, half], GROUP * (k % PER_TILE))
+        return [
+            jnp.where(open_to > float(k), 0.5 * (mix + near), 0.0)
+            for open_to, near in zip(shallow, (east(mix, halo), west(mix, halo), roll(mix, -1, 0)))
         ]
-        packed = fold(merged[tile])
-        low = jnp.zeros((8, LANES), jnp.float32)
-        high = low
-        for q in range(4):
-            value = fold(fields[q, k])
-            halo = rim(packed, base + 4 * q)
-            part = value
-            for near_value, weight in zip(
-                (east(value, halo), west(value, halo), inner(value)), weights
-            ):
-                part = part + weight * (near_value - value)
-            for n, thing in ((q, value), (4 + q, part)):
-                low = jnp.where(sub == n, roll(thing, n, 0), low)
-                high = jnp.where(sub == n, roll(thing, n - 7, 0), high)
-        at = slice(8 * k, 8 * k + 8)
-        lower[at] = low
-        upper[at] = high
-        for n, array in enumerate((mix_h, mix_v)):
-            at = slice((8 + n) * depth + k, (8 + n) * depth + k + 1)
-            lower[at] = array[k, :1]
-            upper[at] = array[k, ROWS - 1 :]
-        return 0
-
-    loop(depth, row, 0)
+
+    def halo_of(k, q):
+        return rim(merged[k // PER_TILE, half], GROUP * (k % PER_TILE) + 4 * q)
+
+    row_blocks(depth, 0, half, weights_of, halo_of, -1, fields, mix_h, mix_v, lower)
+    lower[10 * depth : 10 * depth + 8] = jnp.where(
+        iota(8, 0) == 0, level[:1], roll(rest[...], 1, 0)
+    )
 
 
 def both(low, high):
@@ -318,7 +352,7 @@
     out = roll(rows, LANES - 2 - shift, 1)
     for q in range(1, 4):
         out = jnp.where(sub == q, roll(rows, LANES - 2 - shift - 4 * q, 1), out)
-    return out
+    return jnp.broadcast_to(out, (8, LANES))
 
 
 def stacked(*rows):
@@ -557,10 +591,40 @@
             edges[EDGES.index(name), k] = value
 
 
+def turned_corner(block, merged, tiles, border):
+    code = coefficient(merged[tiles, :8], FILLER)[:1]
+    swapped = jnp.where(iota(8, 1) % 4 == 1, roll(block, -2, 1), roll(block, 2, 1))
+    return jnp.where((lax.axis_index("tx") == border) & (code > 0.5), swapped, block)
+
+
+def open_below(seam, corner, merged, edges, edge_levels, opened):
+    depth = opened.shape[1]
+    tiles = depth // PER_TILE
+    turn = (seam[0] == 1) & (lax.axis_index("tx") == 0)
+    block = corner[...]
+    flows = jnp.where(turn, crossed(block), block)
+    block = turned_corner(block, merged, tiles, 0)
+    sub, lane = iota(8, 0), iota(8, 1)
+    inside = (sub < 4) & ((lane == 0) | (lane == LANES - 1))
+    level = jnp.minimum(
+        rim(block[tiles : tiles + 1], 8), edge_levels[EDGE_LEVELS.index("column")]
+    )
+    for k in range(depth):
+        j, i = divmod(k, PER_TILE)
+        mix = rim(block[tiles + j : tiles + j + 1], GROUP * i)
+        weight = 0.5 * (mix + edges[EDGES.index("mix_column"), k])
+        opened[0, k] = at_edges(block[j : j + 1], GROUP * i) - edges[EDGES.index("column"), k]
+        opened[1, k] = jnp.where(level > float(k), weight, 0.0)
+        opened[2, k] = jnp.where(
+            inside, at_edges(flows[2 * tiles + j : 2 * tiles + j + 1], GROUP * i), 0.0
+        )
+
+
 def finish(
     seam,
     from_below,
     from_above,
+    opened,
     merged,
     edges,
     edge_levels,
@@ -617,15 +681,7 @@
         grad_h[k] = grad_h_in[k]
         grad_v[k] = grad_v_in[k]
 
-    turned = coefficient(merged[tiles, :8], FILLER)[:1]
-    corners = []
-    for target, border in ((below, 0), (above, last)):
-        block = target[base_level : base_level + 8]
-        swapped = jnp.where(lane % 4 == 1, roll(block, -2, 1), roll(block, 2, 1))
-        corners.append(jnp.where((place == border) & (turned > 0.5), swapped, block))
-
-    def corner(r):
-        return both(corners[0][r : r + 1], corners[1][r : r + 1])
+    corner = turned_corner(above[base_level : base_level + 8], merged, tiles, last)
 
     def outer(start, k=0):
         at = slice(start + k, start + k + 1)
@@ -633,7 +689,7 @@
 
     level_out = outer(base_level)
     level_face = jnp.minimum(level_out, edge_level("own"))
-    level_corner = jnp.minimum(rim(corner(1 + tiles), 8), edge_level("column"))
+    level_corner = jnp.minimum(rim(corner[1 + tiles : 2 + tiles], 8), edge_level("column"))
 
     bond_above = inverse = out_value = added = column_added = zero
     flows = []
@@ -648,18 +704,20 @@
         )
         inverse = pivot(bond_above, bond_here, inverse)
         out = both(below_block, roll(above_block, 4, 0))
-        part = both(roll(below_block, 4, 0), above_block)
+        part = both(roll(below_block, 4, 0), above_block) + opened[2, k]
         step = out - edge("field", k)
         weight = jnp.where(level_face > float(k), 0.5 * (outer(base_mix, k) + edge("mix", k)), 0.0)
         flow = weight * step
         out_value = (part - flow) * inverse + bond_above * inverse * out_value
         added = flow * edge("inv_down", k) + edge("up_down", k) * added
-        weight_corner = jnp.where(
-            level_corner > float(k),
-            0.5 * (rim(corner(1 + tiles + j), GROUP * i) + edge("mix_column", k)),
-            0.0,
-        )
-        step_corner = at_edges(corner(1 + j), GROUP * i) - edge("column", k)
+        mix_corner = rim(corner[1 + tiles + j : 2 + tiles + j], GROUP * i)
+        weight_corner = both(
+            opened[1, k],
+            jnp.where(level_corner > float(k), 0.5 * (mix_corner + edge("mix_column", k)), 0.0),
+        )
+        step_corner = both(
+            opened[0, k], at_edges(corner[1 + j : 2 + j], GROUP * i) - edge("column", k)
+        )
         column_added = (
             weight_corner * step_corner * edge("inv_column", k)
             + edge("up_column", k) * column_added
@@ -790,20 +848,29 @@
     far_pairs = [(i, (i + 1 if i % 2 else i - 1) % count) for i in range(count)]
     far = lax.ppermute(own, "ty", far_pairs)
     near = lax.ppermute(own, "ty", near_pairs)
-    lower, upper, merged = pl.pallas_call(
-        pack_rows,
-        out_shape=(
-            vmem_out(height, LANES),
-            vmem_out(height, LANES),
-            vmem_out(2 * tiles, *tile),
-        ),
-        compiler_params=params,
-        name="pack_rows",
-    )(*(in_vmem(a) for a in (near, far, fields, mix_h, mix_v, levels_here)))
+
+    def call(body, outs, *operands, **options):
+        return pl.pallas_call(
+            body, out_shape=outs, compiler_params=params, name=body.__name__, **options
+        )(*(in_vmem(a) for a in operands))
 
     count = lax.axis_size("tx")
-    from_below = lax.ppermute(upper, "tx", [(i, (i + 1) % count) for i in range(count)])
-    from_above = lax.ppermute(lower, "tx", [(i, (i - 1) % count) for i in range(count)])
+    upward = [(i, (i + 1) % count) for i in range(count)]
+    downward = [(i, (i - 1) % count) for i in range(count)]
+    upper = call(pack_up, vmem_out(height, LANES), fields, mix_h, mix_v, levels_here)
+    from_below = lax.ppermute(upper, "tx", upward)
+    merged, corner, rest = call(
+        pack_sides,
+        (vmem_out(2 * tiles, *tile), vmem_out(8, LANES), vmem_out(8, LANES)),
+        near,
+        far,
+        own,
+    )
+    corner_below = lax.ppermute(corner, "tx", upward)
+    lower = call(
+        pack_down, vmem_out(height, LANES), merged, rest, fields, mix_h, mix_v, levels_here
+    )
+    from_above = lax.ppermute(lower, "tx", downward)
     row_block = (depth, 8, LANES)
     inner = pl.pallas_call(
         interior,
@@ -824,7 +891,7 @@
             vmem_out(3, depth, *tile),
         ],
         compiler_params=params,
-        cost_estimate=pl.CostEstimate(flops=20_000_000, bytes_accessed=8_000_000, transcendentals=0),
+        cost_estimate=pl.CostEstimate(flops=100_000_000, bytes_accessed=100_000_000, transcendentals=0),
         name="interior",
     )(
         *(
@@ -832,11 +899,19 @@
             for a in (merged, own, fields, factors, mix_h, mix_v, levels_here, lower, upper)
         )
     )
+    opened = pl.pallas_call(
+        open_below,
+        out_shape=vmem_out(3, *row_block),
+        in_specs=[smem] + [vmem] * 4,
+        compiler_params=params,
+        cost_estimate=pl.CostEstimate(flops=900_000_000, bytes_accessed=900_000_000, transcendentals=0),
+        name="open_below",
+    )(seam_code, *(in_vmem(a) for a in (corner_below, merged, *inner[:2])))
     block = jax.ShapeDtypeStruct(mixing_h.shape, jnp.float32)
     return pl.pallas_call(
         finish,
         out_shape=(jax.ShapeDtypeStruct(tracers.shape, jnp.float32), block, block),
-        in_specs=[smem] + [vmem] * 8,
+        in_specs=[smem] + [vmem] * 9,
         out_specs=(hbm, hbm, hbm),
         scratch_shapes=[
             vmem_out(height, LANES),
@@ -850,7 +925,7 @@
         ],
         compiler_params=params,
         name="finish",
-    )(seam_code, *(in_vmem(a) for a in (from_below, from_above, merged, *inner)))
+    )(seam_code, *(in_vmem(a) for a in (from_below, from_above, opened, merged, *inner)))
 
 
 def solution(mesh):

time: 17.8 us -> 16.7 us (0.938)
  waiting for transfers between devices: 3.82 us -> 0.01 us
  starting transfers between devices: 7.01 us -> 8.69 us
  Pallas kernels: 5.39 us -> 6.43 us
    ppermute x2 -> x3, waiting for transfers between devices: 2.15 us -> 0.01 us  [the longest x1 0.01 us: per_device(): corner_below = lax.ppermute(corner, 'tx', upward)]
    ppermute x2 -> x3, starting transfers between devices: 3.88 us -> 5.56 us  [the longest x1 2.3 us: per_device(): from_above = lax.ppermute(lower, 'tx', downward)]
    ppermute x1, waiting for transfers between devices: 1.67 us -> 0.01 us  [per_device(): far = lax.ppermute(own, 'ty', far_pairs)]
    pallas_call x1 -> x4, Pallas kernels: 0.41 us -> 1.33 us  [the longest x3 0.89 us: call(): pl.pallas_call(body, out_shape=outs, compiler_params=params, name=body.__...]
  transfers between devices with their start and end apart: 4 -> 5, of which waited for: 3 -> 0; matrix products, arithmetic and copies ran while one was open for 0% -> 0% of each run, Pallas kernels for 12% -> 21%
where the time goes in v4:
time: 16.7 us; the launch traced here: 16.5 us
  starting transfers between devices  8.69 us (52%)
  Pallas kernels  6.43 us (39%)
  between operations  1.35 us (8%)
    ppermute x1, starting transfers between devices, per_device(): far = lax.ppermute(own, 'ty', far_pairs)  2.61 us
    ppermute x1, starting transfers between devices, per_device(): from_above = lax.ppermute(lower, 'tx', downward)  2.3 us
    pallas_call x1, Pallas kernels, per_device(): pl.pallas_call(interior, out_shape=(vmem_out(len(EDGES), *row_block), vme...  2.2 us
    ppermute x1, starting transfers between devices, per_device(): from_below = lax.ppermute(upper, 'tx', upward)  1.63 us
    ppermute x1, starting transfers between devices, per_device(): corner_below = lax.ppermute(corner, 'tx', upward)  1.63 us
    pallas_call x1, Pallas kernels, per_device(): pl.pallas_call(prepare, out_shape=(vmem_out(4, depth, *tile), vmem_out(3,...  1.45 us
    pallas_call x1, Pallas kernels, per_device(): pl.pallas_call(finish, out_shape=(jax.ShapeDtypeStruct(tracers.shape, jnp...  1.45 us
    pallas_call x3, Pallas kernels, call(): pl.pallas_call(body, out_shape=outs, compiler_params=params, name=body.__...  0.89 us
  transfers between devices with their start and end apart: 5, of which 0 were waited for; matrix products, arithmetic and copies ran while one was open for 0% of the time, Pallas kernels for 21%

profile of v4, /device:TPU:0, one launch (start us, length us, event | category | flops | bytes accessed | tf_op | source)
XLA Modules:
  0.0 16.5 jit_solution(17500949515245474313)
XLA Ops:
  1.3 1.5 %prepare.1 = (f32[4,16,16,128]{3,2,1,0:T(8,128)S(1)}, f32[3,16,16,128]{3,2,1,0:T(8,128)S(1)}, f32[4,16,128]{2,1,0:T(8,128)S(1)}, f32[16,16,128]{2,1,0:T(8,128)S(...) custom-call(s32[1]{0:T(128)S(6)} %copy.9.seam, f32[2,16,16,128]{3,2,1,0:T(8,128)} %tracers.1, ...), custom_call_target="tpu_custom_call" | custom-call | tf_op jit(solution)/shard_map/prepare/pallas_call | solution.py:830
  2.7 0.5 %collective-permute-start.1 = (f32[4,16,128]{2,1,0:T(8,128)S(1)}, f32[4,16,128]{2,1,0:T(8,128)S(1)}, u32[]{:S(2)}, u32[]{:S(2)}) collective-permute-start(f32[4,16,128]{2,1,0:T(8,128)S(1)} %get-tuple-element.21.own), channel_id=1, source_target_pairs={{0,1},{1,0},{2,3},{3,2},{4,5},{5,4},{6,7},{7,6},{8,9},{9,8},{10,11... | collective-permute-start | bytes 98312 | tf_op jit(solution)/shard_map/ppermute | solution.py:850
  3.3 2.6 %collective-permute-start.2 = (f32[4,16,128]{2,1,0:T(8,128)S(1)}, f32[4,16,128]{2,1,0:T(8,128)S(1)}, u32[]{:S(2)}, u32[]{:S(2)}) collective-permute-start(f32[4,16,128]{2,1,0:T(8,128)S(1)} %get-tuple-element.21.own), channel_id=1, source_target_pairs={{0,3},{1,2},{2,1},{3,0},{4,7},{5,6},{6,5},{7,4},{8,11},{9,10},{10,... | collective-permute-start | bytes 98312 | tf_op jit(solution)/shard_map/ppermute | solution.py:849
  5.9 0.2 %pack_up.1.upper = f32[168,128]{1,0:T(8,128)S(1)} custom-call(f32[4,16,16,128]{3,2,1,0:T(8,128)S(1)} %get-tuple-element.17.fields, f32[16,16,128]{2,1,0:T(8,128)S(1)} %get-tuple-element.18.mix_h, f32[16,16,128]{2,1,0:T(8,128)S(1)} %get-tuple-element.19.mix_v, s32[16,128]{1,0:T(8,128)S(1)} %get-tuple-element.20.levels), custom_call_target="tpu_custom_call" | custom-call | tf_op jit(solution)/shard_map/pack_up/pallas_call | solution.py:853
  6.1 1.6 %collective-permute-start = (f32[168,128]{1,0:T(8,128)S(1)}, f32[168,128]{1,0:T(8,128)S(1)}, u32[]{:S(2)}, u32[]{:S(2)}) collective-permute-start(f32[168,128]{1,0:T(8,128)S(1)} %pack_up.1.upper), channel_id=1, source_target_pairs={{0,4},{4,8},{8,12},{12,0},{1,5},{5,9},{9,13},{13,1},{2,6},{6,10},{... | collective-permute-start | bytes 258056 | tf_op jit(solution)/shard_map/ppermute | solution.py:861
  7.8 0.0 collective-permute-done.1.near
  7.8 0.0 collective-permute-done.2.far
  7.8 0.3 %pack_sides.1 = (f32[4,16,128]{2,1,0:T(8,128)S(1)}, f32[8,128]{1,0:T(8,128)S(1)}, f32[8,128]{1,0:T(8,128)S(1)}) custom-call(f32[4,16,128]{2,1,0:T(8,128)S(1)} %collective-permute-done.1.near, f32[4,16,128]{2,1,0:T(8,128)S(1)} %collective-permute-done.2.far, f32[4,16,128]{2,1,0:T(8,128)S(1)} %get-tuple-element.21.own), custom_call_target="tpu_custom_call" | custom-call | tf_op jit(solution)/shard_map/pack_sides/pallas_call | solution.py:853
  8.1 1.6 %collective-permute-start.4 = (f32[8,128]{1,0:T(8,128)S(1)}, f32[8,128]{1,0:T(8,128)S(1)}, u32[]{:S(2)}, u32[]{:S(2)}) collective-permute-start(f32[8,128]{1,0:T(8,128)S(1)} %get-tuple-element.24), channel_id=1, source_target_pairs={{0,4},{4,8},{8,12},{12,0},{1,5},{5,9},{9,13},{13,1},{2,6},{6,10},{... | collective-permute-start | bytes 12296 | tf_op jit(solution)/shard_map/ppermute | solution.py:869
  9.7 0.3 %pack_down.1.lower = f32[168,128]{1,0:T(8,128)S(1)} custom-call(f32[4,16,128]{2,1,0:T(8,128)S(1)} %get-tuple-element.22.merged, f32[8,128]{1,0:T(8,128)S(1)} %get-tuple-element.23.rest, f32[4,16,16,128]{3,2,1,0:T(8,128)S(1)} %get-tuple-element.17.fields, f32[16,16,128]{2,1,0:T(8,128)S(1)} %get-tuple-element.18.mix_h, ...), custom_call_target="tpu_custom_call" | custom-call | tf_op jit(solution)/shard_map/pack_down/pallas_call | solution.py:853
  10.0 2.3 %collective-permute-start.3 = (f32[168,128]{1,0:T(8,128)S(1)}, f32[168,128]{1,0:T(8,128)S(1)}, u32[]{:S(2)}, u32[]{:S(2)}) collective-permute-start(f32[168,128]{1,0:T(8,128)S(1)} %pack_down.1.lower), channel_id=1, source_target_pairs={{0,12},{4,0},{8,4},{12,8},{1,13},{5,1},{9,5},{13,9},{2,14},{6,2},{... | collective-permute-start | bytes 258056 | tf_op jit(solution)/shard_map/ppermute | solution.py:873
  12.3 2.2 %interior.1 = (f32[31,16,8,128]{3,2,1,0:T(8,128)S(1)}, f32[6,8,128]{2,1,0:T(8,128)S(1)}, f32[2,16,16,128]{3,2,1,0:T(8,128)S(1)}, f32[16,16,128]{2,1,0:T(8,128)S(1)}, f32[16,16,128]{2,1,0:T(8,128)S(1)}) custom-call(f32[4,16,128]{2,1,0:T(8,128)S(1)} %get-tuple-element.22.merged, f32[4,16,128]{2,1,0:T(8,128)S(1)} %get-tuple-element.21.own, ...), custom_call_target="tpu_custom_call" | custom-call | flops 100000000 | bytes 100000000 | tf_op jit(solution)/shard_map/interior/pallas_call | solution.py:875
  14.6 0.0 collective-permute-done.4.corner
  14.6 0.4 %open_below.1.opened = f32[3,16,8,128]{3,2,1,0:T(8,128)S(1)} custom-call(s32[1]{0:T(128)S(6)} %copy.9.seam, f32[8,128]{1,0:T(8,128)S(1)} %collective-permute-done.4.corner, f32[4,16,128]{2,1,0:T(8,128)S(1)} %get-tuple-element.22.merged, f32[31,16,8,128]{3,2,1,0:T(8,128)S(1)} %get-tuple-element.26.edges, f32[6,8,128]{2,1,0:T(8,128)S(1)} %get-tuple-element.27.edge_levels), custom_call_target="tpu_custom_call" | custom-call | flops 900000000 | bytes 900000000 | tf_op jit(solution)/shard_map/open_below/pallas_call | solution.py:902
  15.0 0.0 collective-permute-done.from_below
  15.0 0.0 collective-permute-done.3.from_above
  15.0 1.4 %finish.1 = (f32[2,16,16,128]{3,2,1,0:T(8,128)}, f32[16,16,128]{2,1,0:T(8,128)}, f32[16,16,128]{2,1,0:T(8,128)}) custom-call(s32[1]{0:T(128)S(6)} %copy.9.seam, f32[168,128]{1,0:T(8,128)S(1)} %collective-permute-done.from_below, f32[168,128]{1,0:T(8,128)S(1)} %collective-permute-done.3.from_above, f32[3,16,8,128]{3,2,1,0:T(8,128)S(1)} %open_below.1.opened, ...), custom_call_target="tpu_custom_call" | custom-call | tf_op jit(solution)/shard_map/finish/pallas_call | solution.py:911
Async XLA Ops:
  2.7 5.0 %collective-permute-start.1 = (f32[4,16,128]{2,1,0:T(8,128)S(1)}, f32[4,16,128]{2,1,0:T(8,128)S(1)}, u32[]{:S(2)}, u32[]{:S(2)}) collective-permute-start(f32[4,16,128]{2,1,0:T(8,128)S(1)} %get-tuple-element.21.own), channel_id=1, source_target_pairs={{0,1},{1,0},{2,3},{3,2},{4,5},{5,4},{6,7},{7,6},{8,9},{9,8},{10,11... | collective-permute-start | bytes 98312 | tf_op jit(solution)/shard_map/ppermute | solution.py:850
  3.3 4.5 %collective-permute-start.2 = (f32[4,16,128]{2,1,0:T(8,128)S(1)}, f32[4,16,128]{2,1,0:T(8,128)S(1)}, u32[]{:S(2)}, u32[]{:S(2)}) collective-permute-start(f32[4,16,128]{2,1,0:T(8,128)S(1)} %get-tuple-element.21.own), channel_id=1, source_target_pairs={{0,3},{1,2},{2,1},{3,0},{4,7},{5,6},{6,5},{7,4},{8,11},{9,10},{10,... | collective-permute-start | bytes 98312 | tf_op jit(solution)/shard_map/ppermute | solution.py:849
  6.1 8.9 %collective-permute-start = (f32[168,128]{1,0:T(8,128)S(1)}, f32[168,128]{1,0:T(8,128)S(1)}, u32[]{:S(2)}, u32[]{:S(2)}) collective-permute-start(f32[168,128]{1,0:T(8,128)S(1)} %pack_up.1.upper), channel_id=1, source_target_pairs={{0,4},{4,8},{8,12},{12,0},{1,5},{5,9},{9,13},{13,1},{2,6},{6,10},{... | collective-permute-start | bytes 258056 | tf_op jit(solution)/shard_map/ppermute | solution.py:861
  8.1 6.5 %collective-permute-start.4 = (f32[8,128]{1,0:T(8,128)S(1)}, f32[8,128]{1,0:T(8,128)S(1)}, u32[]{:S(2)}, u32[]{:S(2)}) collective-permute-start(f32[8,128]{1,0:T(8,128)S(1)} %get-tuple-element.24), channel_id=1, source_target_pairs={{0,4},{4,8},{8,12},{12,0},{1,5},{5,9},{9,13},{13,1},{2,6},{6,10},{... | collective-permute-start | bytes 12296 | tf_op jit(solution)/shard_map/ppermute | solution.py:869
  10.0 5.0 %collective-permute-start.3 = (f32[168,128]{1,0:T(8,128)S(1)}, f32[168,128]{1,0:T(8,128)S(1)}, u32[]{:S(2)}, u32[]{:S(2)}) collective-permute-start(f32[168,128]{1,0:T(8,128)S(1)} %pack_down.1.lower), channel_id=1, source_target_pairs={{0,12},{4,0},{8,4},{12,8},{1,13},{5,1},{9,5},{13,9},{2,14},{6,2},{... | collective-permute-start | bytes 258056 | tf_op jit(solution)/shard_map/ppermute | solution.py:873

commit v5 on v4

--- a/solution.py
+++ b/solution.py
@@ -57,22 +57,18 @@
     )
 
 
-def loop(count, body, carry):
-    for n in range(count):
-        carry = body(n, carry)
-    return carry
-
-
-def north(value, beyond):
-    sub = iota(8, 0)
+def tile_of(q, k, depth):
+    return slice((q * depth + k) * ROWS, (q * depth + k + 1) * ROWS)
+
+
+def up(value):
     low, high = roll(value[:8], -1, 0), roll(value[8:], -1, 0)
-    return jnp.concatenate([jnp.where(sub == 7, high, low), jnp.where(sub == 7, beyond, high)], axis=0)
-
-
-def south(value, beyond):
-    sub = iota(8, 0)
+    return jnp.concatenate([jnp.where(iota(8, 0) == 7, high, low), high], axis=0)
+
+
+def down(value):
     low, high = roll(value[:8], 1, 0), roll(value[8:], 1, 0)
-    return jnp.concatenate([jnp.where(sub == 0, beyond, low), jnp.where(sub == 0, low, high)], axis=0)
+    return jnp.concatenate([low, jnp.where(iota(8, 0) == 0, low, high)], axis=0)
 
 
 def bond(mix_v, level, k, depth):
@@ -118,8 +114,8 @@
             (
                 (levels_in, levels),
                 (mix_v_in, mix_v),
-                (costate, fields.at[2:]),
-                (tracers, fields.at[:2]),
+                (costate, fields.at[2 * depth * ROWS :]),
+                (tracers, fields.at[: 2 * depth * ROWS]),
                 (mix_h_in, mix_h),
             )
         )
@@ -150,16 +146,17 @@
     values = [zero, zero]
     for k in range(depth):
         for t in range(2):
-            values[t] = fields[2 + t, k] * factors[0, k] + factors[1, k] * values[t]
-            fields[2 + t, k] = values[t]
+            values[t] = fields[tile_of(2 + t, k, depth)] * factors[0, k] + factors[1, k] * values[t]
+            fields[tile_of(2 + t, k, depth)] = values[t]
     firsts = [zero] * tiles
     values = [zero, zero]
     for k in range(depth - 1, -1, -1):
         tile, base = k // PER_TILE, GROUP * (k % PER_TILE)
         for t in range(2):
-            values[t] = fields[2 + t, k] + factors[2, k] * values[t]
-            fields[2 + t, k] = values[t]
-        for q, value in enumerate((fields[0, k], fields[1, k], *values)):
+            values[t] = fields[tile_of(2 + t, k, depth)] + factors[2, k] * values[t]
+            fields[tile_of(2 + t, k, depth)] = values[t]
+        for q in range(4):
+            value = fields[tile_of(q, k, depth)] if q < 2 else values[q - 2]
             firsts[tile] = jnp.where(
                 place == base // 4 + q, roll(value, base + 4 * q + 2, 1), firsts[tile]
             )
@@ -178,7 +175,7 @@
         weights = weights_of(k)
         block = jnp.zeros((8, LANES), jnp.float32)
         for q in range(4):
-            value = fields[q, k, half]
+            value = fields[tile_of(q, k, depth)][half]
             halo = halo_of(k, q)
             part = value
             for near, weight in zip(
@@ -292,21 +289,6 @@
     return value + roll(value, 8, 1)
 
 
-def near_all(value, halo, below_row=0.0, above_row=0.0):
-    return (
-        north(value, above_row),
-        south(value, below_row),
-        east(value, halo),
-        west(value, halo),
-    )
-
-
-def steps_of(fields, merged, k, q):
-    value = fields[q, k]
-    halo = rim(merged[k // PER_TILE], GROUP * (k % PER_TILE) + 4 * q)
-    return value, [near - value for near in near_all(value, halo)]
-
-
 EDGES = (
     "field",
     "mix",
@@ -326,9 +308,8 @@
     "cross_west",
     "cross_inner",
     "inside",
-    "adjoint",
-    "adjoint_1",
-    "later",
+    "after",
+    "after_1",
     "ahead",
     "ahead_1",
     "grad_h",
@@ -364,7 +345,15 @@
     return out
 
 
-def interior(
+def nears_of(value, halo):
+    return east(value, halo), west(value, halo), up(value), down(value)
+
+
+def at(q):
+    return slice(q * ROWS, (q + 1) * ROWS)
+
+
+def interior_down(
     merged,
     own,
     fields,
@@ -372,208 +361,235 @@
     mix_h,
     mix_v,
     levels,
-    lower,
-    upper,
-    edges,
-    edge_levels,
-    adjoint,
-    grad_h,
-    grad_v,
+    sent,
     inside,
+    steps,
+    weights,
     columns,
     column_factors,
-    weights,
+    up_factors,
+    shallow_out,
     packed,
-    later,
-    up_factors,
 ):
     depth = mix_h.shape[0]
-    face_below = jnp.zeros((ROWS, LANES), jnp.float32)
-    inverse = face_below
-    level_int = levels[...]
+    tiles = depth // PER_TILE
+    lane = iota(ROWS, 1)
+    zero = jnp.zeros((ROWS, LANES), jnp.float32)
+    level = levels[...]
+    face_below = inverse = zero
     for k in range(depth - 1, -1, -1):
-        face_above = bond(mix_v, level_int, k - 1, depth)
+        face_above = bond(mix_v, level, k - 1, depth)
         inverse = pivot(face_below, face_above, inverse)
         up_factors[0, k] = inverse
         up_factors[1, k] = face_below * inverse
         up_factors[2, k] = face_above * inverse
         face_below = face_above
-    tiles = depth // PER_TILE
-    lane = iota(ROWS, 1)
-    zero = jnp.zeros((ROWS, LANES), jnp.float32)
 
     column = lane % 4
-
-    def around(value, mine):
-        return (
-            mine,
-            jnp.where(column == 1, roll(value, -2, 1), roll(value, 2, 1)),
-            north(value, 0.0),
-            south(value, 0.0),
-        )
-
+    last_row, first_row = iota(ROWS, 0) == ROWS - 1, iota(ROWS, 0) == 0
     for j in range(tiles):
         level_k = (lane // GROUP + j * PER_TILE).astype(jnp.float32)
-        here = [coefficient(merged[tiles + j], n) for n in range(3)]
-        (mix, mixes), (level, level_near) = [
-            (here[n], around(here[n], coefficient(own[tiles + j], n))) for n in (0, 2)
-        ]
+        mix, bonds, depths = [coefficient(merged[tiles + j], n) for n in range(3)]
+        own_mix, own_depths = [coefficient(own[tiles + j], n) for n in (0, 2)]
         value = merged[j]
-        mixed = value
-        for near, near_mix, near_level in zip(around(value, own[j]), mixes, level_near):
-            weight = jnp.where(
-                jnp.minimum(level, near_level) > level_k, 0.5 * (mix + near_mix), 0.0
+
+        def outer(array):
+            return jnp.where(column == 1, roll(array, -2, 1), roll(array, 2, 1))
+
+        def weight(near_depths, near_mix):
+            return jnp.where(
+                jnp.minimum(depths, near_depths) > level_k, 0.5 * (mix + near_mix), 0.0
             )
-            mixed = mixed + weight * (near - value)
+
+        mixed = value + weight(own_depths, own_mix) * (own[j] - value)
+        mixed = mixed + weight(outer(depths), outer(mix)) * (outer(value) - value)
+        for border, shift in ((last_row, up), (first_row, down)):
+            flow = weight(shift(depths), shift(mix)) * (shift(value) - value)
+            mixed = mixed + jnp.where(border, 0.0, flow)
         packed[0, j] = mixed
-        packed[1, j] = here[1]
+        packed[1, j] = bonds
         if j == 0:
-            level_columns = level
+            level_columns = depths
 
     def unpacked(n, k):
         return roll(packed[n, k // PER_TILE], -GROUP * (k % PER_TILE), 1)
 
-    level = levels[...].astype(jnp.float32)
-    shallow = [jnp.minimum(level, near) for near in near_all(level, rim(merged[tiles], 8))]
-
-    def first(k, carry):
-        (col_bond, col_inverse, col_value), values = carry
+    level = level.astype(jnp.float32)
+    shallow = [jnp.minimum(level, near) for near in nears_of(level, rim(merged[tiles], 8))]
+    shallow[2] = jnp.where(last_row, 0.0, shallow[2])
+    shallow[3] = jnp.where(first_row, 0.0, shallow[3])
+    for n in range(4):
+        shallow_out[n] = shallow[n]
+
+    bond_above = col_inverse = col_value = zero
+    values = [zero] * 4
+    for k in range(depth):
+        j, i = divmod(k, PER_TILE)
         under = min(k + 1, depth - 1)
         bond_here = jnp.where(
             level_columns > k + 1.0, 0.5 * (unpacked(1, k) + unpacked(1, under)), 0.0
         )
-        col_inverse = pivot(col_bond, bond_here, col_inverse)
-        col_factor = col_bond * col_inverse
+        col_inverse = pivot(bond_above, bond_here, col_inverse)
+        col_factor = bond_above * col_inverse
         col_value = unpacked(0, k) * col_inverse + col_factor * col_value
         columns[k] = col_value
         column_factors[0, k] = col_inverse
         column_factors[1, k] = col_factor
         column_factors[2, k] = bond_here * col_inverse
+        bond_above = bond_here
         mix = mix_h[k]
-        mix_rim = rim(merged[tiles + k // PER_TILE], GROUP * (k % PER_TILE))
         weight = [
             jnp.where(open_to > float(k), 0.5 * (mix + near), 0.0)
-            for open_to, near in zip(shallow, near_all(mix, mix_rim))
+            for open_to, near in zip(shallow, nears_of(mix, rim(merged[tiles + j], GROUP * i)))
         ]
         for n in range(4):
             weights[k, n] = weight[n]
-        inverse, factor = factors[0, k], factors[1, k]
-        values = list(values)
         for q in range(4):
-            value, steps = steps_of(fields, merged, k, q)
+            value = fields[tile_of(q, k, depth)]
+            step = [near - value for near in nears_of(value, rim(merged[j], GROUP * i + 4 * q))]
             for n in range(4):
-                value = value + weight[n] * steps[n]
-            values[q] = value * inverse + factor * values[q]
-            inside[k, q] = values[q]
-        return (bond_here, col_inverse, col_value), tuple(values)
-
-    loop(depth, first, ((zero,) * 3, (zero,) * 4))
-
-    def second(n, carry):
-        col_value, values, later_values = carry
-        k = depth - 1 - n
+                steps[k, q, n] = step[n]
+                value = value + weight[n] * step[n]
+            values[q] = value * factors[0, k] + factors[1, k] * values[q]
+            inside[k, at(q)] = values[q]
+
+
+def interior_up(
+    inside_in,
+    steps,
+    weights,
+    columns,
+    column_factors,
+    up_factors,
+    shallow_in,
+    factors,
+    inside,
+    after,
+    adjoint,
+    grad_h,
+):
+    depth = grad_h.shape[0]
+    zero = jnp.zeros((ROWS, LANES), jnp.float32)
+    shallow = [shallow_in[n] for n in range(4)]
+    col_value = zero
+    values = [zero] * 4
+    later_values = [zero] * 2
+    for k in range(depth - 1, -1, -1):
         col_value = columns[k] + column_factors[2, k] * col_value
-        columns[k] = col_value
-        values, later_values = list(values), list(later_values)
-        first_steps, later_steps = [], []
+        later_steps = []
         for q in range(4):
-            value = inside[k, q] + factors[2, k] * values[q]
-            inside[k, q] = value
+            value = inside_in[k, at(q)] + factors[2, k] * values[q]
+            inside[k, at(q)] = value
             values[q] = value
-            steps = [near - value for near in near_all(value, rim(col_value, 4 * q))]
-            later_steps.append(steps)
-            first_steps.append(steps_of(fields, merged, k, q)[1])
+            step = [near - value for near in nears_of(value, rim(col_value, 4 * q))]
+            later_steps.append(step)
             for n in range(4):
-                value = value + weights[k, n] * steps[n]
+                value = value + weights[k, n] * step[n]
             if q < 2:
                 later_values[q] = value * up_factors[0, k] + up_factors[1, k] * later_values[q]
-                later[k, q] = later_values[q]
+                value = later_values[q]
             else:
                 adjoint[q - 2, k] = value
+            after[k, at(q)] = value
         total = zero
         for n in range(4):
             face = zero
             for t in range(2):
-                face = face + first_steps[t][n] * later_steps[2 + t][n]
-                face = face + later_steps[t][n] * first_steps[2 + t][n]
+                face = face + steps[k, t, n] * later_steps[2 + t][n]
+                face = face + later_steps[t][n] * steps[k, 2 + t, n]
             total = total + jnp.where(shallow[n] > float(k), face, 0.0)
         grad_h[k] = -0.5 * total
-        return col_value, tuple(values), tuple(later_values)
-
-    loop(depth, second, (zero, (zero,) * 4, (zero,) * 2))
-
+
+
+def interior_edges(
+    merged,
+    fields,
+    factors,
+    mix_h,
+    levels,
+    inside,
+    after,
+    weights,
+    column_factors,
+    up_factors,
+    shallow,
+    grad_h,
+    edges,
+    edge_levels,
+    grad_v,
+    later,
+):
+    depth = mix_h.shape[0]
+    tiles = depth // PER_TILE
+    zero = jnp.zeros((ROWS, LANES), jnp.float32)
+    level = levels[...].astype(jnp.float32)
     face_above = zero
+    for t in range(2):
+        later[0, at(t)] = after[0, at(t)]
     for k in range(depth):
         if k > 0:
             total = zero
             for t in range(2):
-                later[k, t] = later[k, t] + up_factors[2, k] * later[k - 1, t]
-                total = total + (inside[k - 1, 2 + t] - inside[k, 2 + t]) * (
-                    inside[k - 1, t] - inside[k, t]
+                later_here = after[k, at(t)] + up_factors[2, k] * later[k - 1, at(t)]
+                later[k, at(t)] = later_here
+                total = total + (inside[k - 1, at(2 + t)] - inside[k, at(2 + t)]) * (
+                    inside[k - 1, at(t)] - inside[k, at(t)]
                 )
-                total = total + (fields[2 + t, k - 1] - fields[2 + t, k]) * (
-                    later[k - 1, t] - later[k, t]
-                )
+                total = total + (
+                    fields[tile_of(2 + t, k - 1, depth)] - fields[tile_of(2 + t, k, depth)]
+                ) * (later[k - 1, at(t)] - later_here)
             face = jnp.where(level > float(k), total, 0.0)
             grad_v[k - 1] = -0.5 * (face + face_above)
             face_above = face
     grad_v[depth - 1] = -0.5 * face_above
 
-    def ends(value, depth_in=0):
-        return both(value[depth_in : depth_in + 1], value[ROWS - 1 - depth_in : ROWS - depth_in])
+    def ends(value, inset=0):
+        return both(value[inset : inset + 1], value[ROWS - 1 - inset : ROWS - inset])
+
+    def four(ref, start, stride, inset=0):
+        low, high = start + inset, start + ROWS - 1 - inset
+        return stacked(
+            *(ref[row + q * stride : row + q * stride + 1] for row in (low, high) for q in range(4))
+        )
+
+    last_lane, first_lane = iota(8, 1) == LANES - 1, iota(8, 1) == 0
 
     coef_rows = ends(merged[tiles])
     for n, value in enumerate(
         (
             ends(level),
             ends(level, 1),
-            ends(shallow[2]),
-            ends(shallow[3]),
-            both(shallow[0][:1], shallow[1][ROWS - 1 :]),
+            ends(shallow[0]),
+            ends(shallow[1]),
+            both(shallow[2, :1], shallow[3, ROWS - 1 :]),
             rim(coef_rows, 8),
         )
     ):
         edge_levels[n] = value
-    last_lane, first_lane = iota(8, 1) == LANES - 1, iota(8, 1) == 0
-
-    def four(row, depth_in):
-        low, high = depth_in, ROWS - 1 - depth_in
-        return stacked(
-            *(row(q, slice(low, low + 1)) for q in range(4)),
-            *(row(q, slice(high, high + 1)) for q in range(4)),
-        )
 
     for k in range(depth):
         j, i = divmod(k, PER_TILE)
-        block = slice(8 * k, 8 * k + 8)
-        field = both(lower[block], roll(upper[block], 4, 0))
-        field_1 = four(lambda q, r: fields[q, k, r], 1)
+        field = four(fields, k * ROWS, depth * ROWS)
+        field_1 = four(fields, k * ROWS, depth * ROWS, 1)
         column = at_edges(ends(merged[j]), GROUP * i)
-        steps = (
-            jnp.where(last_lane, column, roll(field, -1, 1)) - field,
-            jnp.where(first_lane, column, roll(field, 1, 1)) - field,
-            field_1 - field,
-        )
-
-        def tracer(ref):
-            return lambda q, r: ref[k, q, r] if q < 2 else None
-
-        def result(q, r):
-            return adjoint[q - 2, k, r] if q > 1 else None
-
         things = dict(
             field=field,
             mix=ends(mix_h[k]),
-            to_east=ends(weights[k, 2]),
-            to_west=ends(weights[k, 3]),
-            to_inner=both(weights[k, 0, :1], weights[k, 1, ROWS - 1 :]),
-            cross_east=exchange(steps[0]),
-            cross_west=exchange(steps[1]),
-            cross_inner=exchange(steps[2]),
-            inside=four(lambda q, r: inside[k, q, r], 0),
-            adjoint=four(result, 0),
-            adjoint_1=four(result, 1),
-            later=four(tracer(later), 0),
+            to_east=ends(weights[k, 0]),
+            to_west=ends(weights[k, 1]),
+            to_inner=both(weights[k, 2, :1], weights[k, 3, ROWS - 1 :]),
+            cross_east=exchange(jnp.where(last_lane, column, roll(field, -1, 1)) - field),
+            cross_west=exchange(jnp.where(first_lane, column, roll(field, 1, 1)) - field),
+            cross_inner=exchange(field_1 - field),
+            inside=four(inside.at[k], 0, ROWS),
+            after=stacked(
+                *(
+                    (later if q < 2 else after)[k, q * ROWS + row : q * ROWS + row + 1]
+                    for row in (0, ROWS - 1)
+                    for q in range(4)
+                )
+            ),
+            after_1=four(after.at[k], 0, ROWS, 1),
             ahead=roll(field, -2, 0),
             ahead_1=roll(field_1, -2, 0),
             grad_h=ends(grad_h[k]),
@@ -597,27 +613,16 @@
     return jnp.where((lax.axis_index("tx") == border) & (code > 0.5), swapped, block)
 
 
-def open_below(seam, corner, merged, edges, edge_levels, opened):
-    depth = opened.shape[1]
-    tiles = depth // PER_TILE
+def open_below(seam, corner, merged, edge_levels, opened):
+    tiles = merged.shape[0] // 2
     turn = (seam[0] == 1) & (lax.axis_index("tx") == 0)
     block = corner[...]
     flows = jnp.where(turn, crossed(block), block)
     block = turned_corner(block, merged, tiles, 0)
-    sub, lane = iota(8, 0), iota(8, 1)
-    inside = (sub < 4) & ((lane == 0) | (lane == LANES - 1))
-    level = jnp.minimum(
+    opened[0] = jnp.where(iota(8, 0) < 2 * tiles, block, flows)
+    opened[1] = jnp.minimum(
         rim(block[tiles : tiles + 1], 8), edge_levels[EDGE_LEVELS.index("column")]
     )
-    for k in range(depth):
-        j, i = divmod(k, PER_TILE)
-        mix = rim(block[tiles + j : tiles + j + 1], GROUP * i)
-        weight = 0.5 * (mix + edges[EDGES.index("mix_column"), k])
-        opened[0, k] = at_edges(block[j : j + 1], GROUP * i) - edges[EDGES.index("column"), k]
-        opened[1, k] = jnp.where(level > float(k), weight, 0.0)
-        opened[2, k] = jnp.where(
-            inside, at_edges(flows[2 * tiles + j : 2 * tiles + j + 1], GROUP * i), 0.0
-        )
 
 
 def finish(
@@ -681,7 +686,12 @@
         grad_h[k] = grad_h_in[k]
         grad_v[k] = grad_v_in[k]
 
-    corner = turned_corner(above[base_level : base_level + 8], merged, tiles, last)
+    corner_above = turned_corner(above[base_level : base_level + 8], merged, tiles, last)
+
+    def corner(r):
+        return both(opened[0, r : r + 1], corner_above[1 + r : 2 + r])
+
+    beside = (sub < 4) & ((lane == 0) | (lane == LANES - 1))
 
     def outer(start, k=0):
         at = slice(start + k, start + k + 1)
@@ -689,7 +699,10 @@
 
     level_out = outer(base_level)
     level_face = jnp.minimum(level_out, edge_level("own"))
-    level_corner = jnp.minimum(rim(corner[1 + tiles : 2 + tiles], 8), edge_level("column"))
+    level_corner = both(
+        opened[1],
+        jnp.minimum(rim(corner_above[1 + tiles : 2 + tiles], 8), edge_level("column")),
+    )
 
     bond_above = inverse = out_value = added = column_added = zero
     flows = []
@@ -704,20 +717,19 @@
         )
         inverse = pivot(bond_above, bond_here, inverse)
         out = both(below_block, roll(above_block, 4, 0))
-        part = both(roll(below_block, 4, 0), above_block) + opened[2, k]
+        part = both(roll(below_block, 4, 0), above_block) + jnp.where(
+            beside, at_edges(opened[0, 2 * tiles + j : 2 * tiles + j + 1], GROUP * i), 0.0
+        )
         step = out - edge("field", k)
         weight = jnp.where(level_face > float(k), 0.5 * (outer(base_mix, k) + edge("mix", k)), 0.0)
         flow = weight * step
         out_value = (part - flow) * inverse + bond_above * inverse * out_value
         added = flow * edge("inv_down", k) + edge("up_down", k) * added
-        mix_corner = rim(corner[1 + tiles + j : 2 + tiles + j], GROUP * i)
-        weight_corner = both(
-            opened[1, k],
-            jnp.where(level_corner > float(k), 0.5 * (mix_corner + edge("mix_column", k)), 0.0),
-        )
-        step_corner = both(
-            opened[0, k], at_edges(corner[1 + j : 2 + j], GROUP * i) - edge("column", k)
-        )
+        mix_corner = rim(corner(tiles + j), GROUP * i)
+        weight_corner = jnp.where(
+            level_corner > float(k), 0.5 * (mix_corner + edge("mix_column", k)), 0.0
+        )
+        step_corner = at_edges(corner(j), GROUP * i) - edge("column", k)
         column_added = (
             weight_corner * step_corner * edge("inv_column", k)
             + edge("up_column", k) * column_added
@@ -752,8 +764,8 @@
         later_1 = inner_flow * edge("inv_up_1", k) + edge("up_up_1", k) * later_1
         later[0, k] = later_0
         later[1, k] = later_1
-        result = edge("adjoint", k) + change
-        result_1 = edge("adjoint_1", k) + inner_flow
+        result = edge("after", k) + change
+        result_1 = edge("after_1", k) + inner_flow
         for t in range(2):
             for at, source, row in (
                 (0, result, 2),
@@ -798,7 +810,7 @@
         if k < depth:
             step = rows[0, k - 1] - rows[0, k]
             next_0 = step * roll(step, -2, 0) + (edge("ahead", k - 1) - edge("ahead", k)) * (
-                edge("later", k - 1) + above_0 - edge("later", k) - later_0
+                edge("after", k - 1) + above_0 - edge("after", k) - later_0
             )
             next_1 = (edge("ahead_1", k - 1) - edge("ahead_1", k)) * (above_1 - later_1)
             next_0 = jnp.where(
@@ -827,10 +839,14 @@
     vmem = pl.BlockSpec(memory_space=pltpu.VMEM)
     hbm = pl.BlockSpec(memory_space=pltpu.HBM)
     tile = (ROWS, LANES)
+
+    def flat(array):
+        return array.reshape(-1, LANES)
+
     fields, factors, own, mix_h, mix_v, levels_here = pl.pallas_call(
         prepare,
         out_shape=(
-            vmem_out(4, depth, *tile),
+            vmem_out(4 * depth * ROWS, LANES),
             vmem_out(3, depth, *tile),
             vmem_out(2 * tiles, *tile),
             vmem_out(depth, *tile),
@@ -841,13 +857,16 @@
         scratch_shapes=[pltpu.SemaphoreType.DMA((5,))],
         compiler_params=params,
         name="prepare",
-    )(seam_code, *(in_hbm(a) for a in (tracers, costate, mixing_h, mixing_v, levels)))
+    )(seam_code, *(in_hbm(a) for a in (flat(tracers), flat(costate), mixing_h, mixing_v, levels)))
 
     count = lax.axis_size("ty")
     near_pairs = [(i, i ^ 1) for i in range(count)]
     far_pairs = [(i, (i + 1 if i % 2 else i - 1) % count) for i in range(count)]
     far = lax.ppermute(own, "ty", far_pairs)
     near = lax.ppermute(own, "ty", near_pairs)
+
+    def cost(work):
+        return pl.CostEstimate(flops=work, bytes_accessed=work, transcendentals=0)
 
     def call(body, outs, *operands, **options):
         return pl.pallas_call(
@@ -872,41 +891,53 @@
     )
     from_above = lax.ppermute(lower, "tx", downward)
     row_block = (depth, 8, LANES)
-    inner = pl.pallas_call(
-        interior,
-        out_shape=(
-            vmem_out(len(EDGES), *row_block),
-            vmem_out(len(EDGE_LEVELS), 8, LANES),
-            vmem_out(2, depth, *tile),
-            vmem_out(depth, *tile),
-            vmem_out(depth, *tile),
-        ),
-        scratch_shapes=[
+    inside, steps, weights, columns, column_factors, up_factors, shallow = call(
+        interior_down,
+        (
+            vmem_out(depth, 4 * ROWS, LANES),
+            vmem_out(depth, 4, 4, *tile),
             vmem_out(depth, 4, *tile),
             vmem_out(depth, *tile),
             vmem_out(3, depth, *tile),
-            vmem_out(depth, 4, *tile),
-            vmem_out(2, tiles, *tile),
-            vmem_out(depth, 2, *tile),
             vmem_out(3, depth, *tile),
-        ],
-        compiler_params=params,
-        cost_estimate=pl.CostEstimate(flops=100_000_000, bytes_accessed=100_000_000, transcendentals=0),
-        name="interior",
-    )(
-        *(
-            in_vmem(a)
-            for a in (merged, own, fields, factors, mix_h, mix_v, levels_here, lower, upper)
-        )
-    )
+            vmem_out(4, *tile),
+        ),
+        *(merged, own, fields, factors, mix_h, mix_v, levels_here, lower),
+        scratch_shapes=[vmem_out(2, tiles, *tile)],
+        cost_estimate=cost(30_000_000),
+    )
+    inside, after, adjoint, grad_h = call(
+        interior_up,
+        (
+            vmem_out(depth, 4 * ROWS, LANES),
+            vmem_out(depth, 4 * ROWS, LANES),
+            vmem_out(2, depth, *tile),
+            vmem_out(depth, *tile),
+        ),
+        *(inside, steps, weights, columns, column_factors, up_factors, shallow, factors),
+        cost_estimate=cost(30_000_000),
+    )
+    edges, edge_levels, grad_v = call(
+        interior_edges,
+        (
+            vmem_out(len(EDGES), *row_block),
+            vmem_out(len(EDGE_LEVELS), 8, LANES),
+            vmem_out(depth, *tile),
+        ),
+        *(merged, fields, factors, mix_h, levels_here, inside, after),
+        *(weights, column_factors, up_factors, shallow, grad_h),
+        scratch_shapes=[vmem_out(depth, 2 * ROWS, LANES)],
+        cost_estimate=cost(40_000_000),
+    )
+    inner = (edges, edge_levels, adjoint, grad_h, grad_v)
     opened = pl.pallas_call(
         open_below,
-        out_shape=vmem_out(3, *row_block),
-        in_specs=[smem] + [vmem] * 4,
+        out_shape=vmem_out(2, 8, LANES),
+        in_specs=[smem] + [vmem] * 3,
         compiler_params=params,
-        cost_estimate=pl.CostEstimate(flops=900_000_000, bytes_accessed=900_000_000, transcendentals=0),
+        cost_estimate=cost(900_000_000),
         name="open_below",
-    )(seam_code, *(in_vmem(a) for a in (corner_below, merged, *inner[:2])))
+    )(seam_code, *(in_vmem(a) for a in (corner_below, merged, inner[1])))
     block = jax.ShapeDtypeStruct(mixing_h.shape, jnp.float32)
     return pl.pallas_call(
         finish,

time: 16.7 us -> 16.4 us (0.982)
  Pallas kernels: 6.43 us -> 5.98 us
    pallas_call x3 -> x2, Pallas kernels: 4.09 us -> 1.74 us  [the longest x1 1.46 us: per_device(): pl.pallas_call(prepare, out_shape=(vmem_out(4 * depth * ROWS, LANES), vme...]
    pallas_call x3 -> x6, Pallas kernels: 0.89 us -> 2.82 us  [call(): pl.pallas_call(body, out_shape=outs, compiler_params=params, name=body.__...]
    ppermute x1, starting transfers between devices: 2.61 us -> 2.44 us  [per_device(): far = lax.ppermute(own, 'ty', far_pairs)]
  transfers between devices with their start and end apart: 5 -> 5, of which waited for: 0 -> 1; matrix products, arithmetic and copies ran while one was open for 0% -> 0% of each run, Pallas kernels for 21% -> 19%
where the time goes in v5:
time: 16.4 us; the launch traced here: 16.1 us
  starting transfers between devices  8.68 us (53%)
  Pallas kernels  5.98 us (36%)
  between operations  1.34 us (8%)
    pallas_call x6, Pallas kernels, call(): pl.pallas_call(body, out_shape=outs, compiler_params=params, name=body.__...  2.82 us
    ppermute x1, starting transfers between devices, per_device(): far = lax.ppermute(own, 'ty', far_pairs)  2.44 us
    ppermute x1, starting transfers between devices, per_device(): from_above = lax.ppermute(lower, 'tx', downward)  2.16 us
    ppermute x1, starting transfers between devices, per_device(): corner_below = lax.ppermute(corner, 'tx', upward)  1.77 us
    ppermute x1, starting transfers between devices, per_device(): from_below = lax.ppermute(upper, 'tx', upward)  1.63 us
    pallas_call x1, Pallas kernels, per_device(): pl.pallas_call(prepare, out_shape=(vmem_out(4 * depth * ROWS, LANES), vme...  1.46 us
    pallas_call x1, Pallas kernels, per_device(): pl.pallas_call(finish, out_shape=(jax.ShapeDtypeStruct(tracers.shape, jnp...  1.42 us
    ppermute x1, starting transfers between devices, per_device(): near = lax.ppermute(own, 'ty', near_pairs)  0.68 us
  transfers between devices with their start and end apart: 5, of which 1 were waited for; matrix products, arithmetic and copies ran while one was open for 0% of the time, Pallas kernels for 19%

profile of v5, /device:TPU:0, one launch (start us, length us, event | category | flops | bytes accessed | tf_op | source)
XLA Modules:
  0.0 16.1 jit_solution(2789828824020126370)
XLA Ops:
  1.3 1.5 %prepare.1 = (f32[1024,128]{1,0:T(8,128)S(1)}, f32[3,16,16,128]{3,2,1,0:T(8,128)S(1)}, f32[4,16,128]{2,1,0:T(8,128)S(1)}, f32[16,16,128]{2,1,0:T(8,128)S(1)}, f3...) custom-call(s32[1]{0:T(128)S(6)} %copy.9.seam, f32[512,128]{1,0:T(8,128)} %bitcast.2, f32[512,128]{1,0:T(8,128)} %bitcast.3, ...), custom_call_target="tpu_custom_call" | custom-call | tf_op jit(solution)/shard_map/prepare/pallas_call | solution.py:846
  2.7 2.4 %collective-permute-start.2 = (f32[4,16,128]{2,1,0:T(8,128)S(1)}, f32[4,16,128]{2,1,0:T(8,128)S(1)}, u32[]{:S(2)}, u32[]{:S(2)}) collective-permute-start(f32[4,16,128]{2,1,0:T(8,128)S(1)} %get-tuple-element.30.own), channel_id=1, source_target_pairs={{0,3},{1,2},{2,1},{3,0},{4,7},{5,6},{6,5},{7,4},{8,11},{9,10},{10,... | collective-permute-start | bytes 98312 | tf_op jit(solution)/shard_map/ppermute | solution.py:865
  5.2 0.7 %collective-permute-start.1 = (f32[4,16,128]{2,1,0:T(8,128)S(1)}, f32[4,16,128]{2,1,0:T(8,128)S(1)}, u32[]{:S(2)}, u32[]{:S(2)}) collective-permute-start(f32[4,16,128]{2,1,0:T(8,128)S(1)} %get-tuple-element.30.own), channel_id=1, source_target_pairs={{0,1},{1,0},{2,3},{3,2},{4,5},{5,4},{6,7},{7,6},{8,9},{9,8},{10,11... | collective-permute-start | bytes 98312 | tf_op jit(solution)/shard_map/ppermute | solution.py:866
  5.9 0.3 %pack_up.1 = f32[168,128]{1,0:T(8,128)S(1)} custom-call(f32[1024,128]{1,0:T(8,128)S(1)} %get-tuple-element.26.fields, f32[16,16,128]{2,1,0:T(8,128)S(1)} %get-tuple-element.27.mix_h, f32[16,16,128]{2,1,0:T(8,128)S(1)} %get-tuple-element.28.mix_v, s32[16,128]{1,0:T(8,128)S(1)} %get-tuple-element.29.levels), custom_call_target="tpu_custom_call" | custom-call | tf_op jit(solution)/shard_map/pack_up/pallas_call | solution.py:872
  6.1 1.6 %collective-permute-start = (f32[168,128]{1,0:T(8,128)S(1)}, f32[168,128]{1,0:T(8,128)S(1)}, u32[]{:S(2)}, u32[]{:S(2)}) collective-permute-start(f32[168,128]{1,0:T(8,128)S(1)} %pack_up.1), channel_id=1, source_target_pairs={{0,4},{4,8},{8,12},{12,0},{1,5},{5,9},{9,13},{13,1},{2,6},{6,10},{... | collective-permute-start | bytes 258056 | tf_op jit(solution)/shard_map/ppermute | solution.py:880
  7.7 0.0 collective-permute-done.2.far
  7.8 0.0 collective-permute-done.1.near
  7.8 0.3 %pack_sides.1 = (f32[4,16,128]{2,1,0:T(8,128)S(1)}, f32[8,128]{1,0:T(8,128)S(1)}, f32[8,128]{1,0:T(8,128)S(1)}) custom-call(f32[4,16,128]{2,1,0:T(8,128)S(1)} %collective-permute-done.1.near, f32[4,16,128]{2,1,0:T(8,128)S(1)} %collective-permute-done.2.far, f32[4,16,128]{2,1,0:T(8,128)S(1)} %get-tuple-element.30.own), custom_call_target="tpu_custom_call" | custom-call | tf_op jit(solution)/shard_map/pack_sides/pallas_call | solution.py:872
  8.1 1.8 %collective-permute-start.4 = (f32[8,128]{1,0:T(8,128)S(1)}, f32[8,128]{1,0:T(8,128)S(1)}, u32[]{:S(2)}, u32[]{:S(2)}) collective-permute-start(f32[8,128]{1,0:T(8,128)S(1)} %get-tuple-element.33), channel_id=1, source_target_pairs={{0,4},{4,8},{8,12},{12,0},{1,5},{5,9},{9,13},{13,1},{2,6},{6,10},{... | collective-permute-start | bytes 12296 | tf_op jit(solution)/shard_map/ppermute | solution.py:888
  9.9 0.3 %pack_down.1.sent = f32[168,128]{1,0:T(8,128)S(1)} custom-call(f32[4,16,128]{2,1,0:T(8,128)S(1)} %get-tuple-element.31.merged, f32[8,128]{1,0:T(8,128)S(1)} %get-tuple-element.32.rest, f32[1024,128]{1,0:T(8,128)S(1)} %get-tuple-element.26.fields, f32[16,16,128]{2,1,0:T(8,128)S(1)} %get-tuple-element.27.mix_h, f32[16,16,128]{2,1,0:T(8,128)S(1)} %get-tuple-element.28.mix_v, ...), custom_call_target="tpu_custom_call" | custom-call | tf_op jit(solution)/shard_map/pack_down/pallas_call | solution.py:872
  10.2 2.2 %collective-permute-start.3 = (f32[168,128]{1,0:T(8,128)S(1)}, f32[168,128]{1,0:T(8,128)S(1)}, u32[]{:S(2)}, u32[]{:S(2)}) collective-permute-start(f32[168,128]{1,0:T(8,128)S(1)} %pack_down.1.sent), channel_id=1, source_target_pairs={{0,12},{4,0},{8,4},{12,8},{1,13},{5,1},{9,5},{13,9},{2,14},{6,2},{... | collective-permute-start | bytes 258056 | tf_op jit(solution)/shard_map/ppermute | solution.py:892
  12.3 0.8 %interior_down.1 = (f32[16,64,128]{2,1,0:T(8,128)S(1)}, f32[16,4,4,16,128]{4,3,2,1,0:T(8,128)S(1)}, f32[16,4,16,128]{3,2,1,0:T(8,128)S(1)}, f32[16,16,128]{2,1,0...) custom-call(f32[4,16,128]{2,1,0:T(8,128)S(1)} %get-tuple-element.31.merged,, ...), custom_call_target="tpu_custom_call" | custom-call | flops 30000000 | bytes 30000000 | tf_op jit(solution)/shard_map/interior_down/pallas_call | solution.py:872
  13.2 0.6 %interior_up.1 = (f32[16,64,128]{2,1,0:T(8,128)S(1)}, f32[16,64,128]{2,1,0:T(8,128)S(1)}, f32[2,16,16,128]{3,2,1,0:T(8,128)S(1)}, f32[16,16,128]{2,1,0:T(8,128)S(1)}) custom-call(f32[16,64,128]{2,1,0:T(8,128)S(1)} %get-tuple-element.35.inside_in, f32[16,4,4,16,128]{4,3,2,1,0:T(8,128)S(1)} %get-tuple-element.36.steps, ...), custom_call_target="tpu_custom_call" | custom-call | flops 30000000 | bytes 30000000 | tf_op jit(solution)/shard_map/interior_up/pallas_call | solution.py:872
  13.8 0.5 %interior_edges.1 = (f32[30,16,8,128]{3,2,1,0:T(8,128)S(1)}, f32[6,8,128]{2,1,0:T(8,128)S(1)}, f32[16,16,128]{2,1,0:T(8,128)S(1)}) custom-call(f32[4,16,128]{2,1,0:T(8,128)S(1)} %get-tuple-element.31.merged, f32[1024,128]{1,0:T(8,128)S(1)} %get-tuple-element.26.fields, f32[3,16,16,128]{3,2,1,0:T(8,128)S(1)} %get-tuple-element.34.factors, ...), custom_call_target="tpu_custom_call" | custom-call | flops 40000000 | bytes 40000000 | tf_op jit(solution)/shard_map/interior_edges/pallas_call | solution.py:872
  14.3 0.0 collective-permute-done.4.corner
  14.3 0.3 %open_below.1.opened = f32[2,8,128]{2,1,0:T(8,128)S(1)} custom-call(s32[1]{0:T(128)S(6)} %copy.9.seam, f32[8,128]{1,0:T(8,128)S(1)} %collective-permute-done.4.corner, f32[4,16,128]{2,1,0:T(8,128)S(1)} %get-tuple-element.31.merged, f32[6,8,128]{2,1,0:T(8,128)S(1)} %get-tuple-element.45.edge_levels), custom_call_target="tpu_custom_call" | custom-call | flops 900000000 | bytes 900000000 | tf_op jit(solution)/shard_map/open_below/pallas_call | solution.py:933
  14.6 0.0 collective-permute-done.from_below
  14.6 0.1 collective-permute-done.3.from_above
  14.7 1.4 %finish.1 = (f32[2,16,16,128]{3,2,1,0:T(8,128)}, f32[16,16,128]{2,1,0:T(8,128)}, f32[16,16,128]{2,1,0:T(8,128)}) custom-call(s32[1]{0:T(128)S(6)} %copy.9.seam, f32[168,128]{1,0:T(8,128)S(1)} %collective-permute-done.from_below, f32[168,128]{1,0:T(8,128)S(1)} %collective-permute-done.3.from_above, f32[2,8,128]{2,1,0:T(8,128)S(1)} %open_below.1.opened, ...), custom_call_target="tpu_custom_call" | custom-call | tf_op jit(solution)/shard_map/finish/pallas_call | solution.py:942
Async XLA Ops:
  2.7 5.0 %collective-permute-start.2 = (f32[4,16,128]{2,1,0:T(8,128)S(1)}, f32[4,16,128]{2,1,0:T(8,128)S(1)}, u32[]{:S(2)}, u32[]{:S(2)}) collective-permute-start(f32[4,16,128]{2,1,0:T(8,128)S(1)} %get-tuple-element.30.own), channel_id=1, source_target_pairs={{0,3},{1,2},{2,1},{3,0},{4,7},{5,6},{6,5},{7,4},{8,11},{9,10},{10,... | collective-permute-start | bytes 98312 | tf_op jit(solution)/shard_map/ppermute | solution.py:865
  5.2 2.6 %collective-permute-start.1 = (f32[4,16,128]{2,1,0:T(8,128)S(1)}, f32[4,16,128]{2,1,0:T(8,128)S(1)}, u32[]{:S(2)}, u32[]{:S(2)}) collective-permute-start(f32[4,16,128]{2,1,0:T(8,128)S(1)} %get-tuple-element.30.own), channel_id=1, source_target_pairs={{0,1},{1,0},{2,3},{3,2},{4,5},{5,4},{6,7},{7,6},{8,9},{9,8},{10,11... | collective-permute-start | bytes 98312 | tf_op jit(solution)/shard_map/ppermute | solution.py:866
  6.1 8.5 %collective-permute-start = (f32[168,128]{1,0:T(8,128)S(1)}, f32[168,128]{1,0:T(8,128)S(1)}, u32[]{:S(2)}, u32[]{:S(2)}) collective-permute-start(f32[168,128]{1,0:T(8,128)S(1)} %pack_up.1), channel_id=1, source_target_pairs={{0,4},{4,8},{8,12},{12,0},{1,5},{5,9},{9,13},{13,1},{2,6},{6,10},{... | collective-permute-start | bytes 258056 | tf_op jit(solution)/shard_map/ppermute | solution.py:880
  8.1 6.2 %collective-permute-start.4 = (f32[8,128]{1,0:T(8,128)S(1)}, f32[8,128]{1,0:T(8,128)S(1)}, u32[]{:S(2)}, u32[]{:S(2)}) collective-permute-start(f32[8,128]{1,0:T(8,128)S(1)} %get-tuple-element.33), channel_id=1, source_target_pairs={{0,4},{4,8},{8,12},{12,0},{1,5},{5,9},{9,13},{13,1},{2,6},{6,10},{... | collective-permute-start | bytes 12296 | tf_op jit(solution)/shard_map/ppermute | solution.py:888
  10.2 4.5 %collective-permute-start.3 = (f32[168,128]{1,0:T(8,128)S(1)}, f32[168,128]{1,0:T(8,128)S(1)}, u32[]{:S(2)}, u32[]{:S(2)}) collective-permute-start(f32[168,128]{1,0:T(8,128)S(1)} %pack_down.1.sent), channel_id=1, source_target_pairs={{0,12},{4,0},{8,4},{12,8},{1,13},{5,1},{9,5},{13,9},{2,14},{6,2},{... | collective-permute-start | bytes 258056 | tf_op jit(solution)/shard_map/ppermute | solution.py:892

commit v6 on v5

--- a/solution.py
+++ b/solution.py
@@ -88,7 +88,7 @@
 
 
 def pivot(bond_above, bond_here, inverse):
-    return 1.0 / (1.0 + bond_above + bond_here - bond_above * (bond_above * inverse))
+    return 1.0 / (1.0 + bond_above + bond_here - bond_above * bond_above * inverse)
 
 
 def prepare(
@@ -108,20 +108,21 @@
 ):
     depth = mix_h.shape[0]
     tiles = depth // PER_TILE
-    copies = [
-        pltpu.make_async_copy(source, target, sems.at[n])
-        for n, (source, target) in enumerate(
-            (
-                (levels_in, levels),
-                (mix_v_in, mix_v),
-                (costate, fields.at[2 * depth * ROWS :]),
-                (tracers, fields.at[: 2 * depth * ROWS]),
-                (mix_h_in, mix_h),
-            )
-        )
-    ]
-    for copy in copies:
-        copy.start()
+    copies = []
+    for n, (source, target, parts) in enumerate(
+        (
+            (levels_in, levels, 1),
+            (mix_v_in, mix_v, 4),
+            (costate, fields.at[2 * depth * ROWS :], 4),
+            (tracers, fields.at[: 2 * depth * ROWS], 4),
+            (mix_h_in, mix_h, 4),
+        )
+    ):
+        size = source.shape[0] // parts
+        for m in range(parts):
+            cut = slice(m * size, (m + 1) * size)
+            pltpu.make_async_copy(source.at[cut], target.at[cut], sems.at[n]).start()
+        copies.append(pltpu.make_async_copy(source, target, sems.at[n]))
     for copy in copies[:2]:
         copy.wait()
     level = levels[...]
@@ -141,8 +142,7 @@
             seconds[tile] = jnp.where(
                 place == base // 4 + n, roll(value, base + 4 * n + 2, 1), seconds[tile]
             )
-    for copy in copies[2:]:
-        copy.wait()
+    copies[2].wait()
     values = [zero, zero]
     for k in range(depth):
         for t in range(2):
@@ -150,16 +150,22 @@
             fields[tile_of(2 + t, k, depth)] = values[t]
     firsts = [zero] * tiles
     values = [zero, zero]
+
+    def add(k, q, value):
+        tile, base = k // PER_TILE, GROUP * (k % PER_TILE) + 4 * q
+        firsts[tile] = jnp.where(place == base // 4, roll(value, base + 2, 1), firsts[tile])
+
     for k in range(depth - 1, -1, -1):
-        tile, base = k // PER_TILE, GROUP * (k % PER_TILE)
         for t in range(2):
             values[t] = fields[tile_of(2 + t, k, depth)] + factors[2, k] * values[t]
             fields[tile_of(2 + t, k, depth)] = values[t]
-        for q in range(4):
-            value = fields[tile_of(q, k, depth)] if q < 2 else values[q - 2]
-            firsts[tile] = jnp.where(
-                place == base // 4 + q, roll(value, base + 4 * q + 2, 1), firsts[tile]
-            )
+            add(k, 2 + t, values[t])
+    for copy in copies[3:]:
+        copy.wait()
+    for k in range(depth):
+        tile, base = k // PER_TILE, GROUP * (k % PER_TILE)
+        for t in range(2):
+            add(k, t, fields[tile_of(t, k, depth)])
         seconds[tile] = jnp.where(
             place == base // 4, roll(mix_h[k], base + 2, 1), seconds[tile]
         )
@@ -168,114 +174,88 @@
         message[tiles + tile] = seconds[tile]
 
 
-def row_blocks(depth, row, half, weights_of, halo_of, inner_shift, fields, mix_h, mix_v, target):
+def pack_rows(fields, mix_h, mix_v, levels, lower, upper):
+    depth = mix_h.shape[0]
     sub = iota(8, 0)
-    at = row % 8
+
+    def nears(value):
+        inner = jnp.where(sub < 4, roll(value, -1, 0), roll(value, 1, 0))
+        return east(value, 0.0), west(value, 0.0), inner
+
+    level = fold(levels[...].astype(jnp.float32))
+    shallow = [jnp.minimum(level, near) for near in nears(level)]
     for k in range(depth):
-        weights = weights_of(k)
-        block = jnp.zeros((8, LANES), jnp.float32)
+        mix = fold(mix_h[k])
+        weights = [
+            jnp.where(open_to > float(k), 0.5 * (mix + near), 0.0)
+            for open_to, near in zip(shallow, nears(mix))
+        ]
+        low = jnp.zeros((8, LANES), jnp.float32)
+        high = low
         for q in range(4):
-            value = fields[tile_of(q, k, depth)][half]
-            halo = halo_of(k, q)
+            value = fold(fields[tile_of(q, k, depth)])
             part = value
-            for near, weight in zip(
-                (east(value, halo), west(value, halo), roll(value, inner_shift, 0)), weights
-            ):
+            for near, weight in zip(nears(value), weights):
                 part = part + weight * (near - value)
             for n, thing in ((q, value), (4 + q, part)):
-                block = jnp.where(sub == n, roll(thing, n - at, 0), block)
-        target[8 * k : 8 * k + 8] = block
+                low = jnp.where(sub == n, roll(thing, n, 0), low)
+                high = jnp.where(sub == n, roll(thing, n - 7, 0), high)
+        lower[8 * k : 8 * k + 8] = low
+        upper[8 * k : 8 * k + 8] = high
         for n, array in enumerate((mix_h, mix_v)):
             start = (8 + n) * depth + k
-            target[start : start + 1] = array[k, row : row + 1]
-
-
-def pack_up(fields, mix_h, mix_v, levels, upper):
-    depth = mix_h.shape[0]
-    half = slice(8, 16)
-    level = levels[half].astype(jnp.float32)
-    shallow = [
-        jnp.minimum(level, near)
-        for near in (east(level, 0.0), west(level, 0.0), roll(level, 1, 0))
-    ]
-
-    def weights_of(k):
-        mix = mix_h[k, half]
-        return [
-            jnp.where(open_to > float(k), 0.5 * (mix + near), 0.0)
-            for open_to, near in zip(shallow, (east(mix, 0.0), west(mix, 0.0), roll(mix, 1, 0)))
-        ]
-
-    row_blocks(depth, 15, half, weights_of, lambda k, q: 0.0, 1, fields, mix_h, mix_v, upper)
+            lower[start : start + 1] = array[k, :1]
+            upper[start : start + 1] = array[k, ROWS - 1 :]
+    lower[10 * depth : 10 * depth + 8] = stacked(level[:1])
     upper[10 * depth : 10 * depth + 8] = stacked(level[7:])
 
 
-def pack_sides(near, far, own, merged, corner, rest):
+def pack_sides(near, far, own, early, merged, corner, lower):
     tiles = near.shape[0] // 2
     place = lax.axis_index("ty")
     last = lax.axis_size("ty") - 1
     even = place % 2 == 0
     column = iota(ROWS, 1) % 4
-    from_west = column < 2
-    missing = ((place == 0) & from_west) | ((place == last) & jnp.logical_not(from_west))
     corners = []
+    edge = iota(8, 1) % 4
     for j in range(2 * tiles):
         west_tile = jnp.where(even, far[j], near[j])
         east_tile = jnp.where(even, near[j], far[j])
-        tile = jnp.where(from_west, west_tile, east_tile)
         if j >= tiles:
-            tile = jnp.where(missing, 0.0, tile)
-        merged[j] = crossed(tile)
+            west_tile = jnp.where(place == 0, 0.0, west_tile)
+            east_tile = jnp.where(place == last, 0.0, east_tile)
+        middle = jnp.where(column == 1, roll(east_tile, -1, 1), roll(west_tile, 1, 1))
+        merged[j] = jnp.where(
+            column == 0, west_tile, jnp.where(column == 3, east_tile, middle)
+        )
+        west_rows, east_rows = fold(west_tile), fold(east_tile)
+        middle = jnp.where(edge == 1, roll(east_rows, -1, 1), roll(west_rows, 1, 1))
         corners.append(
-            crossed(
-                fold(
-                    jnp.where(
-                        column == 0,
-                        roll(west_tile, -2, 1),
-                        jnp.where(column == 3, roll(east_tile, 2, 1), tile),
-                    )
-                )
+            jnp.where(
+                edge == 0,
+                roll(west_rows, -2, 1),
+                jnp.where(edge == 3, roll(east_rows, 2, 1), middle),
             )
         )
-    flows = []
     lane = iota(1, 1)
-    for j in range(tiles):
-        level_k = (lane // GROUP + j * PER_TILE).astype(jnp.float32)
-        mix, level = [
-            [coefficient(ref[tiles + j, ROWS - 1 :], n) for ref in (merged, own)] for n in (0, 2)
-        ]
-        weight = jnp.where(jnp.minimum(*level) > level_k, 0.5 * (mix[0] + mix[1]), 0.0)
-        flows.append(weight * (merged[j, ROWS - 1 :] - own[j, ROWS - 1 :]))
-    corner[...] = stacked(*(value[7:] for value in corners), *flows)
-    rest[...] = stacked(*(value[:1] for value in corners))
-
-
-def pack_down(merged, rest, fields, mix_h, mix_v, levels, lower):
-    depth = mix_h.shape[0]
-    tiles = depth // PER_TILE
-    half = slice(0, 8)
-    level = levels[half].astype(jnp.float32)
-    halo = rim(merged[tiles, half], 8)
-    shallow = [
-        jnp.minimum(level, near)
-        for near in (east(level, halo), west(level, halo), roll(level, -1, 0))
-    ]
-
-    def weights_of(k):
-        mix = mix_h[k, half]
-        halo = rim(merged[tiles + k // PER_TILE, half], GROUP * (k % PER_TILE))
-        return [
-            jnp.where(open_to > float(k), 0.5 * (mix + near), 0.0)
-            for open_to, near in zip(shallow, (east(mix, halo), west(mix, halo), roll(mix, -1, 0)))
-        ]
-
-    def halo_of(k, q):
-        return rim(merged[k // PER_TILE, half], GROUP * (k % PER_TILE) + 4 * q)
-
-    row_blocks(depth, 0, half, weights_of, halo_of, -1, fields, mix_h, mix_v, lower)
-    lower[10 * depth : 10 * depth + 8] = jnp.where(
-        iota(8, 0) == 0, level[:1], roll(rest[...], 1, 0)
-    )
+
+    def for_row(row, sub):
+        flows = []
+        for j in range(tiles):
+            level_k = (lane // GROUP + j * PER_TILE).astype(jnp.float32)
+            mix, level = [
+                [coefficient(ref[tiles + j, row : row + 1], n) for ref in (merged, own)]
+                for n in (0, 2)
+            ]
+            weight = jnp.where(jnp.minimum(*level) > level_k, 0.5 * (mix[0] + mix[1]), 0.0)
+            flows.append(weight * (merged[j, row : row + 1] - own[j, row : row + 1]))
+        return [value[sub : sub + 1] for value in corners] + flows
+
+    corner[...] = stacked(*for_row(ROWS - 1, 7))
+    last_block = early.shape[0] - 8
+    for r in range(0, last_block, 8):
+        lower[r : r + 8] = early[r : r + 8]
+    lower[last_block:] = stacked(early[last_block : last_block + 1], *for_row(0, 0))
 
 
 def both(low, high):
@@ -284,9 +264,11 @@
 
 def coefficient(value, n):
     kept = iota(value.shape[0], 1) % GROUP // 4 == n
-    value = roll(jnp.where(kept, value, 0.0), -4 * n, 1)
-    value = value + roll(value, 4, 1)
-    return value + roll(value, 8, 1)
+    value = jnp.where(kept, value, 0.0)
+    out = roll(value, -4 * n, 1)
+    for q in range(1, 4):
+        out = out + roll(value, 4 * (q - n), 1)
+    return out
 
 
 EDGES = (
@@ -686,12 +668,19 @@
         grad_h[k] = grad_h_in[k]
         grad_v[k] = grad_v_in[k]
 
-    corner_above = turned_corner(above[base_level : base_level + 8], merged, tiles, last)
+    last_block = above[base_level : base_level + 8]
+    corner_above = turned_corner(last_block, merged, tiles, last)
+    turn_above = (seam[0] == 1) & (place == last)
+    flows_above = jnp.where(turn_above, crossed(last_block), last_block)
 
     def corner(r):
         return both(opened[0, r : r + 1], corner_above[1 + r : 2 + r])
 
-    beside = (sub < 4) & ((lane == 0) | (lane == LANES - 1))
+    def flow_of(j):
+        r = 2 * tiles + j
+        return both(opened[0, r : r + 1], flows_above[1 + r : 2 + r])
+
+    beside = (lane == 0) | (lane == LANES - 1)
 
     def outer(start, k=0):
         at = slice(start + k, start + k + 1)
@@ -718,7 +707,7 @@
         inverse = pivot(bond_above, bond_here, inverse)
         out = both(below_block, roll(above_block, 4, 0))
         part = both(roll(below_block, 4, 0), above_block) + jnp.where(
-            beside, at_edges(opened[0, 2 * tiles + j : 2 * tiles + j + 1], GROUP * i), 0.0
+            beside, at_edges(flow_of(j), GROUP * i), 0.0
         )
         step = out - edge("field", k)
         weight = jnp.where(level_face > float(k), 0.5 * (outer(base_mix, k) + edge("mix", k)), 0.0)
@@ -876,19 +865,18 @@
     count = lax.axis_size("tx")
     upward = [(i, (i + 1) % count) for i in range(count)]
     downward = [(i, (i - 1) % count) for i in range(count)]
-    upper = call(pack_up, vmem_out(height, LANES), fields, mix_h, mix_v, levels_here)
+    early, upper = call(
+        pack_rows,
+        (vmem_out(height, LANES), vmem_out(height, LANES)),
+        *(fields, mix_h, mix_v, levels_here),
+    )
     from_below = lax.ppermute(upper, "tx", upward)
-    merged, corner, rest = call(
+    merged, corner, lower = call(
         pack_sides,
-        (vmem_out(2 * tiles, *tile), vmem_out(8, LANES), vmem_out(8, LANES)),
-        near,
-        far,
-        own,
+        (vmem_out(2 * tiles, *tile), vmem_out(8, LANES), vmem_out(height, LANES)),
+        *(near, far, own, early),
     )
     corner_below = lax.ppermute(corner, "tx", upward)
-    lower = call(
-        pack_down, vmem_out(height, LANES), merged, rest, fields, mix_h, mix_v, levels_here
-    )
     from_above = lax.ppermute(lower, "tx", downward)
     row_block = (depth, 8, LANES)
     inside, steps, weights, columns, column_factors, up_factors, shallow = call(

time: 16.4 us -> 16 us (0.976)
  Pallas kernels: 5.98 us -> 5.38 us
  waiting for transfers between devices: 0.15 us -> 0.44 us
    pallas_call x6 -> x5, Pallas kernels: 2.82 us -> 2.41 us  [call(): pl.pallas_call(body, out_shape=outs, compiler_params=params, name=body.__...]
    ppermute x1, waiting for transfers between devices: 0.14 us -> 0.43 us  [per_device(): from_above = lax.ppermute(lower, 'tx', downward)]
  transfers between devices with their start and end apart: 5 -> 5, of which waited for: 1 -> 1; matrix products, arithmetic and copies ran while one was open for 0% -> 0% of each run, Pallas kernels for 19% -> 16%
where the time goes in v6:
time: 16 us; the launch traced here: 15.8 us
  starting transfers between devices  8.62 us (54%)
  Pallas kernels  5.38 us (34%)
  between operations  1.34 us (8%)
  waiting for transfers between devices  0.44 us (3%)
    ppermute x1, starting transfers between devices, per_device(): far = lax.ppermute(own, 'ty', far_pairs)  2.44 us
    pallas_call x5, Pallas kernels, call(): pl.pallas_call(body, out_shape=outs, compiler_params=params, name=body.__...  2.41 us
    ppermute x1, starting transfers between devices, per_device(): from_above = lax.ppermute(lower, 'tx', downward)  2.12 us
    ppermute x1, starting transfers between devices, per_device(): corner_below = lax.ppermute(corner, 'tx', upward)  1.75 us
    ppermute x1, starting transfers between devices, per_device(): from_below = lax.ppermute(upper, 'tx', upward)  1.63 us
    pallas_call x1, Pallas kernels, per_device(): pl.pallas_call(prepare, out_shape=(vmem_out(4 * depth * ROWS, LANES), vme...  1.43 us
    pallas_call x1, Pallas kernels, per_device(): pl.pallas_call(finish, out_shape=(jax.ShapeDtypeStruct(tracers.shape, jnp...  1.38 us
    ppermute x1, starting transfers between devices, per_device(): near = lax.ppermute(own, 'ty', near_pairs)  0.68 us
  transfers between devices with their start and end apart: 5, of which 1 were waited for; matrix products, arithmetic and copies ran while one was open for 0% of the time, Pallas kernels for 16%

profile of v6, /device:TPU:0, one launch (start us, length us, event | category | flops | bytes accessed | tf_op | source)
XLA Modules:
  0.0 15.8 jit_solution(16403351817906546712)
XLA Ops:
  1.3 1.4 %prepare.1 = (f32[1024,128]{1,0:T(8,128)S(1)}, f32[3,16,16,128]{3,2,1,0:T(8,128)S(1)}, f32[4,16,128]{2,1,0:T(8,128)S(1)}, f32[16,16,128]{2,1,0:T(8,128)S(1)}, f3...) custom-call(s32[1]{0:T(128)S(6)} %copy.9.seam, f32[512,128]{1,0:T(8,128)} %bitcast.2, f32[512,128]{1,0:T(8,128)} %bitcast.3, ...), custom_call_target="tpu_custom_call" | custom-call | tf_op jit(solution)/shard_map/prepare/pallas_call | solution.py:835
  2.7 2.4 %collective-permute-start.2 = (f32[4,16,128]{2,1,0:T(8,128)S(1)}, f32[4,16,128]{2,1,0:T(8,128)S(1)}, u32[]{:S(2)}, u32[]{:S(2)}) collective-permute-start(f32[4,16,128]{2,1,0:T(8,128)S(1)} %get-tuple-element.33.own), channel_id=1, source_target_pairs={{0,3},{1,2},{2,1},{3,0},{4,7},{5,6},{6,5},{7,4},{8,11},{9,10},{10,... | collective-permute-start | bytes 98312 | tf_op jit(solution)/shard_map/ppermute | solution.py:854
  5.2 0.7 %collective-permute-start.1 = (f32[4,16,128]{2,1,0:T(8,128)S(1)}, f32[4,16,128]{2,1,0:T(8,128)S(1)}, u32[]{:S(2)}, u32[]{:S(2)}) collective-permute-start(f32[4,16,128]{2,1,0:T(8,128)S(1)} %get-tuple-element.33.own), channel_id=1, source_target_pairs={{0,1},{1,0},{2,3},{3,2},{4,5},{5,4},{6,7},{7,6},{8,9},{9,8},{10,11... | collective-permute-start | bytes 98312 | tf_op jit(solution)/shard_map/ppermute | solution.py:855
  5.8 0.3 %pack_rows.1 = (f32[168,128]{1,0:T(8,128)S(1)}, f32[168,128]{1,0:T(8,128)S(1)}) custom-call(f32[1024,128]{1,0:T(8,128)S(1)} %get-tuple-element.28.fields, f32[16,16,128]{2,1,0:T(8,128)S(1)} %get-tuple-element.29.mix_h, f32[16,16,128]{2,1,0:T(8,128)S(1)} %get-tuple-element.30.mix_v, s32[16,128]{1,0:T(8,128)S(1)} %get-tuple-element.31.levels), custom_call_target="tpu_custom_call" | custom-call | tf_op jit(solution)/shard_map/pack_rows/pallas_call | solution.py:861
  6.1 1.6 %collective-permute-start = (f32[168,128]{1,0:T(8,128)S(1)}, f32[168,128]{1,0:T(8,128)S(1)}, u32[]{:S(2)}, u32[]{:S(2)}) collective-permute-start(f32[168,128]{1,0:T(8,128)S(1)} %get-tuple-element.32), channel_id=1, source_target_pairs={{0,4},{4,8},{8,12},{12,0},{1,5},{5,9},{9,13},{13,1},{2,6},{6,10},{... | collective-permute-start | bytes 258056 | tf_op jit(solution)/shard_map/ppermute | solution.py:873
  7.7 0.0 collective-permute-done.2.far
  7.7 0.0 collective-permute-done.1.near
  7.8 0.2 %pack_sides.1 = (f32[4,16,128]{2,1,0:T(8,128)S(1)}, f32[8,128]{1,0:T(8,128)S(1)}, f32[168,128]{1,0:T(8,128)S(1)}) custom-call(f32[4,16,128]{2,1,0:T(8,128)S(1)} %collective-permute-done.1.near, f32[4,16,128]{2,1,0:T(8,128)S(1)} %collective-permute-done.2.far, f32[4,16,128]{2,1,0:T(8,128)S(1)} %get-tuple-element.33.own, f32[168,128]{1,0:T(8,128)S(1)} %get-tuple-element.34.early), custom_call_target="tpu_custom_call" | custom-call | tf_op jit(solution)/shard_map/pack_sides/pallas_call | solution.py:861
  8.0 1.8 %collective-permute-start.4 = (f32[8,128]{1,0:T(8,128)S(1)}, f32[8,128]{1,0:T(8,128)S(1)}, u32[]{:S(2)}, u32[]{:S(2)}) collective-permute-start(f32[8,128]{1,0:T(8,128)S(1)} %get-tuple-element.36), channel_id=1, source_target_pairs={{0,4},{4,8},{8,12},{12,0},{1,5},{5,9},{9,13},{13,1},{2,6},{6,10},{... | collective-permute-start | bytes 12296 | tf_op jit(solution)/shard_map/ppermute | solution.py:879
  9.7 2.1 %collective-permute-start.3 = (f32[168,128]{1,0:T(8,128)S(1)}, f32[168,128]{1,0:T(8,128)S(1)}, u32[]{:S(2)}, u32[]{:S(2)}) collective-permute-start(f32[168,128]{1,0:T(8,128)S(1)} %get-tuple-element.35.sent), channel_id=1, source_target_pairs={{0,12},{4,0},{8,4},{12,8},{1,13},{5,1},{9,5},{13,9},{2,14},{6,2},{... | collective-permute-start | bytes 258056 | tf_op jit(solution)/shard_map/ppermute | solution.py:880
  11.8 0.8 %interior_down.1 = (f32[16,64,128]{2,1,0:T(8,128)S(1)}, f32[16,4,4,16,128]{4,3,2,1,0:T(8,128)S(1)}, f32[16,4,16,128]{3,2,1,0:T(8,128)S(1)}, f32[16,16,128]{2,1,0...) custom-call(f32[4,16,128]{2,1,0:T(8,128)S(1)} %get-tuple-element.37.merged,, ...), custom_call_target="tpu_custom_call" | custom-call | flops 30000000 | bytes 30000000 | tf_op jit(solution)/shard_map/interior_down/pallas_call | solution.py:861
  12.7 0.6 %interior_up.1 = (f32[16,64,128]{2,1,0:T(8,128)S(1)}, f32[16,64,128]{2,1,0:T(8,128)S(1)}, f32[2,16,16,128]{3,2,1,0:T(8,128)S(1)}, f32[16,16,128]{2,1,0:T(8,128)S(1)}) custom-call(f32[16,64,128]{2,1,0:T(8,128)S(1)} %get-tuple-element.39.inside_in, f32[16,4,4,16,128]{4,3,2,1,0:T(8,128)S(1)} %get-tuple-element.40.steps, ...), custom_call_target="tpu_custom_call" | custom-call | flops 30000000 | bytes 30000000 | tf_op jit(solution)/shard_map/interior_up/pallas_call | solution.py:861
  13.3 0.5 %interior_edges.1 = (f32[30,16,8,128]{3,2,1,0:T(8,128)S(1)}, f32[6,8,128]{2,1,0:T(8,128)S(1)}, f32[16,16,128]{2,1,0:T(8,128)S(1)}) custom-call(f32[4,16,128]{2,1,0:T(8,128)S(1)} %get-tuple-element.37.merged, f32[1024,128]{1,0:T(8,128)S(1)} %get-tuple-element.28.fields, f32[3,16,16,128]{3,2,1,0:T(8,128)S(1)} %get-tuple-element.38.factors, ...), custom_call_target="tpu_custom_call" | custom-call | flops 40000000 | bytes 40000000 | tf_op jit(solution)/shard_map/interior_edges/pallas_call | solution.py:861
  13.8 0.0 collective-permute-done.4.corner
  13.8 0.2 open_below.1.opened
  14.0 0.0 collective-permute-done.from_below
  14.0 0.4 %collective-permute-done.3.from_above = f32[168,128]{1,0:T(8,128)S(1)} collective-permute-done((f32[168,128]{1,0:T(8,128)S(1)}, f32[168,128]{1,0:T(8,128)S(1)}, u32[]{:S(2)}, u32[]{:S(2)}) %collective-permute-start.3) | collective-permute-done | bytes 86048 | tf_op jit(solution)/shard_map/ppermute | solution.py:880
  14.4 1.4 %finish.1 = (f32[2,16,16,128]{3,2,1,0:T(8,128)}, f32[16,16,128]{2,1,0:T(8,128)}, f32[16,16,128]{2,1,0:T(8,128)}) custom-call(s32[1]{0:T(128)S(6)} %copy.9.seam, f32[168,128]{1,0:T(8,128)S(1)} %collective-permute-done.from_below, f32[168,128]{1,0:T(8,128)S(1)} %collective-permute-done.3.from_above, f32[2,8,128]{2,1,0:T(8,128)S(1)} %open_below.1.opened, ...), custom_call_target="tpu_custom_call" | custom-call | tf_op jit(solution)/shard_map/finish/pallas_call | solution.py:930
Async XLA Ops:
  2.7 5.0 %collective-permute-start.2 = (f32[4,16,128]{2,1,0:T(8,128)S(1)}, f32[4,16,128]{2,1,0:T(8,128)S(1)}, u32[]{:S(2)}, u32[]{:S(2)}) collective-permute-start(f32[4,16,128]{2,1,0:T(8,128)S(1)} %get-tuple-element.33.own), channel_id=1, source_target_pairs={{0,3},{1,2},{2,1},{3,0},{4,7},{5,6},{6,5},{7,4},{8,11},{9,10},{10,... | collective-permute-start | bytes 98312 | tf_op jit(solution)/shard_map/ppermute | solution.py:854
  5.2 2.6 %collective-permute-start.1 = (f32[4,16,128]{2,1,0:T(8,128)S(1)}, f32[4,16,128]{2,1,0:T(8,128)S(1)}, u32[]{:S(2)}, u32[]{:S(2)}) collective-permute-start(f32[4,16,128]{2,1,0:T(8,128)S(1)} %get-tuple-element.33.own), channel_id=1, source_target_pairs={{0,1},{1,0},{2,3},{3,2},{4,5},{5,4},{6,7},{7,6},{8,9},{9,8},{10,11... | collective-permute-start | bytes 98312 | tf_op jit(solution)/shard_map/ppermute | solution.py:855
  6.1 7.9 %collective-permute-start = (f32[168,128]{1,0:T(8,128)S(1)}, f32[168,128]{1,0:T(8,128)S(1)}, u32[]{:S(2)}, u32[]{:S(2)}) collective-permute-start(f32[168,128]{1,0:T(8,128)S(1)} %get-tuple-element.32), channel_id=1, source_target_pairs={{0,4},{4,8},{8,12},{12,0},{1,5},{5,9},{9,13},{13,1},{2,6},{6,10},{... | collective-permute-start | bytes 258056 | tf_op jit(solution)/shard_map/ppermute | solution.py:873
  8.0 5.8 %collective-permute-start.4 = (f32[8,128]{1,0:T(8,128)S(1)}, f32[8,128]{1,0:T(8,128)S(1)}, u32[]{:S(2)}, u32[]{:S(2)}) collective-permute-start(f32[8,128]{1,0:T(8,128)S(1)} %get-tuple-element.36), channel_id=1, source_target_pairs={{0,4},{4,8},{8,12},{12,0},{1,5},{5,9},{9,13},{13,1},{2,6},{6,10},{... | collective-permute-start | bytes 12296 | tf_op jit(solution)/shard_map/ppermute | solution.py:879
  9.7 4.7 %collective-permute-start.3 = (f32[168,128]{1,0:T(8,128)S(1)}, f32[168,128]{1,0:T(8,128)S(1)}, u32[]{:S(2)}, u32[]{:S(2)}) collective-permute-start(f32[168,128]{1,0:T(8,128)S(1)} %get-tuple-element.35.sent), channel_id=1, source_target_pairs={{0,12},{4,0},{8,4},{12,8},{1,13},{5,1},{9,5},{13,9},{2,14},{6,2},{... | collective-permute-start | bytes 258056 | tf_op jit(solution)/shard_map/ppermute | solution.py:880

commit v7 on v6

--- a/solution.py
+++ b/solution.py
@@ -113,9 +113,9 @@
         (
             (levels_in, levels, 1),
             (mix_v_in, mix_v, 4),
-            (costate, fields.at[2 * depth * ROWS :], 4),
             (tracers, fields.at[: 2 * depth * ROWS], 4),
             (mix_h_in, mix_h, 4),
+            (costate, fields.at[2 * depth * ROWS :], 4),
         )
     ):
         size = source.shape[0] // parts
@@ -142,25 +142,13 @@
             seconds[tile] = jnp.where(
                 place == base // 4 + n, roll(value, base + 4 * n + 2, 1), seconds[tile]
             )
-    copies[2].wait()
-    values = [zero, zero]
-    for k in range(depth):
-        for t in range(2):
-            values[t] = fields[tile_of(2 + t, k, depth)] * factors[0, k] + factors[1, k] * values[t]
-            fields[tile_of(2 + t, k, depth)] = values[t]
     firsts = [zero] * tiles
-    values = [zero, zero]
 
     def add(k, q, value):
         tile, base = k // PER_TILE, GROUP * (k % PER_TILE) + 4 * q
         firsts[tile] = jnp.where(place == base // 4, roll(value, base + 2, 1), firsts[tile])
 
-    for k in range(depth - 1, -1, -1):
-        for t in range(2):
-            values[t] = fields[tile_of(2 + t, k, depth)] + factors[2, k] * values[t]
-            fields[tile_of(2 + t, k, depth)] = values[t]
-            add(k, 2 + t, values[t])
-    for copy in copies[3:]:
+    for copy in copies[2:4]:
         copy.wait()
     for k in range(depth):
         tile, base = k // PER_TILE, GROUP * (k % PER_TILE)
@@ -169,6 +157,18 @@
         seconds[tile] = jnp.where(
             place == base // 4, roll(mix_h[k], base + 2, 1), seconds[tile]
         )
+    copies[4].wait()
+    values = [zero, zero]
+    for k in range(depth):
+        for t in range(2):
+            values[t] = fields[tile_of(2 + t, k, depth)] * factors[0, k] + factors[1, k] * values[t]
+            fields[tile_of(2 + t, k, depth)] = values[t]
+    values = [zero, zero]
+    for k in range(depth - 1, -1, -1):
+        for t in range(2):
+            values[t] = fields[tile_of(2 + t, k, depth)] + factors[2, k] * values[t]
+            fields[tile_of(2 + t, k, depth)] = values[t]
+            add(k, 2 + t, values[t])
     for tile in range(tiles):
         message[tile] = firsts[tile]
         message[tiles + tile] = seconds[tile]
@@ -202,12 +202,16 @@
                 high = jnp.where(sub == n, roll(thing, n - 7, 0), high)
         lower[8 * k : 8 * k + 8] = low
         upper[8 * k : 8 * k + 8] = high
-        for n, array in enumerate((mix_h, mix_v)):
-            start = (8 + n) * depth + k
-            lower[start : start + 1] = array[k, :1]
-            upper[start : start + 1] = array[k, ROWS - 1 :]
-    lower[10 * depth : 10 * depth + 8] = stacked(level[:1])
-    upper[10 * depth : 10 * depth + 8] = stacked(level[7:])
+        at_mix = slice(8 * depth + k, 8 * depth + k + 1)
+        lower[at_mix] = mix_h[k, :1]
+        upper[at_mix] = mix_h[k, ROWS - 1 :]
+        if k < depth - 1:
+            between = 0.5 * (mix_v[k] + mix_v[k + 1])
+            at_bond = slice(9 * depth + k, 9 * depth + k + 1)
+            lower[at_bond] = between[:1]
+            upper[at_bond] = between[ROWS - 1 :]
+    lower[10 * depth - 1 :] = level[:1]
+    upper[10 * depth - 1 :] = level[7:]
 
 
 def pack_sides(near, far, own, early, merged, corner, lower):
@@ -252,10 +256,10 @@
         return [value[sub : sub + 1] for value in corners] + flows
 
     corner[...] = stacked(*for_row(ROWS - 1, 7))
-    last_block = early.shape[0] - 8
-    for r in range(0, last_block, 8):
+    size = early.shape[0]
+    for r in range(0, size, 8):
         lower[r : r + 8] = early[r : r + 8]
-    lower[last_block:] = stacked(early[last_block : last_block + 1], *for_row(0, 0))
+    lower[size:] = stacked(*for_row(0, 0))
 
 
 def both(low, high):
@@ -635,7 +639,8 @@
     lane = iota(8, 1)
     place = lax.axis_index("tx")
     last = lax.axis_size("tx") - 1
-    base_mix, base_v, base_level = 8 * depth, 9 * depth, 10 * depth
+    base_mix, base_bond, base_level = 8 * depth, 9 * depth, 10 * depth - 1
+    size = 10 * depth
     zero = jnp.zeros((8, LANES), jnp.float32)
 
     def edge(name, k):
@@ -650,16 +655,12 @@
         @pl.when(turn)
         def _():
             back = LANES - 1 - lane
-            for r in range(0, base_level, 8):
+            for r in range(0, size, 8):
                 target[r : r + 8] = jnp.take_along_axis(source[r : r + 8], back, axis=1)
-            block = source[base_level : base_level + 8]
-            target[base_level : base_level + 8] = jnp.where(
-                sub < 1, jnp.take_along_axis(block, back, axis=1), block
-            )
 
         @pl.when(jnp.logical_not(turn))
         def _():
-            for r in range(0, base_level + 8, 8):
+            for r in range(0, size, 8):
                 target[r : r + 8] = source[r : r + 8]
 
     for k in range(depth):
@@ -668,17 +669,17 @@
         grad_h[k] = grad_h_in[k]
         grad_v[k] = grad_v_in[k]
 
-    last_block = above[base_level : base_level + 8]
+    last_block = from_above[size:]
     corner_above = turned_corner(last_block, merged, tiles, last)
     turn_above = (seam[0] == 1) & (place == last)
     flows_above = jnp.where(turn_above, crossed(last_block), last_block)
 
     def corner(r):
-        return both(opened[0, r : r + 1], corner_above[1 + r : 2 + r])
+        return both(opened[0, r : r + 1], corner_above[r : r + 1])
 
     def flow_of(j):
         r = 2 * tiles + j
-        return both(opened[0, r : r + 1], flows_above[1 + r : 2 + r])
+        return both(opened[0, r : r + 1], flows_above[r : r + 1])
 
     beside = (lane == 0) | (lane == LANES - 1)
 
@@ -690,7 +691,7 @@
     level_face = jnp.minimum(level_out, edge_level("own"))
     level_corner = both(
         opened[1],
-        jnp.minimum(rim(corner_above[1 + tiles : 2 + tiles], 8), edge_level("column")),
+        jnp.minimum(rim(corner_above[tiles : tiles + 1], 8), edge_level("column")),
     )
 
     bond_above = inverse = out_value = added = column_added = zero
@@ -699,11 +700,9 @@
         j, i = divmod(k, PER_TILE)
         block = slice(8 * k, 8 * k + 8)
         below_block, above_block = below[block], above[block]
-        bond_here = jnp.where(
-            level_out > k + 1.0,
-            0.5 * (outer(base_v, k) + outer(base_v, min(k + 1, depth - 1))),
-            0.0,
-        )
+        bond_here = zero
+        if k < depth - 1:
+            bond_here = jnp.where(level_out > k + 1.0, outer(base_bond, k), 0.0)
         inverse = pivot(bond_above, bond_here, inverse)
         out = both(below_block, roll(above_block, 4, 0))
         part = both(roll(below_block, 4, 0), above_block) + jnp.where(
@@ -822,7 +821,7 @@
 def per_device(tracers, costate, mixing_h, mixing_v, levels, seam_code):
     depth = tracers.shape[1]
     tiles = depth // PER_TILE
-    height = 10 * depth + 8
+    height = 10 * depth
     params = pltpu.CompilerParams(vmem_limit_bytes=48 * 2**20)
     smem = pl.BlockSpec(memory_space=pltpu.SMEM)
     vmem = pl.BlockSpec(memory_space=pltpu.VMEM)
@@ -873,7 +872,7 @@
     from_below = lax.ppermute(upper, "tx", upward)
     merged, corner, lower = call(
         pack_sides,
-        (vmem_out(2 * tiles, *tile), vmem_out(8, LANES), vmem_out(height, LANES)),
+        (vmem_out(2 * tiles, *tile), vmem_out(8, LANES), vmem_out(height + 8, LANES)),
         *(near, far, own, early),
     )
     corner_below = lax.ppermute(corner, "tx", upward)

time: 16 us -> 15.9 us (level)
  no operation moved by 1% of the time
where the time goes in v7:
time: 15.9 us; the launch traced here: 15.6 us
  starting transfers between devices  8.62 us (54%)
  Pallas kernels  5.29 us (33%)
  between operations  1.34 us (8%)
  waiting for transfers between devices  0.38 us (2%)
    ppermute x1, starting transfers between devices, per_device(): far = lax.ppermute(own, 'ty', far_pairs)  2.44 us
    pallas_call x5, Pallas kernels, call(): pl.pallas_call(body, out_shape=outs, compiler_params=params, name=body.__...  2.41 us
    ppermute x1, starting transfers between devices, per_device(): from_above = lax.ppermute(lower, 'tx', downward)  2.12 us
    ppermute x1, starting transfers between devices, per_device(): corner_below = lax.ppermute(corner, 'tx', upward)  1.75 us
    ppermute x1, starting transfers between devices, per_device(): from_below = lax.ppermute(upper, 'tx', upward)  1.63 us
    pallas_call x1, Pallas kernels, per_device(): pl.pallas_call(prepare, out_shape=(vmem_out(4 * depth * ROWS, LANES), vme...  1.43 us
    pallas_call x1, Pallas kernels, per_device(): pl.pallas_call(finish, out_shape=(jax.ShapeDtypeStruct(tracers.shape, jnp...  1.29 us
    ppermute x1, starting transfers between devices, per_device(): near = lax.ppermute(own, 'ty', near_pairs)  0.68 us
  transfers between devices with their start and end apart: 5, of which 1 were waited for; matrix products, arithmetic and copies ran while one was open for 0% of the time, Pallas kernels for 16%

profile of v7, /device:TPU:0, one launch (start us, length us, event | category | flops | bytes accessed | tf_op | source)
XLA Modules:
  0.0 15.6 jit_solution(13938529479888093377)
XLA Ops:
  1.3 1.4 %prepare.1 = (f32[1024,128]{1,0:T(8,128)S(1)}, f32[3,16,16,128]{3,2,1,0:T(8,128)S(1)}, f32[4,16,128]{2,1,0:T(8,128)S(1)}, f32[16,16,128]{2,1,0:T(8,128)S(1)}, f3...) custom-call(s32[1]{0:T(128)S(6)} %copy.9.seam, f32[512,128]{1,0:T(8,128)} %bitcast.2, f32[512,128]{1,0:T(8,128)} %bitcast.3, ...), custom_call_target="tpu_custom_call" | custom-call | tf_op jit(solution)/shard_map/prepare/pallas_call | solution.py:834
  2.7 2.4 %collective-permute-start.2 = (f32[4,16,128]{2,1,0:T(8,128)S(1)}, f32[4,16,128]{2,1,0:T(8,128)S(1)}, u32[]{:S(2)}, u32[]{:S(2)}) collective-permute-start(f32[4,16,128]{2,1,0:T(8,128)S(1)} %get-tuple-element.33.own), channel_id=1, source_target_pairs={{0,3},{1,2},{2,1},{3,0},{4,7},{5,6},{6,5},{7,4},{8,11},{9,10},{10,... | collective-permute-start | bytes 98312 | tf_op jit(solution)/shard_map/ppermute | solution.py:853
  5.2 0.7 %collective-permute-start.1 = (f32[4,16,128]{2,1,0:T(8,128)S(1)}, f32[4,16,128]{2,1,0:T(8,128)S(1)}, u32[]{:S(2)}, u32[]{:S(2)}) collective-permute-start(f32[4,16,128]{2,1,0:T(8,128)S(1)} %get-tuple-element.33.own), channel_id=1, source_target_pairs={{0,1},{1,0},{2,3},{3,2},{4,5},{5,4},{6,7},{7,6},{8,9},{9,8},{10,11... | collective-permute-start | bytes 98312 | tf_op jit(solution)/shard_map/ppermute | solution.py:854
  5.8 0.3 %pack_rows.1 = (f32[160,128]{1,0:T(8,128)S(1)}, f32[160,128]{1,0:T(8,128)S(1)}) custom-call(f32[1024,128]{1,0:T(8,128)S(1)} %get-tuple-element.28.fields, f32[16,16,128]{2,1,0:T(8,128)S(1)} %get-tuple-element.29.mix_h, f32[16,16,128]{2,1,0:T(8,128)S(1)} %get-tuple-element.30.mix_v, s32[16,128]{1,0:T(8,128)S(1)} %get-tuple-element.31.levels), custom_call_target="tpu_custom_call" | custom-call | tf_op jit(solution)/shard_map/pack_rows/pallas_call | solution.py:860
  6.1 1.6 %collective-permute-start = (f32[160,128]{1,0:T(8,128)S(1)}, f32[160,128]{1,0:T(8,128)S(1)}, u32[]{:S(2)}, u32[]{:S(2)}) collective-permute-start(f32[160,128]{1,0:T(8,128)S(1)} %get-tuple-element.32), channel_id=1, source_target_pairs={{0,4},{4,8},{8,12},{12,0},{1,5},{5,9},{9,13},{13,1},{2,6},{6,10},{... | collective-permute-start | bytes 245768 | tf_op jit(solution)/shard_map/ppermute | solution.py:872
  7.7 0.0 collective-permute-done.2.far
  7.7 0.0 collective-permute-done.1.near
  7.8 0.2 %pack_sides.1 = (f32[4,16,128]{2,1,0:T(8,128)S(1)}, f32[8,128]{1,0:T(8,128)S(1)}, f32[168,128]{1,0:T(8,128)S(1)}) custom-call(f32[4,16,128]{2,1,0:T(8,128)S(1)} %collective-permute-done.1.near, f32[4,16,128]{2,1,0:T(8,128)S(1)} %collective-permute-done.2.far, f32[4,16,128]{2,1,0:T(8,128)S(1)} %get-tuple-element.33.own, f32[160,128]{1,0:T(8,128)S(1)} %get-tuple-element.34.early), custom_call_target="tpu_custom_call" | custom-call | tf_op jit(solution)/shard_map/pack_sides/pallas_call | solution.py:860
  8.0 1.8 %collective-permute-start.4 = (f32[8,128]{1,0:T(8,128)S(1)}, f32[8,128]{1,0:T(8,128)S(1)}, u32[]{:S(2)}, u32[]{:S(2)}) collective-permute-start(f32[8,128]{1,0:T(8,128)S(1)} %get-tuple-element.36), channel_id=1, source_target_pairs={{0,4},{4,8},{8,12},{12,0},{1,5},{5,9},{9,13},{13,1},{2,6},{6,10},{... | collective-permute-start | bytes 12296 | tf_op jit(solution)/shard_map/ppermute | solution.py:878
  9.7 2.1 %collective-permute-start.3 = (f32[168,128]{1,0:T(8,128)S(1)}, f32[168,128]{1,0:T(8,128)S(1)}, u32[]{:S(2)}, u32[]{:S(2)}) collective-permute-start(f32[168,128]{1,0:T(8,128)S(1)} %get-tuple-element.35.sent), channel_id=1, source_target_pairs={{0,12},{4,0},{8,4},{12,8},{1,13},{5,1},{9,5},{13,9},{2,14},{6,2},{... | collective-permute-start | bytes 258056 | tf_op jit(solution)/shard_map/ppermute | solution.py:879
  11.8 0.8 %interior_down.1 = (f32[16,64,128]{2,1,0:T(8,128)S(1)}, f32[16,4,4,16,128]{4,3,2,1,0:T(8,128)S(1)}, f32[16,4,16,128]{3,2,1,0:T(8,128)S(1)}, f32[16,16,128]{2,1,0...) custom-call(f32[4,16,128]{2,1,0:T(8,128)S(1)} %get-tuple-element.37.merged,, ...), custom_call_target="tpu_custom_call" | custom-call | flops 30000000 | bytes 30000000 | tf_op jit(solution)/shard_map/interior_down/pallas_call | solution.py:860
  12.7 0.6 %interior_up.1 = (f32[16,64,128]{2,1,0:T(8,128)S(1)}, f32[16,64,128]{2,1,0:T(8,128)S(1)}, f32[2,16,16,128]{3,2,1,0:T(8,128)S(1)}, f32[16,16,128]{2,1,0:T(8,128)S(1)}) custom-call(f32[16,64,128]{2,1,0:T(8,128)S(1)} %get-tuple-element.39.inside_in, f32[16,4,4,16,128]{4,3,2,1,0:T(8,128)S(1)} %get-tuple-element.40.steps, ...), custom_call_target="tpu_custom_call" | custom-call | flops 30000000 | bytes 30000000 | tf_op jit(solution)/shard_map/interior_up/pallas_call | solution.py:860
  13.3 0.5 %interior_edges.1 = (f32[30,16,8,128]{3,2,1,0:T(8,128)S(1)}, f32[6,8,128]{2,1,0:T(8,128)S(1)}, f32[16,16,128]{2,1,0:T(8,128)S(1)}) custom-call(f32[4,16,128]{2,1,0:T(8,128)S(1)} %get-tuple-element.37.merged, f32[1024,128]{1,0:T(8,128)S(1)} %get-tuple-element.28.fields, f32[3,16,16,128]{3,2,1,0:T(8,128)S(1)} %get-tuple-element.38.factors, ...), custom_call_target="tpu_custom_call" | custom-call | flops 40000000 | bytes 40000000 | tf_op jit(solution)/shard_map/interior_edges/pallas_call | solution.py:860
  13.8 0.0 collective-permute-done.4.corner
  13.8 0.2 open_below.1.opened
  14.0 0.0 collective-permute-done.from_below
  14.0 0.4 %collective-permute-done.3.from_above = f32[168,128]{1,0:T(8,128)S(1)} collective-permute-done((f32[168,128]{1,0:T(8,128)S(1)}, f32[168,128]{1,0:T(8,128)S(1)}, u32[]{:S(2)}, u32[]{:S(2)}) %collective-permute-start.3) | collective-permute-done | bytes 86048 | tf_op jit(solution)/shard_map/ppermute | solution.py:879
  14.3 1.3 %finish.1 = (f32[2,16,16,128]{3,2,1,0:T(8,128)}, f32[16,16,128]{2,1,0:T(8,128)}, f32[16,16,128]{2,1,0:T(8,128)}) custom-call(s32[1]{0:T(128)S(6)} %copy.9.seam, f32[160,128]{1,0:T(8,128)S(1)} %collective-permute-done.from_below, f32[168,128]{1,0:T(8,128)S(1)} %collective-permute-done.3.from_above, f32[2,8,128]{2,1,0:T(8,128)S(1)} %open_below.1.opened, ...), custom_call_target="tpu_custom_call" | custom-call | tf_op jit(solution)/shard_map/finish/pallas_call | solution.py:929
Async XLA Ops:
  2.7 5.0 %collective-permute-start.2 = (f32[4,16,128]{2,1,0:T(8,128)S(1)}, f32[4,16,128]{2,1,0:T(8,128)S(1)}, u32[]{:S(2)}, u32[]{:S(2)}) collective-permute-start(f32[4,16,128]{2,1,0:T(8,128)S(1)} %get-tuple-element.33.own), channel_id=1, source_target_pairs={{0,3},{1,2},{2,1},{3,0},{4,7},{5,6},{6,5},{7,4},{8,11},{9,10},{10,... | collective-permute-start | bytes 98312 | tf_op jit(solution)/shard_map/ppermute | solution.py:853
  5.2 2.6 %collective-permute-start.1 = (f32[4,16,128]{2,1,0:T(8,128)S(1)}, f32[4,16,128]{2,1,0:T(8,128)S(1)}, u32[]{:S(2)}, u32[]{:S(2)}) collective-permute-start(f32[4,16,128]{2,1,0:T(8,128)S(1)} %get-tuple-element.33.own), channel_id=1, source_target_pairs={{0,1},{1,0},{2,3},{3,2},{4,5},{5,4},{6,7},{7,6},{8,9},{9,8},{10,11... | collective-permute-start | bytes 98312 | tf_op jit(solution)/shard_map/ppermute | solution.py:854
  6.1 7.9 %collective-permute-start = (f32[160,128]{1,0:T(8,128)S(1)}, f32[160,128]{1,0:T(8,128)S(1)}, u32[]{:S(2)}, u32[]{:S(2)}) collective-permute-start(f32[160,128]{1,0:T(8,128)S(1)} %get-tuple-element.32), channel_id=1, source_target_pairs={{0,4},{4,8},{8,12},{12,0},{1,5},{5,9},{9,13},{13,1},{2,6},{6,10},{... | collective-permute-start | bytes 245768 | tf_op jit(solution)/shard_map/ppermute | solution.py:872
  8.0 5.8 %collective-permute-start.4 = (f32[8,128]{1,0:T(8,128)S(1)}, f32[8,128]{1,0:T(8,128)S(1)}, u32[]{:S(2)}, u32[]{:S(2)}) collective-permute-start(f32[8,128]{1,0:T(8,128)S(1)} %get-tuple-element.36), channel_id=1, source_target_pairs={{0,4},{4,8},{8,12},{12,0},{1,5},{5,9},{9,13},{13,1},{2,6},{6,10},{... | collective-permute-start | bytes 12296 | tf_op jit(solution)/shard_map/ppermute | solution.py:878
  9.7 4.6 %collective-permute-start.3 = (f32[168,128]{1,0:T(8,128)S(1)}, f32[168,128]{1,0:T(8,128)S(1)}, u32[]{:S(2)}, u32[]{:S(2)}) collective-permute-start(f32[168,128]{1,0:T(8,128)S(1)} %get-tuple-element.35.sent), channel_id=1, source_target_pairs={{0,12},{4,0},{8,4},{12,8},{1,13},{5,1},{9,5},{13,9},{2,14},{6,2},{... | collective-permute-start | bytes 258056 | tf_op jit(solution)/shard_map/ppermute | solution.py:879

commit v8 on v7

--- a/solution.py
+++ b/solution.py
@@ -55,6 +55,10 @@
     return jnp.where(
         column == 1, roll(tile, -1, 1), jnp.where(column == 2, roll(tile, 1, 1), tile)
     )
+
+
+def lane_of(i, q):
+    return GROUP * i + 4 * (3 - q)
 
 
 def tile_of(q, k, depth):
@@ -145,7 +149,7 @@
     firsts = [zero] * tiles
 
     def add(k, q, value):
-        tile, base = k // PER_TILE, GROUP * (k % PER_TILE) + 4 * q
+        tile, base = k // PER_TILE, lane_of(k % PER_TILE, q)
         firsts[tile] = jnp.where(place == base // 4, roll(value, base + 2, 1), firsts[tile])
 
     for copy in copies[2:4]:
@@ -314,12 +318,12 @@
     return jnp.where(iota(8, 0) % 4 < 2, roll(value, -2, 0), roll(value, 2, 0))
 
 
-def at_edges(rows, shift):
-    sub = iota(8, 0) % 4
-    out = roll(rows, LANES - 2 - shift, 1)
-    for q in range(1, 4):
-        out = jnp.where(sub == q, roll(rows, LANES - 2 - shift - 4 * q, 1), out)
-    return jnp.broadcast_to(out, (8, LANES))
+def at_edges(low, high, i):
+    rows = both(low, roll(high, -GROUP, 1))
+    shift = LANES - 2 - lane_of(i, 0)
+    if i == 0:
+        rows, shift = roll(rows, LANES // 2, 1), shift - LANES // 2
+    return pltpu.roll(rows, shift % LANES, 1, stride=4, stride_axis=0)
 
 
 def stacked(*rows):
@@ -432,7 +436,7 @@
             weights[k, n] = weight[n]
         for q in range(4):
             value = fields[tile_of(q, k, depth)]
-            step = [near - value for near in nears_of(value, rim(merged[j], GROUP * i + 4 * q))]
+            step = [near - value for near in nears_of(value, rim(merged[j], lane_of(i, q)))]
             for n in range(4):
                 steps[k, q, n] = step[n]
                 value = value + weight[n] * step[n]
@@ -467,7 +471,7 @@
             value = inside_in[k, at(q)] + factors[2, k] * values[q]
             inside[k, at(q)] = value
             values[q] = value
-            step = [near - value for near in nears_of(value, rim(col_value, 4 * q))]
+            step = [near - value for near in nears_of(value, rim(col_value, lane_of(0, q)))]
             later_steps.append(step)
             for n in range(4):
                 value = value + weights[k, n] * step[n]
@@ -557,7 +561,7 @@
         j, i = divmod(k, PER_TILE)
         field = four(fields, k * ROWS, depth * ROWS)
         field_1 = four(fields, k * ROWS, depth * ROWS, 1)
-        column = at_edges(ends(merged[j]), GROUP * i)
+        column = at_edges(merged[j, :1], merged[j, ROWS - 1 :], i)
         things = dict(
             field=field,
             mix=ends(mix_h[k]),
@@ -611,9 +615,29 @@
     )
 
 
+def turn_rows(seam, border, source, target):
+    turn = (seam[0] == 1) & (lax.axis_index("tx") == border)
+    size = target.shape[0]
+
+    @pl.when(turn)
+    def _():
+        back = LANES - 1 - iota(8, 1)
+        for r in range(0, size, 8):
+            target[r : r + 8] = jnp.take_along_axis(source[r : r + 8], back, axis=1)
+
+    @pl.when(jnp.logical_not(turn))
+    def _():
+        for r in range(0, size, 8):
+            target[r : r + 8] = source[r : r + 8]
+
+
+def turn_below(seam, from_below, below):
+    turn_rows(seam, 0, from_below, below)
+
+
 def finish(
     seam,
-    from_below,
+    below,
     from_above,
     opened,
     merged,
@@ -625,13 +649,12 @@
     adjoint_out,
     grad_h_out,
     grad_v_out,
-    below,
+    adjoint,
+    grad_h,
+    grad_v,
     above,
     rows,
     later,
-    adjoint,
-    grad_h,
-    grad_v,
     sems,
 ):
     depth, tiles = grad_h.shape[0], grad_h.shape[0] // PER_TILE
@@ -649,25 +672,7 @@
     def edge_level(name):
         return edge_levels[EDGE_LEVELS.index(name)]
 
-    for source, target, border in ((from_below, below, 0), (from_above, above, last)):
-        turn = (seam[0] == 1) & (place == border)
-
-        @pl.when(turn)
-        def _():
-            back = LANES - 1 - lane
-            for r in range(0, size, 8):
-                target[r : r + 8] = jnp.take_along_axis(source[r : r + 8], back, axis=1)
-
-        @pl.when(jnp.logical_not(turn))
-        def _():
-            for r in range(0, size, 8):
-                target[r : r + 8] = source[r : r + 8]
-
-    for k in range(depth):
-        for t in range(2):
-            adjoint[t, k] = adjoint_in[t, k]
-        grad_h[k] = grad_h_in[k]
-        grad_v[k] = grad_v_in[k]
+    turn_rows(seam, last, from_above, above)
 
     last_block = from_above[size:]
     corner_above = turned_corner(last_block, merged, tiles, last)
@@ -675,11 +680,11 @@
     flows_above = jnp.where(turn_above, crossed(last_block), last_block)
 
     def corner(r):
-        return both(opened[0, r : r + 1], corner_above[r : r + 1])
+        return opened[0, r : r + 1], corner_above[r : r + 1]
 
     def flow_of(j):
         r = 2 * tiles + j
-        return both(opened[0, r : r + 1], flows_above[r : r + 1])
+        return opened[0, r : r + 1], flows_above[r : r + 1]
 
     beside = (lane == 0) | (lane == LANES - 1)
 
@@ -706,18 +711,18 @@
         inverse = pivot(bond_above, bond_here, inverse)
         out = both(below_block, roll(above_block, 4, 0))
         part = both(roll(below_block, 4, 0), above_block) + jnp.where(
-            beside, at_edges(flow_of(j), GROUP * i), 0.0
+            beside, at_edges(*flow_of(j), i), 0.0
         )
         step = out - edge("field", k)
         weight = jnp.where(level_face > float(k), 0.5 * (outer(base_mix, k) + edge("mix", k)), 0.0)
         flow = weight * step
         out_value = (part - flow) * inverse + bond_above * inverse * out_value
         added = flow * edge("inv_down", k) + edge("up_down", k) * added
-        mix_corner = rim(corner(tiles + j), GROUP * i)
+        mix_corner = rim(both(*corner(tiles + j)), GROUP * i)
         weight_corner = jnp.where(
             level_corner > float(k), 0.5 * (mix_corner + edge("mix_column", k)), 0.0
         )
-        step_corner = at_edges(corner(j), GROUP * i) - edge("column", k)
+        step_corner = at_edges(*corner(j), i) - edge("column", k)
         column_added = (
             weight_corner * step_corner * edge("inv_column", k)
             + edge("up_column", k) * column_added
@@ -729,6 +734,12 @@
         rows[4, k] = weight
         rows[5, k] = exchange(step)
         bond_above = bond_here
+
+    copies = []
+
+    def send(source, target):
+        copies.append(pltpu.make_async_copy(source, target, sems.at[len(copies)]))
+        copies[-1].start()
 
     out_value = added = column_added = later_0 = later_1 = zero
     for k in range(depth - 1, -1, -1):
@@ -776,15 +787,11 @@
             value = edge(name, k) - 0.5 * (value + roll(value, -2, 0))
             grad_h[k, inset : inset + 1] = value[:1]
             grad_h[k, ROWS - 1 - inset : ROWS - inset] = value[4:5]
-
-    copies = [
-        pltpu.make_async_copy(source, target, sems.at[n])
-        for n, (source, target) in enumerate(
-            ((adjoint, adjoint_out), (grad_h, grad_h_out), (grad_v, grad_v_out))
-        )
-    ]
-    copies[0].start()
-    copies[1].start()
+        if k in (0, depth // 2):
+            part = slice(k, k + depth // 2)
+            send(adjoint.at[:, part], adjoint_out.at[:, part])
+            send(grad_h.at[part], grad_h_out.at[part])
+
 
     face_0 = face_1 = later_0 = later_1 = zero
     for k in range(depth + 1):
@@ -813,7 +820,7 @@
             grad_v[k - 1, inset : inset + 1] = value[:1]
             grad_v[k - 1, ROWS - 1 - inset : ROWS - inset] = value[4:5]
         face_0, face_1 = next_0, next_1
-    copies[2].start()
+    send(grad_v, grad_v_out)
     for copy in copies:
         copy.wait()
 
@@ -925,25 +932,36 @@
         cost_estimate=cost(900_000_000),
         name="open_below",
     )(seam_code, *(in_vmem(a) for a in (corner_below, merged, inner[1])))
+    below = pl.pallas_call(
+        turn_below,
+        out_shape=vmem_out(height, LANES),
+        in_specs=[smem, vmem],
+        compiler_params=params,
+        name="turn_below",
+    )(seam_code, in_vmem(from_below))
     block = jax.ShapeDtypeStruct(mixing_h.shape, jnp.float32)
     return pl.pallas_call(
         finish,
-        out_shape=(jax.ShapeDtypeStruct(tracers.shape, jnp.float32), block, block),
+        out_shape=(
+            jax.ShapeDtypeStruct(tracers.shape, jnp.float32),
+            block,
+            block,
+            vmem_out(2, depth, *tile),
+            vmem_out(depth, *tile),
+            vmem_out(depth, *tile),
+        ),
+        input_output_aliases={7: 3, 8: 4, 9: 5},
         in_specs=[smem] + [vmem] * 9,
-        out_specs=(hbm, hbm, hbm),
+        out_specs=(hbm, hbm, hbm, vmem, vmem, vmem),
         scratch_shapes=[
-            vmem_out(height, LANES),
             vmem_out(height, LANES),
             vmem_out(6, *row_block),
             vmem_out(2, *row_block),
-            vmem_out(2, depth, *tile),
-            vmem_out(depth, *tile),
-            vmem_out(depth, *tile),
-            pltpu.SemaphoreType.DMA((3,)),
+            pltpu.SemaphoreType.DMA((5,)),
         ],
         compiler_params=params,
         name="finish",
-    )(seam_code, *(in_vmem(a) for a in (from_below, from_above, opened, merged, *inner)))
+    )(seam_code, *(in_vmem(a) for a in (below, from_above, opened, merged, *inner)))[:3]
 
 
 def solution(mesh):

time: 15.9 us -> 15.8 us (level)
  transfers between devices with their start and end apart: 5 -> 5, of which waited for: 1 -> 1; matrix products, arithmetic and copies ran while one was open for 0% -> 0% of each run, Pallas kernels for 16% -> 17%
where the time goes in v8:
time: 15.8 us; the launch traced here: 15.6 us
  starting transfers between devices  8.62 us (55%)
  Pallas kernels  5.28 us (33%)
  between operations  1.35 us (9%)
  waiting for transfers between devices  0.33 us (2%)
    pallas_call x5, Pallas kernels, call(): pl.pallas_call(body, out_shape=outs, compiler_params=params, name=body.__...  2.45 us
    ppermute x1, starting transfers between devices, per_device(): far = lax.ppermute(own, 'ty', far_pairs)  2.44 us
    ppermute x1, starting transfers between devices, per_device(): from_above = lax.ppermute(lower, 'tx', downward)  2.12 us
    ppermute x1, starting transfers between devices, per_device(): corner_below = lax.ppermute(corner, 'tx', upward)  1.75 us
    ppermute x1, starting transfers between devices, per_device(): from_below = lax.ppermute(upper, 'tx', upward)  1.63 us
    pallas_call x1, Pallas kernels, per_device(): pl.pallas_call(prepare, out_shape=(vmem_out(4 * depth * ROWS, LANES), vme...  1.43 us
    pallas_call x1, Pallas kernels, per_device(): pl.pallas_call(finish, out_shape=(jax.ShapeDtypeStruct(tracers.shape, jnp...  1.23 us
    ppermute x1, starting transfers between devices, per_device(): near = lax.ppermute(own, 'ty', near_pairs)  0.68 us
  transfers between devices with their start and end apart: 5, of which 1 were waited for; matrix products, arithmetic and copies ran while one was open for 0% of the time, Pallas kernels for 17%

profile of v8, /device:TPU:0, one launch (start us, length us, event | category | flops | bytes accessed | tf_op | source)
XLA Modules:
  0.0 15.6 jit_solution(8118594824986761821)
XLA Ops:
  1.3 1.4 %prepare.1 = (f32[1024,128]{1,0:T(8,128)S(1)}, f32[3,16,16,128]{3,2,1,0:T(8,128)S(1)}, f32[4,16,128]{2,1,0:T(8,128)S(1)}, f32[16,16,128]{2,1,0:T(8,128)S(1)}, f3...) custom-call(s32[1]{0:T(128)S(6)} %copy.15.seam, f32[512,128]{1,0:T(8,128)} %bitcast.2, f32[512,128]{1,0:T(8,128)} %bitcast.3, ...), custom_call_target="tpu_custom_call" | custom-call | tf_op jit(solution)/shard_map/prepare/pallas_call | solution.py:841
  2.7 2.4 %collective-permute-start.2 = (f32[4,16,128]{2,1,0:T(8,128)S(1)}, f32[4,16,128]{2,1,0:T(8,128)S(1)}, u32[]{:S(2)}, u32[]{:S(2)}) collective-permute-start(f32[4,16,128]{2,1,0:T(8,128)S(1)} %get-tuple-element.36.own), channel_id=1, source_target_pairs={{0,3},{1,2},{2,1},{3,0},{4,7},{5,6},{6,5},{7,4},{8,11},{9,10},{10,... | collective-permute-start | bytes 98312 | tf_op jit(solution)/shard_map/ppermute | solution.py:860
  5.2 0.7 %collective-permute-start.1 = (f32[4,16,128]{2,1,0:T(8,128)S(1)}, f32[4,16,128]{2,1,0:T(8,128)S(1)}, u32[]{:S(2)}, u32[]{:S(2)}) collective-permute-start(f32[4,16,128]{2,1,0:T(8,128)S(1)} %get-tuple-element.36.own), channel_id=1, source_target_pairs={{0,1},{1,0},{2,3},{3,2},{4,5},{5,4},{6,7},{7,6},{8,9},{9,8},{10,11... | collective-permute-start | bytes 98312 | tf_op jit(solution)/shard_map/ppermute | solution.py:861
  5.8 0.3 %pack_rows.1 = (f32[160,128]{1,0:T(8,128)S(1)}, f32[160,128]{1,0:T(8,128)S(1)}) custom-call(f32[1024,128]{1,0:T(8,128)S(1)} %get-tuple-element.31.fields, f32[16,16,128]{2,1,0:T(8,128)S(1)} %get-tuple-element.32.mix_h, f32[16,16,128]{2,1,0:T(8,128)S(1)} %get-tuple-element.33.mix_v, s32[16,128]{1,0:T(8,128)S(1)} %get-tuple-element.34.levels), custom_call_target="tpu_custom_call" | custom-call | tf_op jit(solution)/shard_map/pack_rows/pallas_call | solution.py:867
  6.1 1.6 %collective-permute-start = (f32[160,128]{1,0:T(8,128)S(1)}, f32[160,128]{1,0:T(8,128)S(1)}, u32[]{:S(2)}, u32[]{:S(2)}) collective-permute-start(f32[160,128]{1,0:T(8,128)S(1)} %get-tuple-element.35), channel_id=1, source_target_pairs={{0,4},{4,8},{8,12},{12,0},{1,5},{5,9},{9,13},{13,1},{2,6},{6,10},{... | collective-permute-start | bytes 245768 | tf_op jit(solution)/shard_map/ppermute | solution.py:879
  7.7 0.0 collective-permute-done.2.far
  7.7 0.0 collective-permute-done.1.near
  7.8 0.2 %pack_sides.1 = (f32[4,16,128]{2,1,0:T(8,128)S(1)}, f32[8,128]{1,0:T(8,128)S(1)}, f32[168,128]{1,0:T(8,128)S(1)}) custom-call(f32[4,16,128]{2,1,0:T(8,128)S(1)} %collective-permute-done.1.near, f32[4,16,128]{2,1,0:T(8,128)S(1)} %collective-permute-done.2.far, f32[4,16,128]{2,1,0:T(8,128)S(1)} %get-tuple-element.36.own, f32[160,128]{1,0:T(8,128)S(1)} %get-tuple-element.37.early), custom_call_target="tpu_custom_call" | custom-call | tf_op jit(solution)/shard_map/pack_sides/pallas_call | solution.py:867
  8.0 1.8 %collective-permute-start.4 = (f32[8,128]{1,0:T(8,128)S(1)}, f32[8,128]{1,0:T(8,128)S(1)}, u32[]{:S(2)}, u32[]{:S(2)}) collective-permute-start(f32[8,128]{1,0:T(8,128)S(1)} %get-tuple-element.39), channel_id=1, source_target_pairs={{0,4},{4,8},{8,12},{12,0},{1,5},{5,9},{9,13},{13,1},{2,6},{6,10},{... | collective-permute-start | bytes 12296 | tf_op jit(solution)/shard_map/ppermute | solution.py:885
  9.7 2.1 %collective-permute-start.3 = (f32[168,128]{1,0:T(8,128)S(1)}, f32[168,128]{1,0:T(8,128)S(1)}, u32[]{:S(2)}, u32[]{:S(2)}) collective-permute-start(f32[168,128]{1,0:T(8,128)S(1)} %get-tuple-element.38.sent), channel_id=1, source_target_pairs={{0,12},{4,0},{8,4},{12,8},{1,13},{5,1},{9,5},{13,9},{2,14},{6,2},{... | collective-permute-start | bytes 258056 | tf_op jit(solution)/shard_map/ppermute | solution.py:886
  11.8 0.8 %interior_down.1 = (f32[16,64,128]{2,1,0:T(8,128)S(1)}, f32[16,4,4,16,128]{4,3,2,1,0:T(8,128)S(1)}, f32[16,4,16,128]{3,2,1,0:T(8,128)S(1)}, f32[16,16,128]{2,1,0...) custom-call(f32[4,16,128]{2,1,0:T(8,128)S(1)} %get-tuple-element.40.merged,, ...), custom_call_target="tpu_custom_call" | custom-call | flops 30000000 | bytes 30000000 | tf_op jit(solution)/shard_map/interior_down/pallas_call | solution.py:867
  12.7 0.6 %interior_up.1 = (f32[16,64,128]{2,1,0:T(8,128)S(1)}, f32[16,64,128]{2,1,0:T(8,128)S(1)}, f32[2,16,16,128]{3,2,1,0:T(8,128)S(1)}, f32[16,16,128]{2,1,0:T(8,128)S(1)}) custom-call(f32[16,64,128]{2,1,0:T(8,128)S(1)} %get-tuple-element.42.inside_in, f32[16,4,4,16,128]{4,3,2,1,0:T(8,128)S(1)} %get-tuple-element.43.steps, ...), custom_call_target="tpu_custom_call" | custom-call | flops 30000000 | bytes 30000000 | tf_op jit(solution)/shard_map/interior_up/pallas_call | solution.py:867
  13.3 0.5 %interior_edges.1 = (f32[30,16,8,128]{3,2,1,0:T(8,128)S(1)}, f32[6,8,128]{2,1,0:T(8,128)S(1)}, f32[16,16,128]{2,1,0:T(8,128)S(1)}) custom-call(f32[4,16,128]{2,1,0:T(8,128)S(1)} %get-tuple-element.40.merged, f32[1024,128]{1,0:T(8,128)S(1)} %get-tuple-element.31.fields, f32[3,16,16,128]{3,2,1,0:T(8,128)S(1)} %get-tuple-element.41.factors, ...), custom_call_target="tpu_custom_call" | custom-call | flops 40000000 | bytes 40000000 | tf_op jit(solution)/shard_map/interior_edges/pallas_call | solution.py:867
  13.8 0.0 collective-permute-done.4.corner
  13.8 0.2 open_below.1.opened
  14.0 0.0 collective-permute-done.from_below
  14.0 0.3 %collective-permute-done.3.from_above = f32[168,128]{1,0:T(8,128)S(1)} collective-permute-done((f32[168,128]{1,0:T(8,128)S(1)}, f32[168,128]{1,0:T(8,128)S(1)}, u32[]{:S(2)}, u32[]{:S(2)}) %collective-permute-start.3) | collective-permute-done | bytes 86048 | tf_op jit(solution)/shard_map/ppermute | solution.py:886
  14.3 1.2 %finish.1 = (f32[2,16,16,128]{3,2,1,0:T(8,128)}, f32[16,16,128]{2,1,0:T(8,128)}, f32[16,16,128]{2,1,0:T(8,128)}, f32[2,16,16,128]{3,2,1,0:T(8,128)S(1)}, f32[16,...) custom-call(s32[1]{0:T(128)S(6)} %copy.15.seam, ...), custom_call_target="tpu_custom_call", output_to_operand_aliasing={{3}: (7, {}), {4}: (8, {}), {5}: (9, {})} | custom-call | tf_op jit(solution)/shard_map/finish/pallas_call | solution.py:943
  (1 shorter events, 0.0 us)
Async XLA Ops:
  2.7 5.0 %collective-permute-start.2 = (f32[4,16,128]{2,1,0:T(8,128)S(1)}, f32[4,16,128]{2,1,0:T(8,128)S(1)}, u32[]{:S(2)}, u32[]{:S(2)}) collective-permute-start(f32[4,16,128]{2,1,0:T(8,128)S(1)} %get-tuple-element.36.own), channel_id=1, source_target_pairs={{0,3},{1,2},{2,1},{3,0},{4,7},{5,6},{6,5},{7,4},{8,11},{9,10},{10,... | collective-permute-start | bytes 98312 | tf_op jit(solution)/shard_map/ppermute | solution.py:860
  5.2 2.6 %collective-permute-start.1 = (f32[4,16,128]{2,1,0:T(8,128)S(1)}, f32[4,16,128]{2,1,0:T(8,128)S(1)}, u32[]{:S(2)}, u32[]{:S(2)}) collective-permute-start(f32[4,16,128]{2,1,0:T(8,128)S(1)} %get-tuple-element.36.own), channel_id=1, source_target_pairs={{0,1},{1,0},{2,3},{3,2},{4,5},{5,4},{6,7},{7,6},{8,9},{9,8},{10,11... | collective-permute-start | bytes 98312 | tf_op jit(solution)/shard_map/ppermute | solution.py:861
  6.1 7.9 %collective-permute-start = (f32[160,128]{1,0:T(8,128)S(1)}, f32[160,128]{1,0:T(8,128)S(1)}, u32[]{:S(2)}, u32[]{:S(2)}) collective-permute-start(f32[160,128]{1,0:T(8,128)S(1)} %get-tuple-element.35), channel_id=1, source_target_pairs={{0,4},{4,8},{8,12},{12,0},{1,5},{5,9},{9,13},{13,1},{2,6},{6,10},{... | collective-permute-start | bytes 245768 | tf_op jit(solution)/shard_map/ppermute | solution.py:879
  8.0 5.9 %collective-permute-start.4 = (f32[8,128]{1,0:T(8,128)S(1)}, f32[8,128]{1,0:T(8,128)S(1)}, u32[]{:S(2)}, u32[]{:S(2)}) collective-permute-start(f32[8,128]{1,0:T(8,128)S(1)} %get-tuple-element.39), channel_id=1, source_target_pairs={{0,4},{4,8},{8,12},{12,0},{1,5},{5,9},{9,13},{13,1},{2,6},{6,10},{... | collective-permute-start | bytes 12296 | tf_op jit(solution)/shard_map/ppermute | solution.py:885
  9.7 4.6 %collective-permute-start.3 = (f32[168,128]{1,0:T(8,128)S(1)}, f32[168,128]{1,0:T(8,128)S(1)}, u32[]{:S(2)}, u32[]{:S(2)}) collective-permute-start(f32[168,128]{1,0:T(8,128)S(1)} %get-tuple-element.38.sent), channel_id=1, source_target_pairs={{0,12},{4,0},{8,4},{12,8},{1,13},{5,1},{9,5},{13,9},{2,14},{6,2},{... | collective-permute-start | bytes 258056 | tf_op jit(solution)/shard_map/ppermute | solution.py:886

commit v9 on v8

--- a/solution.py
+++ b/solution.py
@@ -180,32 +180,34 @@
 
 def pack_rows(fields, mix_h, mix_v, levels, lower, upper):
     depth = mix_h.shape[0]
-    sub = iota(8, 0)
-
-    def nears(value):
-        inner = jnp.where(sub < 4, roll(value, -1, 0), roll(value, 1, 0))
+
+    def four(k, inset):
+        low, high = [
+            fields[pl.ds(k * ROWS + row, 4, stride=depth * ROWS)]
+            for row in (inset, ROWS - 1 - inset)
+        ]
+        return jnp.concatenate([low, high], axis=0)
+
+    def ends(ref, inset):
+        return both(ref[inset : inset + 1], ref[ROWS - 1 - inset : ROWS - inset])
+
+    def nears(value, inner):
         return east(value, 0.0), west(value, 0.0), inner
 
-    level = fold(levels[...].astype(jnp.float32))
-    shallow = [jnp.minimum(level, near) for near in nears(level)]
+    depths = levels[...].astype(jnp.float32)
+    level = ends(depths, 0)
+    shallow = [jnp.minimum(level, near) for near in nears(level, ends(depths, 1))]
     for k in range(depth):
-        mix = fold(mix_h[k])
-        weights = [
-            jnp.where(open_to > float(k), 0.5 * (mix + near), 0.0)
-            for open_to, near in zip(shallow, nears(mix))
-        ]
-        low = jnp.zeros((8, LANES), jnp.float32)
-        high = low
-        for q in range(4):
-            value = fold(fields[tile_of(q, k, depth)])
-            part = value
-            for near, weight in zip(nears(value), weights):
-                part = part + weight * (near - value)
-            for n, thing in ((q, value), (4 + q, part)):
-                low = jnp.where(sub == n, roll(thing, n, 0), low)
-                high = jnp.where(sub == n, roll(thing, n - 7, 0), high)
-        lower[8 * k : 8 * k + 8] = low
-        upper[8 * k : 8 * k + 8] = high
+        mix = ends(mix_h.at[k], 0)
+        value = four(k, 0)
+        part = value
+        for open_to, near_mix, near in zip(
+            shallow, nears(mix, ends(mix_h.at[k], 1)), nears(value, four(k, 1))
+        ):
+            weight = jnp.where(open_to > float(k), 0.5 * (mix + near_mix), 0.0)
+            part = part + weight * (near - value)
+        lower[8 * k : 8 * k + 8] = both(value, roll(part, 4, 0))
+        upper[8 * k : 8 * k + 8] = both(roll(value, 4, 0), part)
         at_mix = slice(8 * depth + k, 8 * depth + k + 1)
         lower[at_mix] = mix_h[k, :1]
         upper[at_mix] = mix_h[k, ROWS - 1 :]
@@ -214,8 +216,8 @@
             at_bond = slice(9 * depth + k, 9 * depth + k + 1)
             lower[at_bond] = between[:1]
             upper[at_bond] = between[ROWS - 1 :]
-    lower[10 * depth - 1 :] = level[:1]
-    upper[10 * depth - 1 :] = level[7:]
+    lower[10 * depth - 1 :] = depths[:1]
+    upper[10 * depth - 1 :] = depths[ROWS - 1 :]
 
 
 def pack_sides(near, far, own, early, merged, corner, lower):

time: 15.8 us -> 15.7 us (level)
  no operation moved by 1% of the time
where the time goes in v9:
time: 15.7 us; the launch traced here: 15.5 us
  starting transfers between devices  8.69 us (55%)
  Pallas kernels  5.26 us (34%)
  between operations  1.35 us (9%)
  waiting for transfers between devices  0.18 us (1%)
    ppermute x1, starting transfers between devices, per_device(): far = lax.ppermute(own, 'ty', far_pairs)  2.44 us
    pallas_call x5, Pallas kernels, call(): pl.pallas_call(body, out_shape=outs, compiler_params=params, name=body.__...  2.35 us
    ppermute x1, starting transfers between devices, per_device(): from_above = lax.ppermute(lower, 'tx', downward)  2.09 us
    ppermute x1, starting transfers between devices, per_device(): corner_below = lax.ppermute(corner, 'tx', upward)  1.85 us
    ppermute x1, starting transfers between devices, per_device(): from_below = lax.ppermute(upper, 'tx', upward)  1.63 us
    pallas_call x1, Pallas kernels, per_device(): pl.pallas_call(prepare, out_shape=(vmem_out(4 * depth * ROWS, LANES), vme...  1.43 us
    pallas_call x1, Pallas kernels, per_device(): pl.pallas_call(finish, out_shape=(jax.ShapeDtypeStruct(tracers.shape, jnp...  1.23 us
    ppermute x1, starting transfers between devices, per_device(): near = lax.ppermute(own, 'ty', near_pairs)  0.68 us
  transfers between devices with their start and end apart: 5, of which 1 were waited for; matrix products, arithmetic and copies ran while one was open for 0% of the time, Pallas kernels for 17%

profile of v9, /device:TPU:0, one launch (start us, length us, event | category | flops | bytes accessed | tf_op | source)
XLA Modules:
  0.0 15.5 jit_solution(18260920665795251455)
XLA Ops:
  1.3 1.4 %prepare.1 = (f32[1024,128]{1,0:T(8,128)S(1)}, f32[3,16,16,128]{3,2,1,0:T(8,128)S(1)}, f32[4,16,128]{2,1,0:T(8,128)S(1)}, f32[16,16,128]{2,1,0:T(8,128)S(1)}, f3...) custom-call(s32[1]{0:T(128)S(6)} %copy.15.seam, f32[512,128]{1,0:T(8,128)} %bitcast.2, f32[512,128]{1,0:T(8,128)} %bitcast.3, ...), custom_call_target="tpu_custom_call" | custom-call | tf_op jit(solution)/shard_map/prepare/pallas_call | solution.py:843
  2.7 2.4 %collective-permute-start.2 = (f32[4,16,128]{2,1,0:T(8,128)S(1)}, f32[4,16,128]{2,1,0:T(8,128)S(1)}, u32[]{:S(2)}, u32[]{:S(2)}) collective-permute-start(f32[4,16,128]{2,1,0:T(8,128)S(1)} %get-tuple-element.36.own), channel_id=1, source_target_pairs={{0,3},{1,2},{2,1},{3,0},{4,7},{5,6},{6,5},{7,4},{8,11},{9,10},{10,... | collective-permute-start | bytes 98312 | tf_op jit(solution)/shard_map/ppermute | solution.py:862
  5.2 0.7 %collective-permute-start.1 = (f32[4,16,128]{2,1,0:T(8,128)S(1)}, f32[4,16,128]{2,1,0:T(8,128)S(1)}, u32[]{:S(2)}, u32[]{:S(2)}) collective-permute-start(f32[4,16,128]{2,1,0:T(8,128)S(1)} %get-tuple-element.36.own), channel_id=1, source_target_pairs={{0,1},{1,0},{2,3},{3,2},{4,5},{5,4},{6,7},{7,6},{8,9},{9,8},{10,11... | collective-permute-start | bytes 98312 | tf_op jit(solution)/shard_map/ppermute | solution.py:863
  5.8 0.2 %pack_rows.1 = (f32[160,128]{1,0:T(8,128)S(1)}, f32[160,128]{1,0:T(8,128)S(1)}) custom-call(f32[1024,128]{1,0:T(8,128)S(1)} %get-tuple-element.31.fields, f32[16,16,128]{2,1,0:T(8,128)S(1)} %get-tuple-element.32.mix_h, f32[16,16,128]{2,1,0:T(8,128)S(1)} %get-tuple-element.33.mix_v, s32[16,128]{1,0:T(8,128)S(1)} %get-tuple-element.34.levels), custom_call_target="tpu_custom_call" | custom-call | tf_op jit(solution)/shard_map/pack_rows/pallas_call | solution.py:869
  6.0 1.6 %collective-permute-start = (f32[160,128]{1,0:T(8,128)S(1)}, f32[160,128]{1,0:T(8,128)S(1)}, u32[]{:S(2)}, u32[]{:S(2)}) collective-permute-start(f32[160,128]{1,0:T(8,128)S(1)} %get-tuple-element.35), channel_id=1, source_target_pairs={{0,4},{4,8},{8,12},{12,0},{1,5},{5,9},{9,13},{13,1},{2,6},{6,10},{... | collective-permute-start | bytes 245768 | tf_op jit(solution)/shard_map/ppermute | solution.py:881
  7.6 0.0 collective-permute-done.2.far
  7.6 0.0 collective-permute-done.1.near
  7.7 0.2 %pack_sides.1 = (f32[4,16,128]{2,1,0:T(8,128)S(1)}, f32[8,128]{1,0:T(8,128)S(1)}, f32[168,128]{1,0:T(8,128)S(1)}) custom-call(f32[4,16,128]{2,1,0:T(8,128)S(1)} %collective-permute-done.1.near, f32[4,16,128]{2,1,0:T(8,128)S(1)} %collective-permute-done.2.far, f32[4,16,128]{2,1,0:T(8,128)S(1)} %get-tuple-element.36.own, f32[160,128]{1,0:T(8,128)S(1)} %get-tuple-element.37.early), custom_call_target="tpu_custom_call" | custom-call | tf_op jit(solution)/shard_map/pack_sides/pallas_call | solution.py:869
  7.9 1.9 %collective-permute-start.4 = (f32[8,128]{1,0:T(8,128)S(1)}, f32[8,128]{1,0:T(8,128)S(1)}, u32[]{:S(2)}, u32[]{:S(2)}) collective-permute-start(f32[8,128]{1,0:T(8,128)S(1)} %get-tuple-element.39), channel_id=1, source_target_pairs={{0,4},{4,8},{8,12},{12,0},{1,5},{5,9},{9,13},{13,1},{2,6},{6,10},{... | collective-permute-start | bytes 12296 | tf_op jit(solution)/shard_map/ppermute | solution.py:887
  9.7 2.1 %collective-permute-start.3 = (f32[168,128]{1,0:T(8,128)S(1)}, f32[168,128]{1,0:T(8,128)S(1)}, u32[]{:S(2)}, u32[]{:S(2)}) collective-permute-start(f32[168,128]{1,0:T(8,128)S(1)} %get-tuple-element.38.sent), channel_id=1, source_target_pairs={{0,12},{4,0},{8,4},{12,8},{1,13},{5,1},{9,5},{13,9},{2,14},{6,2},{... | collective-permute-start | bytes 258056 | tf_op jit(solution)/shard_map/ppermute | solution.py:888
  11.8 0.8 %interior_down.1 = (f32[16,64,128]{2,1,0:T(8,128)S(1)}, f32[16,4,4,16,128]{4,3,2,1,0:T(8,128)S(1)}, f32[16,4,16,128]{3,2,1,0:T(8,128)S(1)}, f32[16,16,128]{2,1,0...) custom-call(f32[4,16,128]{2,1,0:T(8,128)S(1)} %get-tuple-element.40.merged,, ...), custom_call_target="tpu_custom_call" | custom-call | flops 30000000 | bytes 30000000 | tf_op jit(solution)/shard_map/interior_down/pallas_call | solution.py:869
  12.7 0.6 %interior_up.1 = (f32[16,64,128]{2,1,0:T(8,128)S(1)}, f32[16,64,128]{2,1,0:T(8,128)S(1)}, f32[2,16,16,128]{3,2,1,0:T(8,128)S(1)}, f32[16,16,128]{2,1,0:T(8,128)S(1)}) custom-call(f32[16,64,128]{2,1,0:T(8,128)S(1)} %get-tuple-element.42.inside_in, f32[16,4,4,16,128]{4,3,2,1,0:T(8,128)S(1)} %get-tuple-element.43.steps, ...), custom_call_target="tpu_custom_call" | custom-call | flops 30000000 | bytes 30000000 | tf_op jit(solution)/shard_map/interior_up/pallas_call | solution.py:869
  13.3 0.5 %interior_edges.1 = (f32[30,16,8,128]{3,2,1,0:T(8,128)S(1)}, f32[6,8,128]{2,1,0:T(8,128)S(1)}, f32[16,16,128]{2,1,0:T(8,128)S(1)}) custom-call(f32[4,16,128]{2,1,0:T(8,128)S(1)} %get-tuple-element.40.merged, f32[1024,128]{1,0:T(8,128)S(1)} %get-tuple-element.31.fields, f32[3,16,16,128]{3,2,1,0:T(8,128)S(1)} %get-tuple-element.41.factors, ...), custom_call_target="tpu_custom_call" | custom-call | flops 40000000 | bytes 40000000 | tf_op jit(solution)/shard_map/interior_edges/pallas_call | solution.py:869
  13.8 0.0 collective-permute-done.4.corner
  13.8 0.2 %open_below.1.opened = f32[2,8,128]{2,1,0:T(8,128)S(1)} custom-call(s32[1]{0:T(128)S(6)} %copy.15.seam, f32[8,128]{1,0:T(8,128)S(1)} %collective-permute-done.4.corner, f32[4,16,128]{2,1,0:T(8,128)S(1)} %get-tuple-element.40.merged, f32[6,8,128]{2,1,0:T(8,128)S(1)} %get-tuple-element.52.edge_levels), custom_call_target="tpu_custom_call" | custom-call | flops 900000000 | bytes 900000000 | tf_op jit(solution)/shard_map/open_below/pallas_call | solution.py:929
  14.0 0.0 collective-permute-done.from_below
  14.0 0.1 turn_below.1.below
  14.1 0.2 %collective-permute-done.3.from_above = f32[168,128]{1,0:T(8,128)S(1)} collective-permute-done((f32[168,128]{1,0:T(8,128)S(1)}, f32[168,128]{1,0:T(8,128)S(1)}, u32[]{:S(2)}, u32[]{:S(2)}) %collective-permute-start.3) | collective-permute-done | bytes 86048 | tf_op jit(solution)/shard_map/ppermute | solution.py:888
  14.2 1.2 %finish.1 = (f32[2,16,16,128]{3,2,1,0:T(8,128)}, f32[16,16,128]{2,1,0:T(8,128)}, f32[16,16,128]{2,1,0:T(8,128)}, f32[2,16,16,128]{3,2,1,0:T(8,128)S(1)}, f32[16,...) custom-call(s32[1]{0:T(128)S(6)} %copy.15.seam, ...), custom_call_target="tpu_custom_call", output_to_operand_aliasing={{3}: (7, {}), {4}: (8, {}), {5}: (9, {})} | custom-call | tf_op jit(solution)/shard_map/finish/pallas_call | solution.py:945
Async XLA Ops:
  2.7 4.9 %collective-permute-start.2 = (f32[4,16,128]{2,1,0:T(8,128)S(1)}, f32[4,16,128]{2,1,0:T(8,128)S(1)}, u32[]{:S(2)}, u32[]{:S(2)}) collective-permute-start(f32[4,16,128]{2,1,0:T(8,128)S(1)} %get-tuple-element.36.own), channel_id=1, source_target_pairs={{0,3},{1,2},{2,1},{3,0},{4,7},{5,6},{6,5},{7,4},{8,11},{9,10},{10,... | collective-permute-start | bytes 98312 | tf_op jit(solution)/shard_map/ppermute | solution.py:862
  5.2 2.5 %collective-permute-start.1 = (f32[4,16,128]{2,1,0:T(8,128)S(1)}, f32[4,16,128]{2,1,0:T(8,128)S(1)}, u32[]{:S(2)}, u32[]{:S(2)}) collective-permute-start(f32[4,16,128]{2,1,0:T(8,128)S(1)} %get-tuple-element.36.own), channel_id=1, source_target_pairs={{0,1},{1,0},{2,3},{3,2},{4,5},{5,4},{6,7},{7,6},{8,9},{9,8},{10,11... | collective-permute-start | bytes 98312 | tf_op jit(solution)/shard_map/ppermute | solution.py:863
  6.0 8.0 %collective-permute-start = (f32[160,128]{1,0:T(8,128)S(1)}, f32[160,128]{1,0:T(8,128)S(1)}, u32[]{:S(2)}, u32[]{:S(2)}) collective-permute-start(f32[160,128]{1,0:T(8,128)S(1)} %get-tuple-element.35), channel_id=1, source_target_pairs={{0,4},{4,8},{8,12},{12,0},{1,5},{5,9},{9,13},{13,1},{2,6},{6,10},{... | collective-permute-start | bytes 245768 | tf_op jit(solution)/shard_map/ppermute | solution.py:881
  7.9 5.9 %collective-permute-start.4 = (f32[8,128]{1,0:T(8,128)S(1)}, f32[8,128]{1,0:T(8,128)S(1)}, u32[]{:S(2)}, u32[]{:S(2)}) collective-permute-start(f32[8,128]{1,0:T(8,128)S(1)} %get-tuple-element.39), channel_id=1, source_target_pairs={{0,4},{4,8},{8,12},{12,0},{1,5},{5,9},{9,13},{13,1},{2,6},{6,10},{... | collective-permute-start | bytes 12296 | tf_op jit(solution)/shard_map/ppermute | solution.py:887
  9.7 4.5 %collective-permute-start.3 = (f32[168,128]{1,0:T(8,128)S(1)}, f32[168,128]{1,0:T(8,128)S(1)}, u32[]{:S(2)}, u32[]{:S(2)}) collective-permute-start(f32[168,128]{1,0:T(8,128)S(1)} %get-tuple-element.38.sent), channel_id=1, source_target_pairs={{0,12},{4,0},{8,4},{12,8},{1,13},{5,1},{9,5},{13,9},{2,14},{6,2},{... | collective-permute-start | bytes 258056 | tf_op jit(solution)/shard_map/ppermute | solution.py:888

commit v10 on v9

--- a/solution.py
+++ b/solution.py
@@ -544,6 +544,9 @@
             *(ref[row + q * stride : row + q * stride + 1] for row in (low, high) for q in range(4))
         )
 
+    def opened_step(n, k, step):
+        return jnp.where(edge_levels[n] > float(k), exchange(step), 0.0)
+
     last_lane, first_lane = iota(8, 1) == LANES - 1, iota(8, 1) == 0
 
     coef_rows = ends(merged[tiles])
@@ -570,9 +573,9 @@
             to_east=ends(weights[k, 0]),
             to_west=ends(weights[k, 1]),
             to_inner=both(weights[k, 2, :1], weights[k, 3, ROWS - 1 :]),
-            cross_east=exchange(jnp.where(last_lane, column, roll(field, -1, 1)) - field),
-            cross_west=exchange(jnp.where(first_lane, column, roll(field, 1, 1)) - field),
-            cross_inner=exchange(field_1 - field),
+            cross_east=opened_step(2, k, jnp.where(last_lane, column, roll(field, -1, 1)) - field),
+            cross_west=opened_step(3, k, jnp.where(first_lane, column, roll(field, 1, 1)) - field),
+            cross_inner=opened_step(4, k, field_1 - field),
             inside=four(inside.at[k], 0, ROWS),
             after=stacked(
                 *(
@@ -734,7 +737,7 @@
         rows[2, k] = added
         rows[3, k] = column_added
         rows[4, k] = weight
-        rows[5, k] = exchange(step)
+        rows[5, k] = jnp.where(level_face > float(k), exchange(step), 0.0)
         bond_above = bond_here
 
     copies = []
@@ -775,14 +778,12 @@
                 (ROWS - 2, result_1, 6),
             ):
                 adjoint[t, k, at : at + 1] = source[row + t : row + t + 1]
-        product_1 = jnp.where(
-            edge_level("inner") > float(k), -edge("cross_inner", k) * added, 0.0
-        )
+        product_1 = -edge("cross_inner", k) * added
         product = (
             product_1
-            + jnp.where(edge_level("east") > float(k), edge("cross_east", k) * east_step, 0.0)
-            + jnp.where(edge_level("west") > float(k), edge("cross_west", k) * west_step, 0.0)
-            + jnp.where(level_face > float(k), rows[5, k] * out_step, 0.0)
+            + edge("cross_east", k) * east_step
+            + edge("cross_west", k) * west_step
+            + rows[5, k] * out_step
         )
         for name, inset, value in (("grad_h", 0, product), ("grad_h_1", 1, product_1)):
             value = value + roll(value, -1, 0)
@@ -822,7 +823,9 @@
             grad_v[k - 1, inset : inset + 1] = value[:1]
             grad_v[k - 1, ROWS - 1 - inset : ROWS - inset] = value[4:5]
         face_0, face_1 = next_0, next_1
-    send(grad_v, grad_v_out)
+        if k == depth // 2:
+            send(grad_v.at[:k], grad_v_out.at[:k])
+    send(grad_v.at[depth // 2 :], grad_v_out.at[depth // 2 :])
     for copy in copies:
         copy.wait()
 
@@ -959,7 +962,7 @@
             vmem_out(height, LANES),
             vmem_out(6, *row_block),
             vmem_out(2, *row_block),
-            pltpu.SemaphoreType.DMA((5,)),
+            pltpu.SemaphoreType.DMA((6,)),
         ],
         compiler_params=params,
         name="finish",

time: 15.7 us -> 15.7 us (level)
  transfers between devices with their start and end apart: 5 -> 5, of which waited for: 1 -> 1; matrix products, arithmetic and copies ran while one was open for 0% -> 0% of each run, Pallas kernels for 17% -> 16%
where the time goes in v10:
time: 15.7 us; the launch traced here: 15.5 us
  starting transfers between devices  8.69 us (55%)
  Pallas kernels  5.17 us (33%)
  between operations  1.35 us (9%)
  waiting for transfers between devices  0.27 us (2%)
    ppermute x1, starting transfers between devices, per_device(): far = lax.ppermute(own, 'ty', far_pairs)  2.44 us
    pallas_call x5, Pallas kernels, call(): pl.pallas_call(body, out_shape=outs, compiler_params=params, name=body.__...  2.35 us
    ppermute x1, starting transfers between devices, per_device(): from_above = lax.ppermute(lower, 'tx', downward)  2.09 us
    ppermute x1, starting transfers between devices, per_device(): corner_below = lax.ppermute(corner, 'tx', upward)  1.85 us
    ppermute x1, starting transfers between devices, per_device(): from_below = lax.ppermute(upper, 'tx', upward)  1.63 us
    pallas_call x1, Pallas kernels, per_device(): pl.pallas_call(prepare, out_shape=(vmem_out(4 * depth * ROWS, LANES), vme...  1.43 us
    pallas_call x1, Pallas kernels, per_device(): pl.pallas_call(finish, out_shape=(jax.ShapeDtypeStruct(tracers.shape, jnp...  1.23 us
    ppermute x1, starting transfers between devices, per_device(): near = lax.ppermute(own, 'ty', near_pairs)  0.68 us
  transfers between devices with their start and end apart: 5, of which 1 were waited for; matrix products, arithmetic and copies ran while one was open for 0% of the time, Pallas kernels for 16%

profile of v10, /device:TPU:0, one launch (start us, length us, event | category | flops | bytes accessed | tf_op | source)
XLA Modules:
  0.0 15.5 jit_solution(11373379430176561509)
XLA Ops:
  1.3 1.4 %prepare.1 = (f32[1024,128]{1,0:T(8,128)S(1)}, f32[3,16,16,128]{3,2,1,0:T(8,128)S(1)}, f32[4,16,128]{2,1,0:T(8,128)S(1)}, f32[16,16,128]{2,1,0:T(8,128)S(1)}, f3...) custom-call(s32[1]{0:T(128)S(6)} %copy.15.seam, f32[512,128]{1,0:T(8,128)} %bitcast.2, f32[512,128]{1,0:T(8,128)} %bitcast.3, ...), custom_call_target="tpu_custom_call" | custom-call | tf_op jit(solution)/shard_map/prepare/pallas_call | solution.py:846
  2.7 2.4 %collective-permute-start.2 = (f32[4,16,128]{2,1,0:T(8,128)S(1)}, f32[4,16,128]{2,1,0:T(8,128)S(1)}, u32[]{:S(2)}, u32[]{:S(2)}) collective-permute-start(f32[4,16,128]{2,1,0:T(8,128)S(1)} %get-tuple-element.36.own), channel_id=1, source_target_pairs={{0,3},{1,2},{2,1},{3,0},{4,7},{5,6},{6,5},{7,4},{8,11},{9,10},{10,... | collective-permute-start | bytes 98312 | tf_op jit(solution)/shard_map/ppermute | solution.py:865
  5.2 0.7 %collective-permute-start.1 = (f32[4,16,128]{2,1,0:T(8,128)S(1)}, f32[4,16,128]{2,1,0:T(8,128)S(1)}, u32[]{:S(2)}, u32[]{:S(2)}) collective-permute-start(f32[4,16,128]{2,1,0:T(8,128)S(1)} %get-tuple-element.36.own), channel_id=1, source_target_pairs={{0,1},{1,0},{2,3},{3,2},{4,5},{5,4},{6,7},{7,6},{8,9},{9,8},{10,11... | collective-permute-start | bytes 98312 | tf_op jit(solution)/shard_map/ppermute | solution.py:866
  5.8 0.2 %pack_rows.1 = (f32[160,128]{1,0:T(8,128)S(1)}, f32[160,128]{1,0:T(8,128)S(1)}) custom-call(f32[1024,128]{1,0:T(8,128)S(1)} %get-tuple-element.31.fields, f32[16,16,128]{2,1,0:T(8,128)S(1)} %get-tuple-element.32.mix_h, f32[16,16,128]{2,1,0:T(8,128)S(1)} %get-tuple-element.33.mix_v, s32[16,128]{1,0:T(8,128)S(1)} %get-tuple-element.34.levels), custom_call_target="tpu_custom_call" | custom-call | tf_op jit(solution)/shard_map/pack_rows/pallas_call | solution.py:872
  6.0 1.6 %collective-permute-start = (f32[160,128]{1,0:T(8,128)S(1)}, f32[160,128]{1,0:T(8,128)S(1)}, u32[]{:S(2)}, u32[]{:S(2)}) collective-permute-start(f32[160,128]{1,0:T(8,128)S(1)} %get-tuple-element.35), channel_id=1, source_target_pairs={{0,4},{4,8},{8,12},{12,0},{1,5},{5,9},{9,13},{13,1},{2,6},{6,10},{... | collective-permute-start | bytes 245768 | tf_op jit(solution)/shard_map/ppermute | solution.py:884
  7.6 0.0 collective-permute-done.2.far
  7.6 0.0 collective-permute-done.1.near
  7.7 0.2 %pack_sides.1 = (f32[4,16,128]{2,1,0:T(8,128)S(1)}, f32[8,128]{1,0:T(8,128)S(1)}, f32[168,128]{1,0:T(8,128)S(1)}) custom-call(f32[4,16,128]{2,1,0:T(8,128)S(1)} %collective-permute-done.1.near, f32[4,16,128]{2,1,0:T(8,128)S(1)} %collective-permute-done.2.far, f32[4,16,128]{2,1,0:T(8,128)S(1)} %get-tuple-element.36.own, f32[160,128]{1,0:T(8,128)S(1)} %get-tuple-element.37.early), custom_call_target="tpu_custom_call" | custom-call | tf_op jit(solution)/shard_map/pack_sides/pallas_call | solution.py:872
  7.9 1.9 %collective-permute-start.4 = (f32[8,128]{1,0:T(8,128)S(1)}, f32[8,128]{1,0:T(8,128)S(1)}, u32[]{:S(2)}, u32[]{:S(2)}) collective-permute-start(f32[8,128]{1,0:T(8,128)S(1)} %get-tuple-element.39), channel_id=1, source_target_pairs={{0,4},{4,8},{8,12},{12,0},{1,5},{5,9},{9,13},{13,1},{2,6},{6,10},{... | collective-permute-start | bytes 12296 | tf_op jit(solution)/shard_map/ppermute | solution.py:890
  9.7 2.1 %collective-permute-start.3 = (f32[168,128]{1,0:T(8,128)S(1)}, f32[168,128]{1,0:T(8,128)S(1)}, u32[]{:S(2)}, u32[]{:S(2)}) collective-permute-start(f32[168,128]{1,0:T(8,128)S(1)} %get-tuple-element.38.sent), channel_id=1, source_target_pairs={{0,12},{4,0},{8,4},{12,8},{1,13},{5,1},{9,5},{13,9},{2,14},{6,2},{... | collective-permute-start | bytes 258056 | tf_op jit(solution)/shard_map/ppermute | solution.py:891
  11.8 0.8 %interior_down.1 = (f32[16,64,128]{2,1,0:T(8,128)S(1)}, f32[16,4,4,16,128]{4,3,2,1,0:T(8,128)S(1)}, f32[16,4,16,128]{3,2,1,0:T(8,128)S(1)}, f32[16,16,128]{2,1,0...) custom-call(f32[4,16,128]{2,1,0:T(8,128)S(1)} %get-tuple-element.40.merged,, ...), custom_call_target="tpu_custom_call" | custom-call | flops 30000000 | bytes 30000000 | tf_op jit(solution)/shard_map/interior_down/pallas_call | solution.py:872
  12.7 0.6 %interior_up.1 = (f32[16,64,128]{2,1,0:T(8,128)S(1)}, f32[16,64,128]{2,1,0:T(8,128)S(1)}, f32[2,16,16,128]{3,2,1,0:T(8,128)S(1)}, f32[16,16,128]{2,1,0:T(8,128)S(1)}) custom-call(f32[16,64,128]{2,1,0:T(8,128)S(1)} %get-tuple-element.42.inside_in, f32[16,4,4,16,128]{4,3,2,1,0:T(8,128)S(1)} %get-tuple-element.43.steps, ...), custom_call_target="tpu_custom_call" | custom-call | flops 30000000 | bytes 30000000 | tf_op jit(solution)/shard_map/interior_up/pallas_call | solution.py:872
  13.3 0.5 %interior_edges.1 = (f32[30,16,8,128]{3,2,1,0:T(8,128)S(1)}, f32[6,8,128]{2,1,0:T(8,128)S(1)}, f32[16,16,128]{2,1,0:T(8,128)S(1)}) custom-call(f32[4,16,128]{2,1,0:T(8,128)S(1)} %get-tuple-element.40.merged, f32[1024,128]{1,0:T(8,128)S(1)} %get-tuple-element.31.fields, f32[3,16,16,128]{3,2,1,0:T(8,128)S(1)} %get-tuple-element.41.factors, ...), custom_call_target="tpu_custom_call" | custom-call | flops 40000000 | bytes 40000000 | tf_op jit(solution)/shard_map/interior_edges/pallas_call | solution.py:872
  13.8 0.0 collective-permute-done.4.corner
  13.8 0.2 %open_below.1.opened = f32[2,8,128]{2,1,0:T(8,128)S(1)} custom-call(s32[1]{0:T(128)S(6)} %copy.15.seam, f32[8,128]{1,0:T(8,128)S(1)} %collective-permute-done.4.corner, f32[4,16,128]{2,1,0:T(8,128)S(1)} %get-tuple-element.40.merged, f32[6,8,128]{2,1,0:T(8,128)S(1)} %get-tuple-element.52.edge_levels), custom_call_target="tpu_custom_call" | custom-call | flops 900000000 | bytes 900000000 | tf_op jit(solution)/shard_map/open_below/pallas_call | solution.py:932
  14.0 0.0 collective-permute-done.from_below
  14.0 0.3 %collective-permute-done.3.from_above = f32[168,128]{1,0:T(8,128)S(1)} collective-permute-done((f32[168,128]{1,0:T(8,128)S(1)}, f32[168,128]{1,0:T(8,128)S(1)}, u32[]{:S(2)}, u32[]{:S(2)}) %collective-permute-start.3) | collective-permute-done | bytes 86048 | tf_op jit(solution)/shard_map/ppermute | solution.py:891
  14.2 1.2 %finish.1 = (f32[2,16,16,128]{3,2,1,0:T(8,128)}, f32[16,16,128]{2,1,0:T(8,128)}, f32[16,16,128]{2,1,0:T(8,128)}, f32[2,16,16,128]{3,2,1,0:T(8,128)S(1)}, f32[16,...) custom-call(s32[1]{0:T(128)S(6)} %copy.15.seam, ...), custom_call_target="tpu_custom_call", output_to_operand_aliasing={{3}: (7, {}), {4}: (8, {}), {5}: (9, {})} | custom-call | tf_op jit(solution)/shard_map/finish/pallas_call | solution.py:948
  (1 shorter events, 0.0 us)
Async XLA Ops:
  2.7 4.9 %collective-permute-start.2 = (f32[4,16,128]{2,1,0:T(8,128)S(1)}, f32[4,16,128]{2,1,0:T(8,128)S(1)}, u32[]{:S(2)}, u32[]{:S(2)}) collective-permute-start(f32[4,16,128]{2,1,0:T(8,128)S(1)} %get-tuple-element.36.own), channel_id=1, source_target_pairs={{0,3},{1,2},{2,1},{3,0},{4,7},{5,6},{6,5},{7,4},{8,11},{9,10},{10,... | collective-permute-start | bytes 98312 | tf_op jit(solution)/shard_map/ppermute | solution.py:865
  5.2 2.5 %collective-permute-start.1 = (f32[4,16,128]{2,1,0:T(8,128)S(1)}, f32[4,16,128]{2,1,0:T(8,128)S(1)}, u32[]{:S(2)}, u32[]{:S(2)}) collective-permute-start(f32[4,16,128]{2,1,0:T(8,128)S(1)} %get-tuple-element.36.own), channel_id=1, source_target_pairs={{0,1},{1,0},{2,3},{3,2},{4,5},{5,4},{6,7},{7,6},{8,9},{9,8},{10,11... | collective-permute-start | bytes 98312 | tf_op jit(solution)/shard_map/ppermute | solution.py:866
  6.0 8.0 %collective-permute-start = (f32[160,128]{1,0:T(8,128)S(1)}, f32[160,128]{1,0:T(8,128)S(1)}, u32[]{:S(2)}, u32[]{:S(2)}) collective-permute-start(f32[160,128]{1,0:T(8,128)S(1)} %get-tuple-element.35), channel_id=1, source_target_pairs={{0,4},{4,8},{8,12},{12,0},{1,5},{5,9},{9,13},{13,1},{2,6},{6,10},{... | collective-permute-start | bytes 245768 | tf_op jit(solution)/shard_map/ppermute | solution.py:884
  7.9 5.9 %collective-permute-start.4 = (f32[8,128]{1,0:T(8,128)S(1)}, f32[8,128]{1,0:T(8,128)S(1)}, u32[]{:S(2)}, u32[]{:S(2)}) collective-permute-start(f32[8,128]{1,0:T(8,128)S(1)} %get-tuple-element.39), channel_id=1, source_target_pairs={{0,4},{4,8},{8,12},{12,0},{1,5},{5,9},{9,13},{13,1},{2,6},{6,10},{... | collective-permute-start | bytes 12296 | tf_op jit(solution)/shard_map/ppermute | solution.py:890
  9.7 4.5 %collective-permute-start.3 = (f32[168,128]{1,0:T(8,128)S(1)}, f32[168,128]{1,0:T(8,128)S(1)}, u32[]{:S(2)}, u32[]{:S(2)}) collective-permute-start(f32[168,128]{1,0:T(8,128)S(1)} %get-tuple-element.38.sent), channel_id=1, source_target_pairs={{0,12},{4,0},{8,4},{12,8},{1,13},{5,1},{9,5},{13,9},{2,14},{6,2},{... | collective-permute-start | bytes 258056 | tf_op jit(solution)/shard_map/ppermute | solution.py:891

commit v11 on v10

--- a/solution.py
+++ b/solution.py
@@ -220,7 +220,7 @@
     upper[10 * depth - 1 :] = depths[ROWS - 1 :]
 
 
-def pack_sides(near, far, own, early, merged, corner, lower):
+def pack_sides(far, near, own, early, merged, corner, lower):
     tiles = near.shape[0] // 2
     place = lax.axis_index("ty")
     last = lax.axis_size("ty") - 1
@@ -885,7 +885,7 @@
     merged, corner, lower = call(
         pack_sides,
         (vmem_out(2 * tiles, *tile), vmem_out(8, LANES), vmem_out(height + 8, LANES)),
-        *(near, far, own, early),
+        *(far, near, own, early),
     )
     corner_below = lax.ppermute(corner, "tx", upward)
     from_above = lax.ppermute(lower, "tx", downward)

time: 15.7 us -> 15.7 us (level)
    ppermute x1, starting transfers between devices: 1.85 us -> 1.63 us  [per_device(): corner_below = lax.ppermute(corner, 'tx', upward)]
    ppermute x1, starting transfers between devices: 2.44 us -> 2.61 us  [per_device(): far = lax.ppermute(own, 'ty', far_pairs)]
    ppermute x1, starting transfers between devices: 0.68 us -> 0.52 us  [per_device(): near = lax.ppermute(own, 'ty', near_pairs)]
  transfers between devices with their start and end apart: 5 -> 5, of which waited for: 1 -> 1; matrix products, arithmetic and copies ran while one was open for 0% -> 0% of each run, Pallas kernels for 16% -> 17%
where the time goes in v11:
time: 15.7 us; the launch traced here: 15.5 us
  starting transfers between devices  8.64 us (55%)
  Pallas kernels  5.25 us (33%)
  between operations  1.35 us (9%)
  waiting for transfers between devices  0.28 us (2%)
    ppermute x1, starting transfers between devices, per_device(): far = lax.ppermute(own, 'ty', far_pairs)  2.61 us
    pallas_call x5, Pallas kernels, call(): pl.pallas_call(body, out_shape=outs, compiler_params=params, name=body.__...  2.35 us
    ppermute x1, starting transfers between devices, per_device(): from_above = lax.ppermute(lower, 'tx', downward)  2.25 us
    ppermute x1, starting transfers between devices, per_device(): from_below = lax.ppermute(upper, 'tx', upward)  1.63 us
    ppermute x1, starting transfers between devices, per_device(): corner_below = lax.ppermute(corner, 'tx', upward)  1.63 us
    pallas_call x1, Pallas kernels, per_device(): pl.pallas_call(prepare, out_shape=(vmem_out(4 * depth * ROWS, LANES), vme...  1.43 us
    pallas_call x1, Pallas kernels, per_device(): pl.pallas_call(finish, out_shape=(jax.ShapeDtypeStruct(tracers.shape, jnp...  1.23 us
    ppermute x1, starting transfers between devices, per_device(): near = lax.ppermute(own, 'ty', near_pairs)  0.52 us
  transfers between devices with their start and end apart: 5, of which 1 were waited for; matrix products, arithmetic and copies ran while one was open for 0% of the time, Pallas kernels for 17%

profile of v11, /device:TPU:0, one launch (start us, length us, event | category | flops | bytes accessed | tf_op | source)
XLA Modules:
  0.0 15.5 jit_solution(13259974266942776463)
XLA Ops:
  1.3 1.4 %prepare.1 = (f32[1024,128]{1,0:T(8,128)S(1)}, f32[3,16,16,128]{3,2,1,0:T(8,128)S(1)}, f32[4,16,128]{2,1,0:T(8,128)S(1)}, f32[16,16,128]{2,1,0:T(8,128)S(1)}, f3...) custom-call(s32[1]{0:T(128)S(6)} %copy.15.seam, f32[512,128]{1,0:T(8,128)} %bitcast.2, f32[512,128]{1,0:T(8,128)} %bitcast.3, ...), custom_call_target="tpu_custom_call" | custom-call | tf_op jit(solution)/shard_map/prepare/pallas_call | solution.py:846
  2.7 0.5 %collective-permute-start.2 = (f32[4,16,128]{2,1,0:T(8,128)S(1)}, f32[4,16,128]{2,1,0:T(8,128)S(1)}, u32[]{:S(2)}, u32[]{:S(2)}) collective-permute-start(f32[4,16,128]{2,1,0:T(8,128)S(1)} %get-tuple-element.36.own), channel_id=1, source_target_pairs={{0,1},{1,0},{2,3},{3,2},{4,5},{5,4},{6,7},{7,6},{8,9},{9,8},{10,11... | collective-permute-start | bytes 98312 | tf_op jit(solution)/shard_map/ppermute | solution.py:866
  3.2 2.6 %collective-permute-start.1 = (f32[4,16,128]{2,1,0:T(8,128)S(1)}, f32[4,16,128]{2,1,0:T(8,128)S(1)}, u32[]{:S(2)}, u32[]{:S(2)}) collective-permute-start(f32[4,16,128]{2,1,0:T(8,128)S(1)} %get-tuple-element.36.own), channel_id=1, source_target_pairs={{0,3},{1,2},{2,1},{3,0},{4,7},{5,6},{6,5},{7,4},{8,11},{9,10},{10,... | collective-permute-start | bytes 98312 | tf_op jit(solution)/shard_map/ppermute | solution.py:865
  5.9 0.2 %pack_rows.1 = (f32[160,128]{1,0:T(8,128)S(1)}, f32[160,128]{1,0:T(8,128)S(1)}) custom-call(f32[1024,128]{1,0:T(8,128)S(1)} %get-tuple-element.31.fields, f32[16,16,128]{2,1,0:T(8,128)S(1)} %get-tuple-element.32.mix_h, f32[16,16,128]{2,1,0:T(8,128)S(1)} %get-tuple-element.33.mix_v, s32[16,128]{1,0:T(8,128)S(1)} %get-tuple-element.34.levels), custom_call_target="tpu_custom_call" | custom-call | tf_op jit(solution)/shard_map/pack_rows/pallas_call | solution.py:872
  6.0 1.6 %collective-permute-start = (f32[160,128]{1,0:T(8,128)S(1)}, f32[160,128]{1,0:T(8,128)S(1)}, u32[]{:S(2)}, u32[]{:S(2)}) collective-permute-start(f32[160,128]{1,0:T(8,128)S(1)} %get-tuple-element.35), channel_id=1, source_target_pairs={{0,4},{4,8},{8,12},{12,0},{1,5},{5,9},{9,13},{13,1},{2,6},{6,10},{... | collective-permute-start | bytes 245768 | tf_op jit(solution)/shard_map/ppermute | solution.py:884
  7.7 0.0 collective-permute-done.2.near
  7.7 0.0 collective-permute-done.1.far
  7.7 0.2 %pack_sides.1 = (f32[4,16,128]{2,1,0:T(8,128)S(1)}, f32[8,128]{1,0:T(8,128)S(1)}, f32[168,128]{1,0:T(8,128)S(1)}) custom-call(f32[4,16,128]{2,1,0:T(8,128)S(1)} %collective-permute-done.1.far, f32[4,16,128]{2,1,0:T(8,128)S(1)} %collective-permute-done.2.near, f32[4,16,128]{2,1,0:T(8,128)S(1)} %get-tuple-element.36.own, f32[160,128]{1,0:T(8,128)S(1)} %get-tuple-element.37.early), custom_call_target="tpu_custom_call" | custom-call | tf_op jit(solution)/shard_map/pack_sides/pallas_call | solution.py:872
  7.9 1.6 %collective-permute-start.4 = (f32[8,128]{1,0:T(8,128)S(1)}, f32[8,128]{1,0:T(8,128)S(1)}, u32[]{:S(2)}, u32[]{:S(2)}) collective-permute-start(f32[8,128]{1,0:T(8,128)S(1)} %get-tuple-element.39), channel_id=1, source_target_pairs={{0,4},{4,8},{8,12},{12,0},{1,5},{5,9},{9,13},{13,1},{2,6},{6,10},{... | collective-permute-start | bytes 12296 | tf_op jit(solution)/shard_map/ppermute | solution.py:890
  9.5 2.2 %collective-permute-start.3 = (f32[168,128]{1,0:T(8,128)S(1)}, f32[168,128]{1,0:T(8,128)S(1)}, u32[]{:S(2)}, u32[]{:S(2)}) collective-permute-start(f32[168,128]{1,0:T(8,128)S(1)} %get-tuple-element.38.sent), channel_id=1, source_target_pairs={{0,12},{4,0},{8,4},{12,8},{1,13},{5,1},{9,5},{13,9},{2,14},{6,2},{... | collective-permute-start | bytes 258056 | tf_op jit(solution)/shard_map/ppermute | solution.py:891
  11.8 0.8 %interior_down.1 = (f32[16,64,128]{2,1,0:T(8,128)S(1)}, f32[16,4,4,16,128]{4,3,2,1,0:T(8,128)S(1)}, f32[16,4,16,128]{3,2,1,0:T(8,128)S(1)}, f32[16,16,128]{2,1,0...) custom-call(f32[4,16,128]{2,1,0:T(8,128)S(1)} %get-tuple-element.40.merged,, ...), custom_call_target="tpu_custom_call" | custom-call | flops 30000000 | bytes 30000000 | tf_op jit(solution)/shard_map/interior_down/pallas_call | solution.py:872
  12.6 0.6 %interior_up.1 = (f32[16,64,128]{2,1,0:T(8,128)S(1)}, f32[16,64,128]{2,1,0:T(8,128)S(1)}, f32[2,16,16,128]{3,2,1,0:T(8,128)S(1)}, f32[16,16,128]{2,1,0:T(8,128)S(1)}) custom-call(f32[16,64,128]{2,1,0:T(8,128)S(1)} %get-tuple-element.42.inside_in, f32[16,4,4,16,128]{4,3,2,1,0:T(8,128)S(1)} %get-tuple-element.43.steps, ...), custom_call_target="tpu_custom_call" | custom-call | flops 30000000 | bytes 30000000 | tf_op jit(solution)/shard_map/interior_up/pallas_call | solution.py:872
  13.2 0.5 %interior_edges.1 = (f32[30,16,8,128]{3,2,1,0:T(8,128)S(1)}, f32[6,8,128]{2,1,0:T(8,128)S(1)}, f32[16,16,128]{2,1,0:T(8,128)S(1)}) custom-call(f32[4,16,128]{2,1,0:T(8,128)S(1)} %get-tuple-element.40.merged, f32[1024,128]{1,0:T(8,128)S(1)} %get-tuple-element.31.fields, f32[3,16,16,128]{3,2,1,0:T(8,128)S(1)} %get-tuple-element.41.factors, ...), custom_call_target="tpu_custom_call" | custom-call | flops 40000000 | bytes 40000000 | tf_op jit(solution)/shard_map/interior_edges/pallas_call | solution.py:872
  13.7 0.0 collective-permute-done.4.corner
  13.8 0.2 %open_below.1.opened = f32[2,8,128]{2,1,0:T(8,128)S(1)} custom-call(s32[1]{0:T(128)S(6)} %copy.15.seam, f32[8,128]{1,0:T(8,128)S(1)} %collective-permute-done.4.corner, f32[4,16,128]{2,1,0:T(8,128)S(1)} %get-tuple-element.40.merged, f32[6,8,128]{2,1,0:T(8,128)S(1)} %get-tuple-element.52.edge_levels), custom_call_target="tpu_custom_call" | custom-call | flops 900000000 | bytes 900000000 | tf_op jit(solution)/shard_map/open_below/pallas_call | solution.py:932
  13.9 0.0 collective-permute-done.from_below
  13.9 0.1 turn_below.1.below
  14.0 0.3 %collective-permute-done.3.from_above = f32[168,128]{1,0:T(8,128)S(1)} collective-permute-done((f32[168,128]{1,0:T(8,128)S(1)}, f32[168,128]{1,0:T(8,128)S(1)}, u32[]{:S(2)}, u32[]{:S(2)}) %collective-permute-start.3) | collective-permute-done | bytes 86048 | tf_op jit(solution)/shard_map/ppermute | solution.py:891
  14.3 1.2 %finish.1 = (f32[2,16,16,128]{3,2,1,0:T(8,128)}, f32[16,16,128]{2,1,0:T(8,128)}, f32[16,16,128]{2,1,0:T(8,128)}, f32[2,16,16,128]{3,2,1,0:T(8,128)S(1)}, f32[16,...) custom-call(s32[1]{0:T(128)S(6)} %copy.15.seam, ...), custom_call_target="tpu_custom_call", output_to_operand_aliasing={{3}: (7, {}), {4}: (8, {}), {5}: (9, {})} | custom-call | tf_op jit(solution)/shard_map/finish/pallas_call | solution.py:948
Async XLA Ops:
  2.7 4.9 %collective-permute-start.2 = (f32[4,16,128]{2,1,0:T(8,128)S(1)}, f32[4,16,128]{2,1,0:T(8,128)S(1)}, u32[]{:S(2)}, u32[]{:S(2)}) collective-permute-start(f32[4,16,128]{2,1,0:T(8,128)S(1)} %get-tuple-element.36.own), channel_id=1, source_target_pairs={{0,1},{1,0},{2,3},{3,2},{4,5},{5,4},{6,7},{7,6},{8,9},{9,8},{10,11... | collective-permute-start | bytes 98312 | tf_op jit(solution)/shard_map/ppermute | solution.py:866
  3.2 4.4 %collective-permute-start.1 = (f32[4,16,128]{2,1,0:T(8,128)S(1)}, f32[4,16,128]{2,1,0:T(8,128)S(1)}, u32[]{:S(2)}, u32[]{:S(2)}) collective-permute-start(f32[4,16,128]{2,1,0:T(8,128)S(1)} %get-tuple-element.36.own), channel_id=1, source_target_pairs={{0,3},{1,2},{2,1},{3,0},{4,7},{5,6},{6,5},{7,4},{8,11},{9,10},{10,... | collective-permute-start | bytes 98312 | tf_op jit(solution)/shard_map/ppermute | solution.py:865
  6.0 7.9 %collective-permute-start = (f32[160,128]{1,0:T(8,128)S(1)}, f32[160,128]{1,0:T(8,128)S(1)}, u32[]{:S(2)}, u32[]{:S(2)}) collective-permute-start(f32[160,128]{1,0:T(8,128)S(1)} %get-tuple-element.35), channel_id=1, source_target_pairs={{0,4},{4,8},{8,12},{12,0},{1,5},{5,9},{9,13},{13,1},{2,6},{6,10},{... | collective-permute-start | bytes 245768 | tf_op jit(solution)/shard_map/ppermute | solution.py:884
  7.9 5.9 %collective-permute-start.4 = (f32[8,128]{1,0:T(8,128)S(1)}, f32[8,128]{1,0:T(8,128)S(1)}, u32[]{:S(2)}, u32[]{:S(2)}) collective-permute-start(f32[8,128]{1,0:T(8,128)S(1)} %get-tuple-element.39), channel_id=1, source_target_pairs={{0,4},{4,8},{8,12},{12,0},{1,5},{5,9},{9,13},{13,1},{2,6},{6,10},{... | collective-permute-start | bytes 12296 | tf_op jit(solution)/shard_map/ppermute | solution.py:890
  9.5 4.8 %collective-permute-start.3 = (f32[168,128]{1,0:T(8,128)S(1)}, f32[168,128]{1,0:T(8,128)S(1)}, u32[]{:S(2)}, u32[]{:S(2)}) collective-permute-start(f32[168,128]{1,0:T(8,128)S(1)} %get-tuple-element.38.sent), channel_id=1, source_target_pairs={{0,12},{4,0},{8,4},{12,8},{1,13},{5,1},{9,5},{13,9},{2,14},{6,2},{... | collective-permute-start | bytes 258056 | tf_op jit(solution)/shard_map/ppermute | solution.py:891
